TPU v7x, 256 devices: a whole 4x4x8 slice. The times are simulated.
256 devices in a mesh: tiles: 64 (over x, z, core), rows: 4 (over y).
Axes of the slice: x: 4, y: 4, z: 8, core: 2. Of those that a mesh axis runs over, the one named last changes fastest.
Arguments:
- returns: bfloat16 [1024, 262144], P('tiles', 'rows'), may hold values from -30 to 30
- security_spans: int32 [2, 262144], P(None, 'rows'), may hold values from 0 to 1023, as said below
- band_returns: bfloat16 [1024, 1024], P('tiles', 'rows'), may hold values from -30 to 30
- band_spans: int32 [2, 1024], replicated, may hold values from 0 to 1023, as said below
- assignment: int32 [4, 128], P('rows'), may hold values from 0 to 127, as said below
Outputs:
- band_cov: bfloat16 [1024, 262144], P('tiles', 'rows')
- col_cov: bfloat16 [4, 65536, 1024], P('rows', 'tiles')
- tile_cov: bfloat16 [4, 128, 1024, 512], P('rows', 'tiles')
Inputs may be any that keep to these rules, and one draw needn't show every extreme that they name: `security_spans`: first <= last for every security. `band_spans`: first <= last for every band security. `assignment`: each row is a permutation of the panels 0 to 127 of its group.
All inputs are finite; a program needn't handle non-finite values.
Results may differ from a plain program's by a relative error of at most 0.001.
Values may be sent and summed in bfloat16 or wider, within the bound.
No kernel may reach another device: no remote copies, remote signals or barrier semaphores. Data moves between devices by JAX's collectives and lax.ppermute only.
A program may use at most 128 MiB of HBM per device.

v0:
```python
import jax
import jax.numpy as jnp
from jax import lax
from jax.sharding import PartitionSpec as P

DAYS = 1024
PANEL = 512


def day_masks(spans_pair, day_total):
    day_index = jnp.arange(day_total, dtype=jnp.int32)[:, None]
    inside = (day_index >= spans_pair[0][None, :]) & (day_index <= spans_pair[1][None, :])
    return inside.astype(jnp.bfloat16)


def finish(product, band_width, panel_width):
    gram = product[:band_width, :panel_width]
    band_sum = product[:band_width, panel_width:]
    column_sum = product[band_width:, :panel_width]
    correlation = product[band_width:, panel_width:]
    centred = gram - band_sum * column_sum / jnp.maximum(correlation, 1.0)
    return (centred / jnp.maximum(correlation - 1.0, 1.0)).astype(jnp.bfloat16)


def stacked_tiles(stacked_left, panels, panel_spans):
    day_total = stacked_left.shape[0]
    band_width = stacked_left.shape[1] // 2
    block_rows = 128
    finished = []
    for slot_index in range(panels.shape[1]):
        column_returns = panels[:, slot_index, :]
        column_spans = panel_spans[:, slot_index, :]
        panel_width = column_returns.shape[1]
        column_mask = day_masks(column_spans, day_total)
        stacked_right = jnp.concatenate([column_returns * column_mask, column_mask], axis=1)
        first_block = jnp.min(column_spans[0]) // block_rows
        last_block = jnp.max(column_spans[1]) // block_rows + 1

        def add_block(block_index, running):
            row_start = block_index * block_rows
            left_block = lax.dynamic_slice_in_dim(stacked_left, row_start, block_rows, 0)
            right_block = lax.dynamic_slice_in_dim(stacked_right, row_start, block_rows, 0)
            return running + lax.dot_general(
                left_block,
                right_block,
                (((0,), (0,)), ((), ())),
                preferred_element_type=jnp.float32,
            )

        running = lax.fori_loop(
            first_block,
            last_block,
            add_block,
            jnp.zeros((2 * band_width, 2 * panel_width), jnp.float32),
        )
        finished.append(finish(running, band_width, panel_width))
    return jnp.stack(finished, axis=0)


def on_device(returns, security_spans, band_returns, band_spans, assignment):
    tile_count = lax.axis_size("tiles")
    tile_index = lax.axis_index("tiles")
    local_days, group_width = returns.shape
    panel_count = group_width // PANEL
    per_device = panel_count // tile_count
    owner_order = assignment[0]
    panel_view = returns.reshape(local_days, panel_count, PANEL)
    owner_send = jnp.take(panel_view, owner_order, axis=1).reshape(
        local_days, tile_count, per_device * PANEL
    )
    band_part = lax.all_gather(band_returns, "rows", axis=1, tiled=True)
    band_full = lax.all_gather(band_part, "tiles", axis=0, tiled=True)
    fetched = lax.all_to_all(owner_send, "tiles", split_axis=1, concat_axis=0, tiled=True)
    fetched = fetched.reshape(DAYS, per_device, PANEL)
    span_view = security_spans.reshape(2, panel_count, PANEL)
    owned_panels = lax.dynamic_slice_in_dim(owner_order, tile_index * per_device, per_device)
    owner_spans = jnp.take(span_view, owned_panels, axis=1)
    band_mask = day_masks(band_spans, DAYS)
    stacked_left = jnp.concatenate([band_full * band_mask, band_mask], axis=1)
    owner_tiles = stacked_tiles(stacked_left, fetched, owner_spans)
    tile_cov = owner_tiles[None]
    arrived = lax.all_to_all(owner_tiles, "tiles", split_axis=1, concat_axis=0, tiled=True)
    positions = jnp.arange(panel_count, dtype=jnp.int32)
    home_slot = jnp.sum(
        jnp.where(owner_order[None, :] == positions[:, None], positions[None, :], 0), axis=1
    )
    home_rows = jnp.take(arrived, home_slot, axis=0)
    band_cov = jnp.transpose(home_rows, (1, 0, 2)).reshape(home_rows.shape[1], group_width)
    home_columns = lax.all_to_all(band_cov, "tiles", split_axis=1, concat_axis=0, tiled=True)
    col_cov = jnp.transpose(home_columns)[None]
    return (band_cov, col_cov, tile_cov)


def solution(mesh):
    placed = (P("tiles", "rows"), P(None, "rows"), P("tiles", "rows"), P(), P("rows", None))
    return jax.shard_map(
        on_device,
        mesh=mesh,
        in_specs=placed,
        out_specs=(P("tiles", "rows"), P("rows", "tiles", None), P("rows", "tiles", None, None)),
        check_vma=False,
    )
```

profile of v0, /device:TPU:1, one launch (start us, length us, event | category | flops | bytes accessed | tf_op | source)
XLA Modules:
  0.0 412.6 jit_solution(8560842307094766019)
XLA Ops:
  11.2 4.1 copy.50
  22.1 13.1 %all-to-all-start = ((bf16[16,64,1024]{2,0,1:T(8,128)(2,1)}), bf16[16,64,1024]{2,0,1:T(8,128)(2,1)S(1)}, u32[]{:S(2)}, u32[]{:S(2)}) async-start(bf16[16,64,1024]{2,0,1:T(8,128)(2,1)} %copy.51), calls=%async_computation | async-start | bytes 4194304 | tf_op jit(solution)/shard_map/all_to_all | solution.py:73
  35.3 10.9 %all_gather.6 = bf16[16,1024]{1,0:T(8,128)(2,1)} all-gather(bf16[16,256]{1,0:T(8,128)(2,1)S(1)} %copy-done.8), channel_id=1, replica_groups=mesh['tiles'=64,'rows'=4] {'rows'}, dimensions={1}, use_global_device_ids=true | all-gather | bytes 40960 | tf_op jit(solution)/shard_map/all_gather | solution.py:71
  63.1 24.3 %all-to-all-done = bf16[16,64,1024]{2,0,1:T(8,128)(2,1)S(1)} async-done(((bf16[16,64,1024]{2,0,1:T(8,128)(2,1)}), bf16[16,64,1024]{2,0,1:T(8,128)(2,1)S(1)}, u32[]{:S(2)}, u32[]{:S(2)}) %all-to-all-start) | async-done | bytes 2097184 | tf_op jit(solution)/shard_map/all_to_all | solution.py:73
  98.9 30.2 %all-gather.2.cloned.1.call-done = bf16[1024,1024]{1,0:T(8,128)(2,1)} async-done(((bf16[16,1024]{1,0:T(8,128)(2,1)}), bf16[1024,1024]{1,0:T(8,128)(2,1)}) %all-gather.2.cloned.1.call-update) | async-done | bytes 2097168 | tf_op jit(solution)/shard_map/all_gather | solution.py:72
  134.3 4.3 %broadcast.114.clone.1 = f32[2048,1024]{1,0:T(8,128)} broadcast(f32[]{:T(128)} %constant.112.clone.1), dimensions={} | broadcast | bytes 8388612 | tf_op jit(solution)/shard_map/broadcast.11
  138.6 65.1 %while.20 = (s32[]{:T(128)}, f32[2048,1024]{1,0:T(8,128)}, s32[]{:T(128)}, bf16[1024,2048]{1,0:T(8,128)(2,1)}, bf16[1024,1024]{1,0:T(8,128)(2,1)}, /*index=5*/s32[]{:T(128)}, s32[]{:T(128)}, s32[]{:T(128)}, s32[]{:T(128)}) while((s32[]{:T(128)}, f32[2048,1024]{1,0:T(8,128)}, s32[]{:T(128)}, bf16[1024,2048]{1,0:T(8,128)(2,1)}, ...), condition=%wide.region_4.5_spmd, body=%wide.region_3.4_spmd.sunk | while | flops 538968064 | bytes 17564812 | solution.py:50
  138.6 8.1 %convolution_add_fusion.4 = f32[2048,1024]{1,0:T(8,128)} fusion(f32[2048,1024]{1,0:T(8,128)} %get-tuple-element.218, bf16[1024,2048]{1,0:T(8,128)(2,1)} %get-tuple-element.229, s32[]{:T(128)S(6)} %select_n.139, bf16[1024,1024]{1,0:T(8,128)(2,1)} %get-tuple-element.230), kind=kOutput, calls=%fused_computation.3.clone.1 | convolution fusion | flops 538968064 | bytes 17564672 | tf_op jit(solution)/shard_map/while/body/dot_general | solution.py:43
  146.7 8.1 %convolution_add_fusion.4 = f32[2048,1024]{1,0:T(8,128)} fusion(f32[2048,1024]{1,0:T(8,128)} %get-tuple-element.218, bf16[1024,2048]{1,0:T(8,128)(2,1)} %get-tuple-element.229, s32[]{:T(128)S(6)} %select_n.139, bf16[1024,1024]{1,0:T(8,128)(2,1)} %get-tuple-element.230), kind=kOutput, calls=%fused_computation.3.clone.1 | convolution fusion | flops 538968064 | bytes 17564672 | tf_op jit(solution)/shard_map/while/body/dot_general | solution.py:43
  154.9 8.1 %convolution_add_fusion.4 = f32[2048,1024]{1,0:T(8,128)} fusion(f32[2048,1024]{1,0:T(8,128)} %get-tuple-element.218, bf16[1024,2048]{1,0:T(8,128)(2,1)} %get-tuple-element.229, s32[]{:T(128)S(6)} %select_n.139, bf16[1024,1024]{1,0:T(8,128)(2,1)} %get-tuple-element.230), kind=kOutput, calls=%fused_computation.3.clone.1 | convolution fusion | flops 538968064 | bytes 17564672 | tf_op jit(solution)/shard_map/while/body/dot_general | solution.py:43
  163.0 8.1 %convolution_add_fusion.4 = f32[2048,1024]{1,0:T(8,128)} fusion(f32[2048,1024]{1,0:T(8,128)} %get-tuple-element.218, bf16[1024,2048]{1,0:T(8,128)(2,1)} %get-tuple-element.229, s32[]{:T(128)S(6)} %select_n.139, bf16[1024,1024]{1,0:T(8,128)(2,1)} %get-tuple-element.230), kind=kOutput, calls=%fused_computation.3.clone.1 | convolution fusion | flops 538968064 | bytes 17564672 | tf_op jit(solution)/shard_map/while/body/dot_general | solution.py:43
  171.2 8.1 %convolution_add_fusion.4 = f32[2048,1024]{1,0:T(8,128)} fusion(f32[2048,1024]{1,0:T(8,128)} %get-tuple-element.218, bf16[1024,2048]{1,0:T(8,128)(2,1)} %get-tuple-element.229, s32[]{:T(128)S(6)} %select_n.139, bf16[1024,1024]{1,0:T(8,128)(2,1)} %get-tuple-element.230), kind=kOutput, calls=%fused_computation.3.clone.1 | convolution fusion | flops 538968064 | bytes 17564672 | tf_op jit(solution)/shard_map/while/body/dot_general | solution.py:43
  179.3 8.1 %convolution_add_fusion.4 = f32[2048,1024]{1,0:T(8,128)} fusion(f32[2048,1024]{1,0:T(8,128)} %get-tuple-element.218, bf16[1024,2048]{1,0:T(8,128)(2,1)} %get-tuple-element.229, s32[]{:T(128)S(6)} %select_n.139, bf16[1024,1024]{1,0:T(8,128)(2,1)} %get-tuple-element.230), kind=kOutput, calls=%fused_computation.3.clone.1 | convolution fusion | flops 538968064 | bytes 17564672 | tf_op jit(solution)/shard_map/while/body/dot_general | solution.py:43
  187.5 8.1 %convolution_add_fusion.4 = f32[2048,1024]{1,0:T(8,128)} fusion(f32[2048,1024]{1,0:T(8,128)} %get-tuple-element.218, bf16[1024,2048]{1,0:T(8,128)(2,1)} %get-tuple-element.229, s32[]{:T(128)S(6)} %select_n.139, bf16[1024,1024]{1,0:T(8,128)(2,1)} %get-tuple-element.230), kind=kOutput, calls=%fused_computation.3.clone.1 | convolution fusion | flops 538968064 | bytes 17564672 | tf_op jit(solution)/shard_map/while/body/dot_general | solution.py:43
  195.6 8.1 %convolution_add_fusion.4 = f32[2048,1024]{1,0:T(8,128)} fusion(f32[2048,1024]{1,0:T(8,128)} %get-tuple-element.218, bf16[1024,2048]{1,0:T(8,128)(2,1)} %get-tuple-element.229, s32[]{:T(128)S(6)} %select_n.139, bf16[1024,1024]{1,0:T(8,128)(2,1)} %get-tuple-element.230), kind=kOutput, calls=%fused_computation.3.clone.1 | convolution fusion | flops 538968064 | bytes 17564672 | tf_op jit(solution)/shard_map/while/body/dot_general | solution.py:43
  203.8 5.7 %fusion.15 = bf16[1,1024,512]{2,1,0:T(8,128)(2,1)} fusion(f32[2048,1024]{1,0:T(8,128)} %get-tuple-element.59), kind=kLoop, calls=%fused_computation.35 | loop fusion | flops 4194304 | bytes 9437184 | tf_op jit(solution)/shard_map/stack | solution.py:57
  209.7 4.3 %broadcast.114.clone = f32[2048,1024]{1,0:T(8,128)} broadcast(f32[]{:T(128)} %constant.112.clone.1), dimensions={} | broadcast | bytes 8388612 | tf_op jit(solution)/shard_map/broadcast.11
  214.0 40.3 %while.21 = (s32[]{:T(128)}, f32[2048,1024]{1,0:T(8,128)}, s32[]{:T(128)}, bf16[1024,2048]{1,0:T(8,128)(2,1)}, bf16[1024,1024]{1,0:T(8,128)(2,1)S(1)}, /*index=5*/s32[]{:T(128)}, s32[]{:T(128)}, s32[]{:T(128)}, s32[]{:T(128)}) while((s32[]{:T(128)}, f32[2048,1024]{1,0:T(8,128)}, s32[]{:T(128)}, bf16[1024,2048]{1,0:T(8,128)(2,1)}, ...), condition=%wide.region_8.9_spmd, body=%wide.region_7.8_spmd.sunk | while | flops 538968064 | bytes 17564812 | solution.py:50
  214.0 8.1 %convolution_add_fusion.5 = f32[2048,1024]{1,0:T(8,128)} fusion(f32[2048,1024]{1,0:T(8,128)} %get-tuple-element.191, bf16[1024,2048]{1,0:T(8,128)(2,1)} %get-tuple-element.202, s32[]{:T(128)S(6)} %select_n.140, bf16[1024,1024]{1,0:T(8,128)(2,1)S(1)} %get-tuple-element.203), kind=kOutput, calls=%fused_computation.7.clone.1 | convolution fusion | flops 538968064 | bytes 17564672 | tf_op jit(solution)/shard_map/while/body/dot_general | solution.py:43
  222.0 8.1 %convolution_add_fusion.5 = f32[2048,1024]{1,0:T(8,128)} fusion(f32[2048,1024]{1,0:T(8,128)} %get-tuple-element.191, bf16[1024,2048]{1,0:T(8,128)(2,1)} %get-tuple-element.202, s32[]{:T(128)S(6)} %select_n.140, bf16[1024,1024]{1,0:T(8,128)(2,1)S(1)} %get-tuple-element.203), kind=kOutput, calls=%fused_computation.7.clone.1 | convolution fusion | flops 538968064 | bytes 17564672 | tf_op jit(solution)/shard_map/while/body/dot_general | solution.py:43
  230.1 8.1 %convolution_add_fusion.5 = f32[2048,1024]{1,0:T(8,128)} fusion(f32[2048,1024]{1,0:T(8,128)} %get-tuple-element.191, bf16[1024,2048]{1,0:T(8,128)(2,1)} %get-tuple-element.202, s32[]{:T(128)S(6)} %select_n.140, bf16[1024,1024]{1,0:T(8,128)(2,1)S(1)} %get-tuple-element.203), kind=kOutput, calls=%fused_computation.7.clone.1 | convolution fusion | flops 538968064 | bytes 17564672 | tf_op jit(solution)/shard_map/while/body/dot_general | solution.py:43
  238.2 8.1 %convolution_add_fusion.5 = f32[2048,1024]{1,0:T(8,128)} fusion(f32[2048,1024]{1,0:T(8,128)} %get-tuple-element.191, bf16[1024,2048]{1,0:T(8,128)(2,1)} %get-tuple-element.202, s32[]{:T(128)S(6)} %select_n.140, bf16[1024,1024]{1,0:T(8,128)(2,1)S(1)} %get-tuple-element.203), kind=kOutput, calls=%fused_computation.7.clone.1 | convolution fusion | flops 538968064 | bytes 17564672 | tf_op jit(solution)/shard_map/while/body/dot_general | solution.py:43
  246.2 8.1 %convolution_add_fusion.5 = f32[2048,1024]{1,0:T(8,128)} fusion(f32[2048,1024]{1,0:T(8,128)} %get-tuple-element.191, bf16[1024,2048]{1,0:T(8,128)(2,1)} %get-tuple-element.202, s32[]{:T(128)S(6)} %select_n.140, bf16[1024,1024]{1,0:T(8,128)(2,1)S(1)} %get-tuple-element.203), kind=kOutput, calls=%fused_computation.7.clone.1 | convolution fusion | flops 538968064 | bytes 17564672 | tf_op jit(solution)/shard_map/while/body/dot_general | solution.py:43
  254.3 4.6 %fusion.16 = bf16[1,1024,512]{2,1,0:T(8,128)(2,1)S(1)} fusion(f32[2048,1024]{1,0:T(8,128)} %get-tuple-element.60), kind=kLoop, calls=%fused_computation.36 | loop fusion | flops 4194304 | bytes 9437184 | tf_op jit(solution)/shard_map/stack | solution.py:57
  260.6 3.5 copy.52
  264.0 14.2 %all-to-all-start.1 = ((bf16[2,1024,512]{2,0,1:T(2,128)(2,1)}), bf16[2,1024,512]{2,0,1:T(2,128)(2,1)S(1)}, u32[]{:S(2)}, u32[]{:S(2)}) async-start(bf16[2,1024,512]{2,0,1:T(2,128)(2,1)} %copy.52), calls=%async_computation.1 | async-start | bytes 4194304 | tf_op jit(solution)/shard_map/all_to_all | solution.py:82
  278.4 51.1 %all-to-all-done.1 = bf16[2,1024,512]{2,0,1:T(2,128)(2,1)S(1)} async-done(((bf16[2,1024,512]{2,0,1:T(2,128)(2,1)}), bf16[2,1024,512]{2,0,1:T(2,128)(2,1)S(1)}, u32[]{:S(2)}, u32[]{:S(2)}) %all-to-all-start.1) | async-done | bytes 2097184 | tf_op jit(solution)/shard_map/all_to_all | solution.py:82
  336.4 4.1 all_to_all.45
  340.5 4.1 copy.57
  344.5 6.0 %all-to-all-start.2 = ((bf16[16,64,1024]{2,0,1:T(8,128)(2,1)}), bf16[16,64,1024]{2,0,1:T(8,128)(2,1)}, u32[]{:S(2)}, u32[]{:S(2)}) async-start(bf16[16,64,1024]{2,0,1:T(8,128)(2,1)} %copy.57), calls=%async_computation.2 | async-start | bytes 4194304 | tf_op jit(solution)/shard_map/all_to_all | solution.py:89
  352.0 49.7 %all-to-all-done.2 = bf16[16,64,1024]{2,0,1:T(8,128)(2,1)} async-done(((bf16[16,64,1024]{2,0,1:T(8,128)(2,1)}), bf16[16,64,1024]{2,0,1:T(8,128)(2,1)}, u32[]{:S(2)}, u32[]{:S(2)}) %all-to-all-start.2) | async-done | bytes 2097184 | tf_op jit(solution)/shard_map/all_to_all | solution.py:89
  401.7 4.0 copy.58
  (65 shorter events, 44.9 us)
Async XLA Ops:
  7.2 39.2 %copy-start = (s32[2,65536]{1,0:T(2,128)S(1)}, s32[2,65536]{1,0:T(2,128)}, u32[]{:S(2)}) copy-start(s32[2,65536]{1,0:T(2,128)} %param.10) | copy-start | bytes 1572868
  7.2 2.0 copy-start.10
  22.1 13.2 %copy-start.8 = (bf16[16,256]{1,0:T(8,128)(2,1)S(1)}, bf16[16,256]{1,0:T(8,128)(2,1)}, u32[]{:S(2)}) copy-start(bf16[16,256]{1,0:T(8,128)(2,1)} %param.11) | copy-start | bytes 24580
  22.1 35.6 %copy-start.9 = (s32[2,1024]{1,0:T(2,128)S(1)}, s32[2,1024]{1,0:T(2,128)}, u32[]{:S(2)}) copy-start(s32[2,1024]{1,0:T(2,128)} %param.12) | copy-start | bytes 24580
  22.1 65.2 %all-to-all-start = ((bf16[16,64,1024]{2,0,1:T(8,128)(2,1)}), bf16[16,64,1024]{2,0,1:T(8,128)(2,1)S(1)}, u32[]{:S(2)}, u32[]{:S(2)}) async-start(bf16[16,64,1024]{2,0,1:T(8,128)(2,1)} %copy.51), calls=%async_computation | async-start | bytes 4194304 | tf_op jit(solution)/shard_map/all_to_all | solution.py:73
  35.3 93.8 %all-gather.2.cloned.1.call-start = ((), (), s32[]{:S(2)}) async-start(), calls=%async_computation.3 | async-start | bytes 2129920 | tf_op jit(solution)/shard_map/all_gather | solution.py:72
  87.4 1.3 copy-start.2
  95.0 2.3 copy-start.6
  98.9 33.0 %copy-start.3 = (bf16[1024,1024]{1,0:T(8,128)(2,1)S(1)}, bf16[1024,1024]{1,0:T(8,128)(2,1)}, u32[]{:S(2)}) copy-start(bf16[1024,1024]{1,0:T(8,128)(2,1)} %fusion.7) | copy-start | bytes 6291460
  203.8 5.7 %copy-start.5 = (bf16[1024,512]{1,0:T(8,128)(2,1)S(1)}, bf16[1024,512]{1,0:T(8,128)(2,1)}, u32[]{:S(2)}) copy-start(bf16[1024,512]{1,0:T(8,128)(2,1)} %fusion.11) | copy-start | bytes 3145732
  203.8 5.7 %copy-start.7 = (bf16[1024,512]{1,0:T(8,128)(2,1)S(1)}, bf16[1024,512]{1,0:T(8,128)(2,1)}, u32[]{:S(2)}) copy-start(bf16[1024,512]{1,0:T(8,128)(2,1)} %get-tuple-element.115) | copy-start | bytes 3145732
  254.3 4.6 %copy-start.4 = (bf16[1,1024,512]{2,1,0:T(8,128)(2,1)S(1)}, bf16[1,1024,512]{2,1,0:T(8,128)(2,1)}, u32[]{:S(2)}) copy-start(bf16[1,1024,512]{2,1,0:T(8,128)(2,1)} %fusion.15) | copy-start | bytes 3145732
  264.0 65.4 %all-to-all-start.1 = ((bf16[2,1024,512]{2,0,1:T(2,128)(2,1)}), bf16[2,1024,512]{2,0,1:T(2,128)(2,1)S(1)}, u32[]{:S(2)}, u32[]{:S(2)}) async-start(bf16[2,1024,512]{2,0,1:T(2,128)(2,1)} %copy.52), calls=%async_computation.1 | async-start | bytes 4194304 | tf_op jit(solution)/shard_map/all_to_all | solution.py:82
  344.5 57.2 %all-to-all-start.2 = ((bf16[16,64,1024]{2,0,1:T(8,128)(2,1)}), bf16[16,64,1024]{2,0,1:T(8,128)(2,1)}, u32[]{:S(2)}, u32[]{:S(2)}) async-start(bf16[16,64,1024]{2,0,1:T(8,128)(2,1)} %copy.57), calls=%async_computation.2 | async-start | bytes 4194304 | tf_op jit(solution)/shard_map/all_to_all | solution.py:89
  401.7 4.0 copy-start.1
Sparse Core Ops, SparseCore 0:
  46.4 82.6 all-gather.1
where the time goes:
time: 414 us; the launch traced here: 413 us
  waiting for transfers between devices  155 us (37%)
  matrix products  105 us (25%)
  local copies, waits for them, and re-layouts  52.9 us (13%)
  starting transfers between devices  33.3 us (8%)
  other arithmetic  30.4 us (7%)
  between operations  24.3 us (6%)
  blocking collectives  10.9 us (3%)
    dot_general x13, matrix products, add_block(): lax.dot_general(left_block, right_block, (((0,), (0,)), ((), ())), prefer...  105 us
    all_to_all x1, waiting for transfers between devices, on_device(): lax.all_to_all(owner_tiles, 'tiles', split_axis=1, concat_axis=0, tiled=T...  51.1 us
    all_to_all x1, waiting for transfers between devices, on_device(): lax.all_to_all(band_cov, 'tiles', split_axis=1, concat_axis=0, tiled=True)  49.7 us
    all_gather x1, waiting for transfers between devices, on_device(): band_full = lax.all_gather(band_part, 'tiles', axis=0, tiled=True)  30.2 us
    all_to_all x1, waiting for transfers between devices, on_device(): lax.all_to_all(owner_send, 'tiles', split_axis=1, concat_axis=0, tiled=True)  24.3 us
    all_to_all x1, starting transfers between devices, on_device(): lax.all_to_all(owner_tiles, 'tiles', split_axis=1, concat_axis=0, tiled=T...  14.2 us
    all_to_all x1, starting transfers between devices, on_device(): lax.all_to_all(owner_send, 'tiles', split_axis=1, concat_axis=0, tiled=True)  13.1 us
    all_gather x1, blocking collectives, on_device(): band_part = lax.all_gather(band_returns, 'rows', axis=1, tiled=True)  10.9 us
  transfers between devices with their start and end apart: 4, of which 4 were waited for; matrix products, arithmetic and copies ran while one was open for 5% of the time, Pallas kernels for 0%

commit v1 on v0

v1 whole, which is shorter than its diff:
```python
import functools

import jax
import jax.numpy as jnp
from jax import lax
from jax.experimental import pallas as pl
from jax.experimental.pallas import tpu as pltpu
from jax.sharding import PartitionSpec as P

DAYS = 1024
PANEL = 512
BAND = 1024
VMEM_LIMIT = 40 * 1024 * 1024


def params():
    return pltpu.CompilerParams(vmem_limit_bytes=VMEM_LIMIT)


def pack_natural(returns, tile_count):
    local_days, group_width = returns.shape
    width = group_width // tile_count
    per_step = 8

    def body(in_ref, out_ref):
        for piece in range(per_step):
            out_ref[piece] = in_ref[:, piece * width : (piece + 1) * width]

    return pl.pallas_call(
        body,
        grid=(tile_count // per_step,),
        in_specs=[pl.BlockSpec((local_days, per_step * width), lambda i: (0, i))],
        out_specs=pl.BlockSpec((per_step, local_days, width), lambda i: (i, 0, 0)),
        out_shape=jax.ShapeDtypeStruct((tile_count, local_days, width), returns.dtype),
        compiler_params=params(),
        name="pack_natural",
    )(returns)


def pack_assigned(returns, order, tile_count):
    local_days, group_width = returns.shape
    panel_count = group_width // PANEL
    per_device = panel_count // tile_count
    tiles_step = tile_count // 4

    def body(order_ref, in_ref, out_ref):
        step = pl.program_id(0)
        for piece in range(tiles_step):
            for slot in range(per_device):
                panel = order_ref[(step * tiles_step + piece) * per_device + slot]
                start = pl.multiple_of(panel * PANEL, PANEL)
                out_ref[piece, :, slot * PANEL : (slot + 1) * PANEL] = in_ref[:, pl.ds(start, PANEL)]

    return pl.pallas_call(
        body,
        grid_spec=pltpu.PrefetchScalarGridSpec(
            num_scalar_prefetch=1,
            grid=(tile_count // tiles_step,),
            in_specs=[pl.BlockSpec((local_days, group_width), lambda i, order: (0, 0))],
            out_specs=pl.BlockSpec((tiles_step, local_days, per_device * PANEL), lambda i, order: (i, 0, 0)),
        ),
        out_shape=jax.ShapeDtypeStruct((tile_count, local_days, per_device * PANEL), returns.dtype),
        compiler_params=params(),
        name="pack_assigned",
    )(order, returns)


def prepare_band(band_full, band_spans):
    block = 256

    def body(spans_ref, band_ref, masked_ref, mask_ref):
        day = lax.broadcasted_iota(jnp.int32, (block, DAYS), 1)
        first = spans_ref[:, 0:1]
        last = spans_ref[:, 1:2]
        inside = (day >= first) & (day <= last)
        flipped = jnp.transpose(band_ref[...].astype(jnp.float32))
        masked_ref[...] = jnp.where(inside, flipped, 0.0).astype(jnp.bfloat16)
        mask_ref[...] = jnp.where(inside, 1.0, 0.0).astype(jnp.bfloat16)

    shape = jax.ShapeDtypeStruct((BAND, DAYS), jnp.bfloat16)
    return pl.pallas_call(
        body,
        grid=(BAND // block,),
        in_specs=[
            pl.BlockSpec((block, 2), lambda i: (i, 0)),
            pl.BlockSpec((DAYS, block), lambda i: (0, i)),
        ],
        out_specs=[pl.BlockSpec((block, DAYS), lambda i: (i, 0))] * 2,
        out_shape=[shape, shape],
        compiler_params=params(),
        name="prepare_band",
    )(jnp.transpose(band_spans), band_full)


def covariance(band_masked, band_mask, band_columns, column_spans, column_returns, width):
    first = column_spans[0:1, :]
    last = column_spans[1:2, :]
    day = lax.broadcasted_iota(jnp.int32, (DAYS, width), 0)
    inside = (day >= first) & (day <= last)
    masked = jnp.where(inside, column_returns.astype(jnp.float32), 0.0).astype(jnp.bfloat16)
    mask = jnp.where(inside, 1.0, 0.0).astype(jnp.bfloat16)
    gram = jnp.dot(band_masked, masked, preferred_element_type=jnp.float32)
    column_sum = jnp.dot(band_mask, masked, preferred_element_type=jnp.float32)
    band_sum = jnp.dot(band_masked, mask, preferred_element_type=jnp.float32)
    common = jnp.minimum(band_columns[:, 1:2], last) - jnp.maximum(band_columns[:, 0:1], first) + 1
    correlation = jnp.maximum(common, 0).astype(jnp.float32)
    at_least = jnp.maximum(correlation, 1.0)
    degrees = jnp.maximum(correlation - 1.0, 1.0)
    return (gram * at_least - band_sum * column_sum) / (at_least * degrees)


def natural_tiles(fetched, spans, band_masked, band_mask, band_columns, tile_index):
    width = 256
    total = fetched.shape[1]
    steps = total // width

    def body(where_ref, spans_ref, band_ref, masked_ref, mask_ref, in_ref, rows_ref, columns_ref):
        result = covariance(
            masked_ref[...], mask_ref[...], band_ref[...], spans_ref[...], in_ref[...], width
        )
        rows_ref[...] = result.astype(jnp.bfloat16)
        columns_ref[0] = jnp.transpose(result).astype(jnp.bfloat16)

    whole = pl.BlockSpec((BAND, DAYS), lambda i, where: (0, 0))
    return pl.pallas_call(
        body,
        grid_spec=pltpu.PrefetchScalarGridSpec(
            num_scalar_prefetch=1,
            grid=(steps,),
            in_specs=[
                pl.BlockSpec((2, width), lambda i, where: (0, where[0] * steps + i)),
                pl.BlockSpec((BAND, 2), lambda i, where: (0, 0)),
                whole,
                whole,
                pl.BlockSpec((DAYS, width), lambda i, where: (0, i)),
            ],
            out_specs=[
                pl.BlockSpec((BAND, width), lambda i, where: (0, i)),
                pl.BlockSpec((1, width, BAND), lambda i, where: (0, i, 0)),
            ],
        ),
        out_shape=[
            jax.ShapeDtypeStruct((BAND, total), jnp.bfloat16),
            jax.ShapeDtypeStruct((1, total, BAND), jnp.bfloat16),
        ],
        compiler_params=params(),
        cost_estimate=pl.CostEstimate(flops=6 * BAND * DAYS * total, bytes_accessed=12 << 20, transcendentals=0),
        name="natural_tiles",
    )(tile_index[None], spans, band_columns, band_masked, band_mask, fetched)


def assigned_tiles(fetched, spans, band_masked, band_mask, band_columns, owned):
    width = 256
    halves = PANEL // width
    slots = fetched.shape[1] // PANEL

    def body(owned_ref, spans_ref, band_ref, masked_ref, mask_ref, in_ref, out_ref):
        result = covariance(
            masked_ref[...], mask_ref[...], band_ref[...], spans_ref[...], in_ref[...], width
        )
        out_ref[0, 0] = result.astype(jnp.bfloat16)

    whole = pl.BlockSpec((BAND, DAYS), lambda i, owned: (0, 0))
    return pl.pallas_call(
        body,
        grid_spec=pltpu.PrefetchScalarGridSpec(
            num_scalar_prefetch=1,
            grid=(slots * halves,),
            in_specs=[
                pl.BlockSpec((2, width), lambda i, owned: (0, owned[i // halves] * halves + i % halves)),
                pl.BlockSpec((BAND, 2), lambda i, owned: (0, 0)),
                whole,
                whole,
                pl.BlockSpec((DAYS, width), lambda i, owned: (0, i)),
            ],
            out_specs=pl.BlockSpec((1, 1, BAND, width), lambda i, owned: (0, i // halves, 0, i % halves)),
        ),
        out_shape=jax.ShapeDtypeStruct((1, slots, BAND, PANEL), jnp.bfloat16),
        compiler_params=params(),
        cost_estimate=pl.CostEstimate(flops=6 * BAND * DAYS * slots * PANEL, bytes_accessed=10 << 20, transcendentals=0),
        name="assigned_tiles",
    )(owned, spans, band_columns, band_masked, band_mask, fetched)


def unpack_rows(arrived):
    tile_count, rows, width = arrived.shape
    per_step = 8

    def body(in_ref, out_ref):
        for piece in range(per_step):
            out_ref[:, piece * width : (piece + 1) * width] = in_ref[piece]

    return pl.pallas_call(
        body,
        grid=(tile_count // per_step,),
        in_specs=[pl.BlockSpec((per_step, rows, width), lambda i: (i, 0, 0))],
        out_specs=pl.BlockSpec((rows, per_step * width), lambda i: (0, i)),
        out_shape=jax.ShapeDtypeStruct((rows, tile_count * width), arrived.dtype),
        compiler_params=params(),
        name="unpack_rows",
    )(arrived)


def exchange(pieces):
    return lax.all_to_all(pieces, "tiles", split_axis=0, concat_axis=0, tiled=True)


def on_device(returns, security_spans, band_returns, band_spans, assignment):
    tile_count = lax.axis_size("tiles")
    tile_index = lax.axis_index("tiles")
    local_days, group_width = returns.shape
    per_device = group_width // PANEL // tile_count
    share = per_device * PANEL
    order = assignment[0]
    owned = lax.dynamic_slice_in_dim(order, tile_index * per_device, per_device)

    natural = exchange(pack_natural(returns, tile_count)).reshape(DAYS, share)
    band_part = lax.all_gather(band_returns, "rows", axis=1, tiled=True)
    band_full = lax.all_gather(band_part, "tiles", axis=0, tiled=True)
    assigned = exchange(pack_assigned(returns, order, tile_count)).reshape(DAYS, share)

    band_masked, band_mask = prepare_band(band_full, band_spans)
    band_columns = jnp.transpose(band_spans)
    rows, col_cov = natural_tiles(natural, security_spans, band_masked, band_mask, band_columns, tile_index)
    arrived = exchange(rows.reshape(tile_count, BAND // tile_count, share))
    tile_cov = assigned_tiles(assigned, security_spans, band_masked, band_mask, band_columns, owned)
    return (unpack_rows(arrived), col_cov, tile_cov)


def solution(mesh):
    placed = (P("tiles", "rows"), P(None, "rows"), P("tiles", "rows"), P(), P("rows", None))
    return jax.shard_map(
        on_device,
        mesh=mesh,
        in_specs=placed,
        out_specs=(P("tiles", "rows"), P("rows", "tiles", None), P("rows", "tiles", None, None)),
        check_vma=False,
    )
```

time: 414 us -> 211 us (0.51)
  matrix products: 105 us -> 0 us
  waiting for transfers between devices: 155 us -> 116 us
  local copies, waits for them, and re-layouts: 52.9 us -> 16.1 us
  other arithmetic: 30.4 us -> 0 us
  Pallas kernels: 0 us -> 26.1 us
  between operations: 24.3 us -> 14.2 us
  starting transfers between devices: 33.3 us -> 27.3 us
    dot_general x13 -> x0, matrix products: 105 us -> none  [add_block(): lax.dot_general(left_block, right_block, (((0,), (0,)), ((), ())), prefer...]
    all_to_all x3, waiting for transfers between devices: 125 us -> 75.5 us  [exchange(): lax.all_to_all(pieces, 'tiles', split_axis=0, concat_axis=0, tiled=True)]
    pallas_call x0 -> x6, Pallas kernels: none -> 26.1 us  [the longest x1 10.2 us: natural_tiles(): pl.pallas_call(body, grid_spec=pltpu.PrefetchScalarGridSpec(num_scalar_pr...]
    another operation x3 -> x0, local copies, waits for them, and re-layouts: 12.1 us -> none
    gather x5 -> x0, local copies, waits for them, and re-layouts: 11.3 us -> none  [the longest x3 8.74 us: on_device(): jnp.take(panel_view, owner_order, axis=1)]
    all_gather x1, waiting for transfers between devices: 30.2 us -> 40.5 us  [on_device(): band_full = lax.all_gather(band_part, 'tiles', axis=0, tiled=True)]
    another operation x2 -> x0, other arithmetic: 10.3 us -> none  [stacked_tiles(): return jnp.stack(finished, axis=0)]
    unnamed x25 -> x33, local copies, waits for them, and re-layouts: 5.91 us -> 16.1 us
  transfers between devices with their start and end apart: 4 -> 4, of which waited for: 4 -> 3; matrix products, arithmetic and copies ran while one was open for 5% -> 0% of each run, Pallas kernels for 0% -> 11%
where the time goes in v1:
time: 211 us
  waiting for transfers between devices  116 us (55%)
  starting transfers between devices  27.3 us (13%)
  Pallas kernels  26.1 us (12%)
  local copies, waits for them, and re-layouts  16.1 us (8%)
  between operations  14.2 us (7%)
  blocking collectives  11 us (5%)
    all_to_all x3, waiting for transfers between devices, exchange(): lax.all_to_all(pieces, 'tiles', split_axis=0, concat_axis=0, tiled=True)  75.5 us
    all_gather x1, waiting for transfers between devices, on_device(): band_full = lax.all_gather(band_part, 'tiles', axis=0, tiled=True)  40.5 us
    all_to_all x3, starting transfers between devices, exchange(): lax.all_to_all(pieces, 'tiles', split_axis=0, concat_axis=0, tiled=True)  27.3 us
    unnamed x33, local copies, waits for them, and re-layouts  16.1 us
    all_gather x1, blocking collectives, on_device(): band_part = lax.all_gather(band_returns, 'rows', axis=1, tiled=True)  11 us
    pallas_call x1, Pallas kernels, natural_tiles(): pl.pallas_call(body, grid_spec=pltpu.PrefetchScalarGridSpec(num_scalar_pr...  10.2 us
    pallas_call x1, Pallas kernels, assigned_tiles(): pl.pallas_call(body, grid_spec=pltpu.PrefetchScalarGridSpec(num_scalar_pr...  9.53 us
  transfers between devices with their start and end apart: 4, of which 3 were waited for; matrix products, arithmetic and copies ran while one was open for 0% of the time, Pallas kernels for 11%

profile of v1, /device:TPU:1, one launch (start us, length us, event | category | flops | bytes accessed | tf_op | source)
XLA Modules:
  0.0 210.9 jit_solution(2114434879558920091)
XLA Ops:
  7.2 0.0 copy-start
  7.2 1.6 copy-done
  8.8 0.4 pack_natural.1
  9.2 0.0 copy-start.3
  9.2 1.3 copy-done.3
  10.5 13.3 %all-to-all-start = ((bf16[64,16,1024]{2,1,0:T(8,128)(2,1)}), bf16[64,16,1024]{2,1,0:T(8,128)(2,1)}, u32[]{:S(2)}, u32[]{:S(2)}) async-start(bf16[64,16,1024]{2,1,0:T(8,128)(2,1)} %copy-done.3), calls=%async_computation | async-start | bytes 4194304 | tf_op jit(solution)/shard_map/all_to_all | solution.py:205
  23.8 0.0 all-gather.2.cloned.1.call-start
  23.9 11.0 %all_gather.6 = bf16[16,1024]{1,0:T(8,128)(2,1)} all-gather(bf16[16,256]{1,0:T(8,128)(2,1)S(1)} %copy-done.15), channel_id=1, replica_groups=mesh['tiles'=64,'rows'=4] {'rows'}, dimensions={1}, use_global_device_ids=true | all-gather | bytes 40960 | tf_op jit(solution)/shard_map/all_gather | solution.py:218
  34.9 0.0 all-gather.2.cloned.1.call-update
  35.0 0.8 pack_assigned.1
  35.8 1.3 copy-done.2
  37.1 38.7 %all-to-all-done = bf16[64,16,1024]{2,1,0:T(8,128)(2,1)} async-done(((bf16[64,16,1024]{2,1,0:T(8,128)(2,1)}), bf16[64,16,1024]{2,1,0:T(8,128)(2,1)}, u32[]{:S(2)}, u32[]{:S(2)}) %all-to-all-start) | async-done | bytes 2097184 | tf_op jit(solution)/shard_map/all_to_all | solution.py:205
  75.8 6.3 %all-to-all-start.2 = ((bf16[64,16,1024]{2,1,0:T(8,128)(2,1)}), bf16[64,16,1024]{2,1,0:T(8,128)(2,1)S(1)}, u32[]{:S(2)}, u32[]{:S(2)}) async-start(bf16[64,16,1024]{2,1,0:T(8,128)(2,1)} %copy-done.2), calls=%async_computation.2 | async-start | bytes 4194304 | tf_op jit(solution)/shard_map/all_to_all | solution.py:205
  82.1 0.0 copy-start.13
  82.1 0.2 copy.8
  82.3 40.5 %all-gather.2.cloned.1.call-done.band_ref = bf16[1024,1024]{1,0:T(8,128)(2,1)} async-done(((bf16[16,1024]{1,0:T(8,128)(2,1)}), bf16[1024,1024]{1,0:T(8,128)(2,1)}) %all-gather.2.cloned.1.call-update) | async-done | bytes 2097168 | tf_op jit(solution)/shard_map/all_gather | solution.py:219
  122.9 1.6 copy-done.4
  124.5 2.2 %prepare_band.1 = (bf16[1024,1024]{1,0:T(8,128)(2,1)S(1)}, bf16[1024,1024]{1,0:T(8,128)(2,1)S(1)}) custom-call(s32[1024,2]{1,0:T(8,128)S(1)} %bitcast.8, bf16[1024,1024]{1,0:T(8,128)(2,1)S(1)} %copy-done.4), custom_call_target="tpu_custom_call" | custom-call | tf_op jit(solution)/shard_map/prepare_band/pallas_call | solution.py:81
  126.7 10.2 %natural_tiles.1 = (bf16[1024,1024]{1,0:T(8,128)(2,1)S(1)}, bf16[1,1024,1024]{2,1,0:T(8,128)(2,1)}) custom-call(s32[1]{0:T(128)} %bitcast.where_ref, s32[2,65536]{1,0:T(2,128)S(1)} %copy-done.13, s32[1024,2]{1,0:T(8,128)S(1)} %bitcast.9, bf16[1024,1024]{1,0:T(8,128)(2,1)S(1)} %get-tuple-element.7.masked_ref, ...), custom_call_target="tpu_custom_call" | custom-call | flops 6442450944 | bytes 12582912 | tf_op jit(solution)/shard_map/natural_tiles/pallas_call | solution.py:125
  136.9 1.3 copy-done.7
  138.2 1.3 copy-done.9
  139.5 1.3 copy-done.11
  140.8 0.0 all-to-all-done.2
  140.8 1.3 copy-done.5
  142.1 7.7 %all-to-all-start.1 = ((bf16[64,16,1024]{2,1,0:T(8,128)(2,1)}), bf16[64,16,1024]{2,1,0:T(8,128)(2,1)S(1)}, u32[]{:S(2)}, u32[]{:S(2)}) async-start(bf16[64,16,1024]{2,1,0:T(8,128)(2,1)} %bitcast.12), calls=%async_computation.1 | async-start | bytes 4194304 | tf_op jit(solution)/shard_map/all_to_all | solution.py:205
  149.8 0.1 dynamic-slice_bitcast_fusion.owned_ref
  149.9 1.6 copy-done.6
  151.5 1.6 copy-done.10
  153.1 1.6 copy-done.12
  154.7 9.5 %assigned_tiles.1 = bf16[1,2,1024,512]{3,2,1,0:T(8,128)(2,1)} custom-call(s32[2]{0:T(128)S(1)} %dynamic-slice_bitcast_fusion.owned_ref, s32[2,65536]{1,0:T(2,128)S(1)} %copy-done.13, s32[1024,2]{1,0:T(8,128)S(1)} %bitcast.10, bf16[1024,1024]{1,0:T(8,128)(2,1)S(1)} %copy-done.10, bf16[1024,1024]{1,0:T(8,128)(2,1)S(1)} %copy-done.12, ...), custom_call_target="tpu_custom_call" | custom-call | flops 6442450944 | bytes 10485760 | tf_op jit(solution)/shard_map/assigned_tiles/pallas_call | solution.py:164
  164.2 36.9 %all-to-all-done.1.in_ref = bf16[64,16,1024]{2,1,0:T(8,128)(2,1)S(1)} async-done(((bf16[64,16,1024]{2,1,0:T(8,128)(2,1)}), bf16[64,16,1024]{2,1,0:T(8,128)(2,1)S(1)}, u32[]{:S(2)}, u32[]{:S(2)}) %all-to-all-start.1) | async-done | bytes 2097184 | tf_op jit(solution)/shard_map/all_to_all | solution.py:205
  201.1 3.0 %unpack_rows.1 = bf16[16,65536]{1,0:T(8,128)(2,1)} custom-call(bf16[64,16,1024]{2,1,0:T(8,128)(2,1)S(1)} %all-to-all-done.1.in_ref), custom_call_target="tpu_custom_call" | custom-call | tf_op jit(solution)/shard_map/unpack_rows/pallas_call | solution.py:193
  (18 shorter events, 0.0 us)
Async XLA Ops:
  7.2 1.6 copy-start
  9.2 1.3 copy-start.3
  10.5 13.4 %copy-start.15 = (bf16[16,256]{1,0:T(8,128)(2,1)S(1)}, bf16[16,256]{1,0:T(8,128)(2,1)}, u32[]{:S(2)}) copy-start(bf16[16,256]{1,0:T(8,128)(2,1)} %param.7) | copy-start | bytes 24580
  10.5 24.4 %copy-start.1 = (bf16[16,65536]{1,0:T(8,128)(2,1)S(1)}, bf16[16,65536]{1,0:T(8,128)(2,1)}, u32[]{:S(2)}) copy-start(bf16[16,65536]{1,0:T(8,128)(2,1)} %in_ref.3) | copy-start | bytes 6291460
  10.5 24.4 %copy-start.8 = (s32[1,128]{1,0:T(1,128)S(1)}, s32[1,128]{1,0:T(1,128)}, u32[]{:S(2)}) copy-start(s32[1,128]{1,0:T(1,128)} %param.9) | copy-start | bytes 1540
  10.5 65.2 %all-to-all-start = ((bf16[64,16,1024]{2,1,0:T(8,128)(2,1)}), bf16[64,16,1024]{2,1,0:T(8,128)(2,1)}, u32[]{:S(2)}, u32[]{:S(2)}) async-start(bf16[64,16,1024]{2,1,0:T(8,128)(2,1)} %copy-done.3), calls=%async_computation | async-start | bytes 4194304 | tf_op jit(solution)/shard_map/all_to_all | solution.py:205
  23.8 99.0 %all-gather.2.cloned.1.call-start = ((), (), s32[]{:S(2)}) async-start(), calls=%async_computation.3 | async-start | bytes 2129920 | tf_op jit(solution)/shard_map/all_gather | solution.py:219
  35.8 1.3 copy-start.2
  37.1 45.0 %copy-start.14 = (s32[2,1024]{1,0:T(2,128)S(1)}, s32[2,1024]{1,0:T(2,128)}, u32[]{:S(2)}) copy-start(s32[2,1024]{1,0:T(2,128)} %param.8) | copy-start | bytes 24580
  75.8 65.1 %all-to-all-start.2 = ((bf16[64,16,1024]{2,1,0:T(8,128)(2,1)}), bf16[64,16,1024]{2,1,0:T(8,128)(2,1)S(1)}, u32[]{:S(2)}, u32[]{:S(2)}) async-start(bf16[64,16,1024]{2,1,0:T(8,128)(2,1)} %copy-done.2), calls=%async_computation.2 | async-start | bytes 4194304 | tf_op jit(solution)/shard_map/all_to_all | solution.py:205
  82.1 44.6 %copy-start.13 = (s32[2,65536]{1,0:T(2,128)S(1)}, s32[2,65536]{1,0:T(2,128)}, u32[]{:S(2)}) copy-start(s32[2,65536]{1,0:T(2,128)} %spans_ref.3) | copy-start | bytes 1572868
  122.9 1.6 copy-start.4
  136.9 1.3 copy-start.7
  138.2 1.3 copy-start.9
  139.5 1.3 copy-start.11
  140.8 1.3 copy-start.5
  142.1 58.9 %all-to-all-start.1 = ((bf16[64,16,1024]{2,1,0:T(8,128)(2,1)}), bf16[64,16,1024]{2,1,0:T(8,128)(2,1)S(1)}, u32[]{:S(2)}, u32[]{:S(2)}) async-start(bf16[64,16,1024]{2,1,0:T(8,128)(2,1)} %bitcast.12), calls=%async_computation.1 | async-start | bytes 4194304 | tf_op jit(solution)/shard_map/all_to_all | solution.py:205
  149.9 1.6 copy-start.6
  151.5 1.6 copy-start.10
  153.1 1.6 copy-start.12
Sparse Core Ops, SparseCore 0:
  35.1 87.7 all-gather.1

commit v2 on v1

--- a/solution.py
+++ b/solution.py
@@ -1,5 +1,3 @@
-import functools
-
 import jax
 import jax.numpy as jnp
 from jax import lax
@@ -10,31 +8,39 @@
 DAYS = 1024
 PANEL = 512
 BAND = 1024
-VMEM_LIMIT = 40 * 1024 * 1024
+N_Y = 4
+N_C = 2
+PART = BAND // (N_Y * N_C)
+VMEM_LIMIT = 24 * 1024 * 1024
 
 
 def params():
     return pltpu.CompilerParams(vmem_limit_bytes=VMEM_LIMIT)
 
 
-def pack_natural(returns, tile_count):
+def pack_natural(returns, band_returns, tile_count):
     local_days, group_width = returns.shape
     width = group_width // tile_count
-    per_step = 8
-
-    def body(in_ref, out_ref):
+    per_step = 16
+
+    def body(in_ref, band_ref, out_ref):
         for piece in range(per_step):
-            out_ref[piece] = in_ref[:, piece * width : (piece + 1) * width]
+            core = piece % N_C
+            out_ref[piece, :, :width] = in_ref[:, piece * width : (piece + 1) * width]
+            out_ref[piece, :, width:] = band_ref[:, core * PART : (core + 1) * PART]
 
     return pl.pallas_call(
         body,
         grid=(tile_count // per_step,),
-        in_specs=[pl.BlockSpec((local_days, per_step * width), lambda i: (0, i))],
-        out_specs=pl.BlockSpec((per_step, local_days, width), lambda i: (i, 0, 0)),
-        out_shape=jax.ShapeDtypeStruct((tile_count, local_days, width), returns.dtype),
+        in_specs=[
+            pl.BlockSpec((local_days, per_step * width), lambda i: (0, i)),
+            pl.BlockSpec((local_days, N_C * PART), lambda i: (0, 0)),
+        ],
+        out_specs=pl.BlockSpec((per_step, local_days, width + PART), lambda i: (i, 0, 0)),
+        out_shape=jax.ShapeDtypeStruct((tile_count, local_days, width + PART), returns.dtype),
         compiler_params=params(),
         name="pack_natural",
-    )(returns)
+    )(returns, band_returns)
 
 
 def pack_assigned(returns, order, tile_count):
@@ -65,31 +71,33 @@
     )(order, returns)
 
 
-def prepare_band(band_full, band_spans):
-    block = 256
-
-    def body(spans_ref, band_ref, masked_ref, mask_ref):
-        day = lax.broadcasted_iota(jnp.int32, (block, DAYS), 1)
-        first = spans_ref[:, 0:1]
-        last = spans_ref[:, 1:2]
-        inside = (day >= first) & (day <= last)
-        flipped = jnp.transpose(band_ref[...].astype(jnp.float32))
-        masked_ref[...] = jnp.where(inside, flipped, 0.0).astype(jnp.bfloat16)
-        mask_ref[...] = jnp.where(inside, 1.0, 0.0).astype(jnp.bfloat16)
-
+def prepare_band(own, swapped, band_columns, where):
+    def body(where_ref, spans_ref, own_ref, swapped_ref, masked_ref, mask_ref):
+        k = pl.program_id(0)
+        y, core = where_ref[1], where_ref[2]
+        day = lax.broadcasted_iota(jnp.int32, (PART, DAYS), 1)
+        for side, part_ref in ((0, own_ref), (1, swapped_ref)):
+            position = lax.rem(y - k + N_Y, N_Y) * N_C + lax.rem(core + side, N_C)
+            rows = pl.ds(pl.multiple_of(position * PART, PART), PART)
+            inside = (day >= spans_ref[rows, 0:1]) & (day <= spans_ref[rows, 1:2])
+            flipped = jnp.transpose(part_ref[0].astype(jnp.float32))
+            masked_ref[rows, :] = jnp.where(inside, flipped, 0.0).astype(jnp.bfloat16)
+            mask_ref[rows, :] = jnp.where(inside, 1.0, 0.0).astype(jnp.bfloat16)
+
+    part = pl.BlockSpec((1, DAYS, PART), lambda i, where: (i, 0, 0))
     shape = jax.ShapeDtypeStruct((BAND, DAYS), jnp.bfloat16)
     return pl.pallas_call(
         body,
-        grid=(BAND // block,),
-        in_specs=[
-            pl.BlockSpec((block, 2), lambda i: (i, 0)),
-            pl.BlockSpec((DAYS, block), lambda i: (0, i)),
-        ],
-        out_specs=[pl.BlockSpec((block, DAYS), lambda i: (i, 0))] * 2,
+        grid_spec=pltpu.PrefetchScalarGridSpec(
+            num_scalar_prefetch=1,
+            grid=(N_Y,),
+            in_specs=[pl.BlockSpec((BAND, 2), lambda i, where: (0, 0)), part, part],
+            out_specs=[pl.BlockSpec((BAND, DAYS), lambda i, where: (0, 0))] * 2,
+        ),
         out_shape=[shape, shape],
         compiler_params=params(),
         name="prepare_band",
-    )(jnp.transpose(band_spans), band_full)
+    )(where, band_columns, own, swapped)
 
 
 def covariance(band_masked, band_mask, band_columns, column_spans, column_returns, width):
@@ -109,9 +117,8 @@
     return (gram * at_least - band_sum * column_sum) / (at_least * degrees)
 
 
-def natural_tiles(fetched, spans, band_masked, band_mask, band_columns, tile_index):
+def natural_tiles(fetched, spans, band_masked, band_mask, band_columns, where, total):
     width = 256
-    total = fetched.shape[1]
     steps = total // width
 
     def body(where_ref, spans_ref, band_ref, masked_ref, mask_ref, in_ref, rows_ref, columns_ref):
@@ -146,7 +153,7 @@
         compiler_params=params(),
         cost_estimate=pl.CostEstimate(flops=6 * BAND * DAYS * total, bytes_accessed=12 << 20, transcendentals=0),
         name="natural_tiles",
-    )(tile_index[None], spans, band_columns, band_masked, band_mask, fetched)
+    )(where, spans, band_columns, band_masked, band_mask, fetched)
 
 
 def assigned_tiles(fetched, spans, band_masked, band_mask, band_columns, owned):
@@ -203,6 +210,14 @@
 
 def exchange(pieces):
     return lax.all_to_all(pieces, "tiles", split_axis=0, concat_axis=0, tiled=True)
+
+
+def shift_rows(array, step):
+    return lax.ppermute(array, "rows", [(y, (y + step) % N_Y) for y in range(N_Y)])
+
+
+def swap_cores(array):
+    return lax.ppermute(array, "tiles", [(i, i ^ 1) for i in range(lax.axis_size("tiles"))])
 
 
 def on_device(returns, security_spans, band_returns, band_spans, assignment):
@@ -214,14 +229,17 @@
     order = assignment[0]
     owned = lax.dynamic_slice_in_dim(order, tile_index * per_device, per_device)
 
-    natural = exchange(pack_natural(returns, tile_count)).reshape(DAYS, share)
-    band_part = lax.all_gather(band_returns, "rows", axis=1, tiled=True)
-    band_full = lax.all_gather(band_part, "tiles", axis=0, tiled=True)
+    where = jnp.stack([tile_index, lax.axis_index("rows"), tile_index % N_C]).astype(jnp.int32)
+
+    natural = exchange(pack_natural(returns, band_returns, tile_count)).reshape(DAYS, share + PART)
     assigned = exchange(pack_assigned(returns, order, tile_count)).reshape(DAYS, share)
 
-    band_masked, band_mask = prepare_band(band_full, band_spans)
+    mine = natural[:, share:]
+    own = jnp.stack([mine] + [shift_rows(mine, k) for k in range(1, N_Y)])
+    swapped = swap_cores(own)
     band_columns = jnp.transpose(band_spans)
-    rows, col_cov = natural_tiles(natural, security_spans, band_masked, band_mask, band_columns, tile_index)
+    band_masked, band_mask = prepare_band(own, swapped, band_columns, where)
+    rows, col_cov = natural_tiles(natural, security_spans, band_masked, band_mask, band_columns, where, share)
     arrived = exchange(rows.reshape(tile_count, BAND // tile_count, share))
     tile_cov = assigned_tiles(assigned, security_spans, band_masked, band_mask, band_columns, owned)
     return (unpack_rows(arrived), col_cov, tile_cov)

time: 211 us -> 194 us (0.919)
  between operations: 14.2 us -> 0.76 us
  blocking collectives: 11 us -> 0 us
  Pallas kernels: 26.1 us -> 30.4 us
  starting transfers between devices: 27.3 us -> 29.7 us
    all_gather x1 -> x0, waiting for transfers between devices: 40.5 us -> none  [on_device(): band_full = lax.all_gather(band_part, 'tiles', axis=0, tiled=True)]
    all_to_all x3, waiting for transfers between devices: 75.5 us -> 100 us  [exchange(): lax.all_to_all(pieces, 'tiles', split_axis=0, concat_axis=0, tiled=True)]
    ppermute x0 -> x4, waiting for transfers between devices: none -> 15.6 us  [the longest x3 14.3 us: shift_rows(): lax.ppermute(array, 'rows', [(y, (y + step) % N_Y) for y in range(N_Y)])]
    all_gather x1 -> x0, blocking collectives: 11 us -> none  [on_device(): band_part = lax.all_gather(band_returns, 'rows', axis=1, tiled=True)]
    ppermute x0 -> x4, starting transfers between devices: none -> 4.43 us  [the longest x3 3.85 us: shift_rows(): lax.ppermute(array, 'rows', [(y, (y + step) % N_Y) for y in range(N_Y)])]
    unnamed x33 -> x37, local copies, waits for them, and re-layouts: 16.1 us -> 15.8 us
  transfers between devices with their start and end apart: 4 -> 7, of which waited for: 3 -> 6; matrix products, arithmetic and copies ran while one was open for 0% -> 1% of each run, Pallas kernels for 11% -> 13%
where the time goes in v2:
time: 194 us
  waiting for transfers between devices  116 us (60%)
  Pallas kernels  30.4 us (16%)
  starting transfers between devices  29.7 us (15%)
  local copies, waits for them, and re-layouts  16.9 us (9%)
    all_to_all x3, waiting for transfers between devices, exchange(): lax.all_to_all(pieces, 'tiles', split_axis=0, concat_axis=0, tiled=True)  100 us
    all_to_all x3, starting transfers between devices, exchange(): lax.all_to_all(pieces, 'tiles', split_axis=0, concat_axis=0, tiled=True)  25.2 us
    unnamed x37, local copies, waits for them, and re-layouts  15.8 us
    ppermute x3, waiting for transfers between devices, shift_rows(): lax.ppermute(array, 'rows', [(y, (y + step) % N_Y) for y in range(N_Y)])  14.3 us
    pallas_call x1, Pallas kernels, natural_tiles(): pl.pallas_call(body, grid_spec=pltpu.PrefetchScalarGridSpec(num_scalar_pr...  11.1 us
    pallas_call x1, Pallas kernels, assigned_tiles(): pl.pallas_call(body, grid_spec=pltpu.PrefetchScalarGridSpec(num_scalar_pr...  9.53 us
    pallas_call x1, Pallas kernels, prepare_band(): pl.pallas_call(body, grid_spec=pltpu.PrefetchScalarGridSpec(num_scalar_pr...  3.93 us
  transfers between devices with their start and end apart: 7, of which 6 were waited for; matrix products, arithmetic and copies ran while one was open for 1% of the time, Pallas kernels for 13%

profile of v2, /device:TPU:1, one launch (start us, length us, event | category | flops | bytes accessed | tf_op | source)
XLA Modules:
  0.0 193.7 jit_solution(14885645610208228301)
XLA Ops:
  0.6 1.6 copy-done
  2.2 0.7 copy-done.9
  2.9 2.1 %pack_natural.1 = bf16[64,16,1152]{2,1,0:T(8,128)(2,1)} custom-call(bf16[16,65536]{1,0:T(8,128)(2,1)S(1)} %copy-done, bf16[16,256]{1,0:T(8,128)(2,1)S(1)} %copy-done.9), custom_call_target="tpu_custom_call" | custom-call | tf_op jit(solution)/shard_map/pack_natural/pallas_call | solution.py:32
  5.0 13.3 %all-to-all-start = ((bf16[64,16,1152]{2,1,0:T(8,128)(2,1)}), bf16[64,16,1152]{2,1,0:T(8,128)(2,1)}, u32[]{:S(2)}, u32[]{:S(2)}) async-start(bf16[64,16,1152]{2,1,0:T(8,128)(2,1)} %pack_natural.1), calls=%async_computation | async-start | bytes 4718592 | tf_op jit(solution)/shard_map/all_to_all | solution.py:212
  18.3 0.8 pack_assigned.1
  19.2 1.3 copy-done.2
  20.5 54.4 %all-to-all-done = bf16[64,16,1152]{2,1,0:T(8,128)(2,1)} async-done(((bf16[64,16,1152]{2,1,0:T(8,128)(2,1)}), bf16[64,16,1152]{2,1,0:T(8,128)(2,1)}, u32[]{:S(2)}, u32[]{:S(2)}) %all-to-all-start) | async-done | bytes 2359328 | tf_op jit(solution)/shard_map/all_to_all | solution.py:212
  74.9 6.0 %all-to-all-start.2 = ((bf16[64,16,1024]{2,1,0:T(8,128)(2,1)}), bf16[64,16,1024]{2,1,0:T(8,128)(2,1)S(1)}, u32[]{:S(2)}, u32[]{:S(2)}) async-start(bf16[64,16,1024]{2,1,0:T(8,128)(2,1)} %copy-done.2), calls=%async_computation.2 | async-start | bytes 4194304 | tf_op jit(solution)/shard_map/all_to_all | solution.py:212
  80.9 1.0 slice_bitcast_fusion
  81.9 2.8 %collective-permute-start.2 = (bf16[1024,128]{1,0:T(8,128)(2,1)S(1)}, bf16[1024,128]{1,0:T(8,128)(2,1)S(1)}, u32[]{:S(2)}, u32[]{:S(2)}) collective-permute-start(bf16[1024,128]{1,0:T(8,128)(2,1)S(1)} %get-tuple-element.12), channel_id=1, source_target_pairs={{0,3},{1,0},{2,1},{3,2},{4,7},{5,4},{6,5},{7,6},{8,11},{9,8},{10,9... | collective-permute-start | bytes 786440 | tf_op jit(solution)/shard_map/ppermute | solution.py:216
  84.7 0.3 collective-permute-start.1
  85.1 0.7 collective-permute-start
  85.8 9.7 %collective-permute-done.2 = bf16[1024,128]{1,0:T(8,128)(2,1)S(1)} collective-permute-done((bf16[1024,128]{1,0:T(8,128)(2,1)S(1)}, bf16[1024,128]{1,0:T(8,128)(2,1)S(1)}, u32[]{:S(2)}, u32[]{:S(2)}) %collective-permute-start.2) | collective-permute-done | bytes 262176 | tf_op jit(solution)/shard_map/ppermute | solution.py:216
  95.4 4.6 %collective-permute-done = bf16[1024,128]{1,0:T(8,128)(2,1)S(1)} collective-permute-done((bf16[1024,128]{1,0:T(8,128)(2,1)S(1)}, bf16[1024,128]{1,0:T(8,128)(2,1)S(1)}, u32[]{:S(2)}, u32[]{:S(2)}) %collective-permute-start) | collective-permute-done | bytes 262176 | tf_op jit(solution)/shard_map/ppermute | solution.py:216
  100.2 0.6 collective-permute-start.3
  100.8 1.0 copy.8
  101.9 1.3 collective-permute-done.3.swapped_ref
  103.2 1.0 copy-done.6
  104.3 3.9 %prepare_band.1 = (bf16[1024,1024]{1,0:T(8,128)(2,1)S(1)}, bf16[1024,1024]{1,0:T(8,128)(2,1)S(1)}) custom-call(s32[3]{0:T(128)S(1)} %pad_add_fusion.where_ref, s32[1024,2]{1,0:T(8,128)S(1)} %bitcast.17, bf16[4,1024,128]{2,1,0:T(8,128)(2,1)S(1)} %pad_maximum_fusion.own_ref, bf16[4,1024,128]{2,1,0:T(8,128)(2,1)} %collective-permute-done.3.swapped_ref), custom_call_target="tpu_custom_call" | custom-call | tf_op jit(solution)/shard_map/prepare_band/pallas_call | solution.py:89
  108.2 11.1 %natural_tiles.1 = (bf16[1024,1024]{1,0:T(8,128)(2,1)S(1)}, bf16[1,1024,1024]{2,1,0:T(8,128)(2,1)}) custom-call(s32[3]{0:T(128)S(1)} %pad_add_fusion.where_ref, s32[2,65536]{1,0:T(2,128)S(1)} %copy-done.15, s32[1024,2]{1,0:T(8,128)S(1)} %bitcast.18, bf16[1024,1024]{1,0:T(8,128)(2,1)S(1)} %get-tuple-element.7.masked_ref, ...), custom_call_target="tpu_custom_call" | custom-call | flops 6442450944 | bytes 12582912 | tf_op jit(solution)/shard_map/natural_tiles/pallas_call | solution.py:132
  119.3 1.3 copy-done.5
  120.6 1.3 copy-done.11
  121.9 1.3 copy-done.13
  123.2 8.9 %all-to-all-done.2 = bf16[64,16,1024]{2,1,0:T(8,128)(2,1)S(1)} async-done(((bf16[64,16,1024]{2,1,0:T(8,128)(2,1)}), bf16[64,16,1024]{2,1,0:T(8,128)(2,1)S(1)}, u32[]{:S(2)}, u32[]{:S(2)}) %all-to-all-start.2) | async-done | bytes 2097184 | tf_op jit(solution)/shard_map/all_to_all | solution.py:212
  132.1 1.4 copy-done.3
  133.5 5.9 %all-to-all-start.1 = ((bf16[64,16,1024]{2,1,0:T(8,128)(2,1)}), bf16[64,16,1024]{2,1,0:T(8,128)(2,1)S(1)}, u32[]{:S(2)}, u32[]{:S(2)}) async-start(bf16[64,16,1024]{2,1,0:T(8,128)(2,1)} %bitcast.16), calls=%async_computation.1 | async-start | bytes 4194304 | tf_op jit(solution)/shard_map/all_to_all | solution.py:212
  139.5 1.6 copy-done.4
  141.1 1.6 copy-done.12
  142.7 1.6 copy-done.14
  144.3 9.5 %assigned_tiles.1 = bf16[1,2,1024,512]{3,2,1,0:T(8,128)(2,1)} custom-call(s32[2]{0:T(128)S(1)} %dynamic-slice_bitcast_fusion.owned_ref, s32[2,65536]{1,0:T(2,128)S(1)} %copy-done.16, s32[1024,2]{1,0:T(8,128)S(1)} %bitcast.19, bf16[1024,1024]{1,0:T(8,128)(2,1)S(1)} %copy-done.12, bf16[1024,1024]{1,0:T(8,128)(2,1)S(1)} %copy-done.14, ...), custom_call_target="tpu_custom_call" | custom-call | flops 6442450944 | bytes 10485760 | tf_op jit(solution)/shard_map/assigned_tiles/pallas_call | solution.py:171
  153.8 36.9 %all-to-all-done.1.in_ref = bf16[64,16,1024]{2,1,0:T(8,128)(2,1)S(1)} async-done(((bf16[64,16,1024]{2,1,0:T(8,128)(2,1)}), bf16[64,16,1024]{2,1,0:T(8,128)(2,1)S(1)}, u32[]{:S(2)}, u32[]{:S(2)}) %all-to-all-start.1) | async-done | bytes 2097184 | tf_op jit(solution)/shard_map/all_to_all | solution.py:212
  190.7 3.0 %unpack_rows.1 = bf16[16,65536]{1,0:T(8,128)(2,1)} custom-call(bf16[64,16,1024]{2,1,0:T(8,128)(2,1)S(1)} %all-to-all-done.1.in_ref), custom_call_target="tpu_custom_call" | custom-call | tf_op jit(solution)/shard_map/unpack_rows/pallas_call | solution.py:200
  (29 shorter events, 0.3 us)
Async XLA Ops:
  0.6 1.6 copy-start
  2.2 0.7 copy-start.9
  5.0 13.3 %copy-start.1 = (bf16[16,65536]{1,0:T(8,128)(2,1)S(1)}, bf16[16,65536]{1,0:T(8,128)(2,1)}, u32[]{:S(2)}) copy-start(bf16[16,65536]{1,0:T(8,128)(2,1)} %in_ref.3) | copy-start | bytes 6291460
  5.0 13.3 %copy-start.10 = (s32[1,128]{1,0:T(1,128)S(1)}, s32[1,128]{1,0:T(1,128)}, u32[]{:S(2)}) copy-start(s32[1,128]{1,0:T(1,128)} %param.9) | copy-start | bytes 1540
  5.0 69.9 %all-to-all-start = ((bf16[64,16,1152]{2,1,0:T(8,128)(2,1)}), bf16[64,16,1152]{2,1,0:T(8,128)(2,1)}, u32[]{:S(2)}, u32[]{:S(2)}) async-start(bf16[64,16,1152]{2,1,0:T(8,128)(2,1)} %pack_natural.1), calls=%async_computation | async-start | bytes 4718592 | tf_op jit(solution)/shard_map/all_to_all | solution.py:212
  19.1 1.4 copy-start.2
  74.9 57.2 %all-to-all-start.2 = ((bf16[64,16,1024]{2,1,0:T(8,128)(2,1)}), bf16[64,16,1024]{2,1,0:T(8,128)(2,1)S(1)}, u32[]{:S(2)}, u32[]{:S(2)}) async-start(bf16[64,16,1024]{2,1,0:T(8,128)(2,1)} %copy-done.2), calls=%async_computation.2 | async-start | bytes 4194304 | tf_op jit(solution)/shard_map/all_to_all | solution.py:212
  80.9 19.9 %copy-start.17 = (s32[2,1024]{1,0:T(2,128)S(1)}, s32[2,1024]{1,0:T(2,128)}, u32[]{:S(2)}) copy-start(s32[2,1024]{1,0:T(2,128)} %param.8) | copy-start | bytes 24580
  81.9 13.5 %collective-permute-start.2 = (bf16[1024,128]{1,0:T(8,128)(2,1)S(1)}, bf16[1024,128]{1,0:T(8,128)(2,1)S(1)}, u32[]{:S(2)}, u32[]{:S(2)}) collective-permute-start(bf16[1024,128]{1,0:T(8,128)(2,1)S(1)} %get-tuple-element.12), channel_id=1, source_target_pairs={{0,3},{1,0},{2,1},{3,2},{4,7},{5,4},{6,5},{7,6},{8,11},{9,8},{10,9... | collective-permute-start | bytes 786440 | tf_op jit(solution)/shard_map/ppermute | solution.py:216
  84.7 10.7 %collective-permute-start.1 = (bf16[1024,128]{1,0:T(8,128)(2,1)S(1)}, bf16[1024,128]{1,0:T(8,128)(2,1)S(1)}, u32[]{:S(2)}, u32[]{:S(2)}) collective-permute-start(bf16[1024,128]{1,0:T(8,128)(2,1)S(1)} %get-tuple-element.12), channel_id=1, source_target_pairs={{0,2},{1,3},{2,0},{3,1},{4,6},{5,7},{6,4},{7,5},{8,10},{9,11},{10,... | collective-permute-start | bytes 786440 | tf_op jit(solution)/shard_map/ppermute | solution.py:216
  85.1 15.0 %collective-permute-start = (bf16[1024,128]{1,0:T(8,128)(2,1)S(1)}, bf16[1024,128]{1,0:T(8,128)(2,1)S(1)}, u32[]{:S(2)}, u32[]{:S(2)}) collective-permute-start(bf16[1024,128]{1,0:T(8,128)(2,1)S(1)} %get-tuple-element.12), channel_id=1, source_target_pairs={{0,1},{1,2},{2,3},{3,0},{4,5},{5,6},{6,7},{7,4},{8,9},{9,10},{10,1... | collective-permute-start | bytes 786440 | tf_op jit(solution)/shard_map/ppermute | solution.py:216
  100.2 3.0 %collective-permute-start.3 = (bf16[4,1024,128]{2,1,0:T(8,128)(2,1)S(1)}, bf16[4,1024,128]{2,1,0:T(8,128)(2,1)}, u32[]{:S(2)}, u32[]{:S(2)}) collective-permute-start(bf16[4,1024,128]{2,1,0:T(8,128)(2,1)S(1)} %pad_maximum_fusion.own_ref), channel_id=1, source_target_pairs={{0,4},{4,0},{8,12},{12,8},{16,20},{20,16},{24,28},{28,24},{32,36},... | collective-permute-start | bytes 3145736 | tf_op jit(solution)/shard_map/ppermute | solution.py:220
  103.2 1.0 copy-start.6
  104.3 3.9 %copy-start.7 = (s32[2,1024]{0,1:T(8,128)S(1)}, s32[2,1024]{0,1:T(8,128)}, u32[]{:S(2)}) copy-start(s32[2,1024]{0,1:T(8,128)} %copy.8) | copy-start | bytes 24580
  104.3 4.0 %copy-start.15 = (s32[2,65536]{1,0:T(2,128)S(1)}, s32[2,65536]{1,0:T(2,128)}, u32[]{:S(2)}) copy-start(s32[2,65536]{1,0:T(2,128)} %spans_ref.3) | copy-start | bytes 1572868
  119.3 1.3 copy-start.5
  120.6 1.3 copy-start.11
  121.9 1.3 copy-start.13
  132.1 1.4 copy-start.3
  133.5 6.0 %copy-start.8 = (s32[2,1024]{0,1:T(8,128)S(1)}, s32[2,1024]{0,1:T(8,128)}, u32[]{:S(2)}) copy-start(s32[2,1024]{0,1:T(8,128)} %copy.8) | copy-start | bytes 24580
  133.5 6.0 %copy-start.16 = (s32[2,65536]{1,0:T(2,128)S(1)}, s32[2,65536]{1,0:T(2,128)}, u32[]{:S(2)}) copy-start(s32[2,65536]{1,0:T(2,128)} %spans_ref.3) | copy-start | bytes 1572868
  133.5 57.2 %all-to-all-start.1 = ((bf16[64,16,1024]{2,1,0:T(8,128)(2,1)}), bf16[64,16,1024]{2,1,0:T(8,128)(2,1)S(1)}, u32[]{:S(2)}, u32[]{:S(2)}) async-start(bf16[64,16,1024]{2,1,0:T(8,128)(2,1)} %bitcast.16), calls=%async_computation.1 | async-start | bytes 4194304 | tf_op jit(solution)/shard_map/all_to_all | solution.py:212
  139.5 1.6 copy-start.4
  141.1 1.6 copy-start.12
  142.7 1.6 copy-start.14

commit v3 on v2

--- a/solution.py
+++ b/solution.py
@@ -12,16 +12,17 @@
 N_C = 2
 PART = BAND // (N_Y * N_C)
 VMEM_LIMIT = 24 * 1024 * 1024
-
-
-def params():
-    return pltpu.CompilerParams(vmem_limit_bytes=VMEM_LIMIT)
+LARGE = 56 * 1024 * 1024
+
+
+def params(limit=VMEM_LIMIT):
+    return pltpu.CompilerParams(vmem_limit_bytes=limit)
 
 
 def pack_natural(returns, band_returns, tile_count):
     local_days, group_width = returns.shape
     width = group_width // tile_count
-    per_step = 16
+    per_step = 32
 
     def body(in_ref, band_ref, out_ref):
         for piece in range(per_step):
@@ -38,7 +39,7 @@
         ],
         out_specs=pl.BlockSpec((per_step, local_days, width + PART), lambda i: (i, 0, 0)),
         out_shape=jax.ShapeDtypeStruct((tile_count, local_days, width + PART), returns.dtype),
-        compiler_params=params(),
+        compiler_params=params(LARGE),
         name="pack_natural",
     )(returns, band_returns)
 
@@ -191,7 +192,7 @@
 
 def unpack_rows(arrived):
     tile_count, rows, width = arrived.shape
-    per_step = 8
+    per_step = 32
 
     def body(in_ref, out_ref):
         for piece in range(per_step):

time: 194 us -> 191 us (0.985)
  local copies, waits for them, and re-layouts: 16.9 us -> 14.6 us
    unnamed x37 -> x33, local copies, waits for them, and re-layouts: 15.8 us -> 13.5 us
where the time goes in v3:
time: 191 us; the launch traced here: 190 us
  waiting for transfers between devices  116 us (61%)
  Pallas kernels  29.7 us (16%)
  starting transfers between devices  29.6 us (15%)
  local copies, waits for them, and re-layouts  14.6 us (8%)
    all_to_all x3, waiting for transfers between devices, exchange(): lax.all_to_all(pieces, 'tiles', split_axis=0, concat_axis=0, tiled=True)  99.9 us
    all_to_all x3, starting transfers between devices, exchange(): lax.all_to_all(pieces, 'tiles', split_axis=0, concat_axis=0, tiled=True)  25.2 us
    ppermute x3, waiting for transfers between devices, shift_rows(): lax.ppermute(array, 'rows', [(y, (y + step) % N_Y) for y in range(N_Y)])  14.3 us
    unnamed x33, local copies, waits for them, and re-layouts  13.5 us
    pallas_call x1, Pallas kernels, natural_tiles(): pl.pallas_call(body, grid_spec=pltpu.PrefetchScalarGridSpec(num_scalar_pr...  11 us
    pallas_call x1, Pallas kernels, assigned_tiles(): pl.pallas_call(body, grid_spec=pltpu.PrefetchScalarGridSpec(num_scalar_pr...  9.79 us
    pallas_call x1, Pallas kernels, prepare_band(): pl.pallas_call(body, grid_spec=pltpu.PrefetchScalarGridSpec(num_scalar_pr...  3.93 us
    ppermute x3, starting transfers between devices, shift_rows(): lax.ppermute(array, 'rows', [(y, (y + step) % N_Y) for y in range(N_Y)])  3.85 us
  transfers between devices with their start and end apart: 7, of which 6 were waited for; matrix products, arithmetic and copies ran while one was open for 1% of the time, Pallas kernels for 13%

profile of v3, /device:TPU:1, one launch (start us, length us, event | category | flops | bytes accessed | tf_op | source)
XLA Modules:
  0.0 190.5 jit_solution(14920152136997499508)
XLA Ops:
  0.6 2.8 %pack_natural.1 = bf16[64,16,1152]{2,1,0:T(8,128)(2,1)} custom-call(bf16[16,65536]{1,0:T(8,128)(2,1)} %in_ref.3, bf16[16,256]{1,0:T(8,128)(2,1)} %band_ref.1), custom_call_target="tpu_custom_call" | custom-call | tf_op jit(solution)/shard_map/pack_natural/pallas_call | solution.py:33
  3.4 13.3 %all-to-all-start = ((bf16[64,16,1152]{2,1,0:T(8,128)(2,1)}), bf16[64,16,1152]{2,1,0:T(8,128)(2,1)}, u32[]{:S(2)}, u32[]{:S(2)}) async-start(bf16[64,16,1152]{2,1,0:T(8,128)(2,1)} %pack_natural.1), calls=%async_computation | async-start | bytes 4718592 | tf_op jit(solution)/shard_map/all_to_all | solution.py:213
  16.7 0.8 pack_assigned.1
  17.5 1.3 copy-done.1
  18.9 54.4 %all-to-all-done = bf16[64,16,1152]{2,1,0:T(8,128)(2,1)} async-done(((bf16[64,16,1152]{2,1,0:T(8,128)(2,1)}), bf16[64,16,1152]{2,1,0:T(8,128)(2,1)}, u32[]{:S(2)}, u32[]{:S(2)}) %all-to-all-start) | async-done | bytes 2359328 | tf_op jit(solution)/shard_map/all_to_all | solution.py:213
  73.3 6.0 %all-to-all-start.2 = ((bf16[64,16,1024]{2,1,0:T(8,128)(2,1)}), bf16[64,16,1024]{2,1,0:T(8,128)(2,1)S(1)}, u32[]{:S(2)}, u32[]{:S(2)}) async-start(bf16[64,16,1024]{2,1,0:T(8,128)(2,1)} %copy-done.1), calls=%async_computation.2 | async-start | bytes 4194304 | tf_op jit(solution)/shard_map/all_to_all | solution.py:213
  79.3 1.0 slice_bitcast_fusion
  80.3 2.8 %collective-permute-start.2 = (bf16[1024,128]{1,0:T(8,128)(2,1)S(1)}, bf16[1024,128]{1,0:T(8,128)(2,1)S(1)}, u32[]{:S(2)}, u32[]{:S(2)}) collective-permute-start(bf16[1024,128]{1,0:T(8,128)(2,1)S(1)} %get-tuple-element.12), channel_id=1, source_target_pairs={{0,3},{1,0},{2,1},{3,2},{4,7},{5,4},{6,5},{7,6},{8,11},{9,8},{10,9... | collective-permute-start | bytes 786440 | tf_op jit(solution)/shard_map/ppermute | solution.py:217
  83.1 0.3 collective-permute-start.1
  83.5 0.7 collective-permute-start
  84.2 9.7 %collective-permute-done.2 = bf16[1024,128]{1,0:T(8,128)(2,1)S(1)} collective-permute-done((bf16[1024,128]{1,0:T(8,128)(2,1)S(1)}, bf16[1024,128]{1,0:T(8,128)(2,1)S(1)}, u32[]{:S(2)}, u32[]{:S(2)}) %collective-permute-start.2) | collective-permute-done | bytes 262176 | tf_op jit(solution)/shard_map/ppermute | solution.py:217
  93.8 4.6 %collective-permute-done = bf16[1024,128]{1,0:T(8,128)(2,1)S(1)} collective-permute-done((bf16[1024,128]{1,0:T(8,128)(2,1)S(1)}, bf16[1024,128]{1,0:T(8,128)(2,1)S(1)}, u32[]{:S(2)}, u32[]{:S(2)}) %collective-permute-start) | collective-permute-done | bytes 262176 | tf_op jit(solution)/shard_map/ppermute | solution.py:217
  98.5 0.1 pad_maximum_fusion.own_ref
  98.6 0.6 collective-permute-start.3
  99.2 1.0 copy.8
  100.2 0.1 pad_add_fusion.where_ref
  100.3 1.3 collective-permute-done.3.swapped_ref
  101.6 1.0 copy-done.5
  102.7 3.9 %prepare_band.1 = (bf16[1024,1024]{1,0:T(8,128)(2,1)S(1)}, bf16[1024,1024]{1,0:T(8,128)(2,1)S(1)}) custom-call(s32[3]{0:T(128)S(1)} %pad_add_fusion.where_ref, s32[1024,2]{1,0:T(8,128)S(1)} %bitcast.17, bf16[4,1024,128]{2,1,0:T(8,128)(2,1)S(1)} %pad_maximum_fusion.own_ref, bf16[4,1024,128]{2,1,0:T(8,128)(2,1)} %collective-permute-done.3.swapped_ref), custom_call_target="tpu_custom_call" | custom-call | tf_op jit(solution)/shard_map/prepare_band/pallas_call | solution.py:90
  106.6 11.0 %natural_tiles.1 = (bf16[1024,1024]{1,0:T(8,128)(2,1)S(1)}, bf16[1,1024,1024]{2,1,0:T(8,128)(2,1)}) custom-call(s32[3]{0:T(128)S(1)} %pad_add_fusion.where_ref, s32[2,65536]{1,0:T(2,128)S(1)} %copy-done.13, s32[1024,2]{1,0:T(8,128)S(1)} %bitcast.18, bf16[1024,1024]{1,0:T(8,128)(2,1)S(1)} %get-tuple-element.7.masked_ref, ...), custom_call_target="tpu_custom_call" | custom-call | flops 6442450944 | bytes 12582912 | tf_op jit(solution)/shard_map/natural_tiles/pallas_call | solution.py:133
  117.6 1.3 copy-done.4
  118.9 1.3 copy-done.9
  120.3 1.3 copy-done.11
  121.6 9.0 %all-to-all-done.2 = bf16[64,16,1024]{2,1,0:T(8,128)(2,1)S(1)} async-done(((bf16[64,16,1024]{2,1,0:T(8,128)(2,1)}), bf16[64,16,1024]{2,1,0:T(8,128)(2,1)S(1)}, u32[]{:S(2)}, u32[]{:S(2)}) %all-to-all-start.2) | async-done | bytes 2097184 | tf_op jit(solution)/shard_map/all_to_all | solution.py:213
  130.5 1.3 copy-done.2
  131.9 5.9 %all-to-all-start.1 = ((bf16[64,16,1024]{2,1,0:T(8,128)(2,1)}), bf16[64,16,1024]{2,1,0:T(8,128)(2,1)S(1)}, u32[]{:S(2)}, u32[]{:S(2)}) async-start(bf16[64,16,1024]{2,1,0:T(8,128)(2,1)} %bitcast.16), calls=%async_computation.1 | async-start | bytes 4194304 | tf_op jit(solution)/shard_map/all_to_all | solution.py:213
  137.9 1.6 copy-done.3
  139.5 1.6 copy-done.10
  141.1 1.6 copy-done.12
  142.7 9.8 %assigned_tiles.1 = bf16[1,2,1024,512]{3,2,1,0:T(8,128)(2,1)} custom-call(s32[2]{0:T(128)S(1)} %dynamic-slice_bitcast_fusion.owned_ref, s32[2,65536]{1,0:T(2,128)S(1)} %copy-done.14, s32[1024,2]{1,0:T(8,128)S(1)} %bitcast.19, bf16[1024,1024]{1,0:T(8,128)(2,1)S(1)} %copy-done.10, bf16[1024,1024]{1,0:T(8,128)(2,1)S(1)} %copy-done.12, ...), custom_call_target="tpu_custom_call" | custom-call | flops 6442450944 | bytes 10485760 | tf_op jit(solution)/shard_map/assigned_tiles/pallas_call | solution.py:172
  152.5 36.6 %all-to-all-done.1.in_ref = bf16[64,16,1024]{2,1,0:T(8,128)(2,1)S(1)} async-done(((bf16[64,16,1024]{2,1,0:T(8,128)(2,1)}), bf16[64,16,1024]{2,1,0:T(8,128)(2,1)S(1)}, u32[]{:S(2)}, u32[]{:S(2)}) %all-to-all-start.1) | async-done | bytes 2097184 | tf_op jit(solution)/shard_map/all_to_all | solution.py:213
  189.1 1.4 unpack_rows.1
  (25 shorter events, 0.1 us)
Async XLA Ops:
  3.4 13.3 %copy-start = (bf16[16,65536]{1,0:T(8,128)(2,1)S(1)}, bf16[16,65536]{1,0:T(8,128)(2,1)}, u32[]{:S(2)}) copy-start(bf16[16,65536]{1,0:T(8,128)(2,1)} %in_ref.3) | copy-start | bytes 6291460
  3.4 13.3 %copy-start.8 = (s32[1,128]{1,0:T(1,128)S(1)}, s32[1,128]{1,0:T(1,128)}, u32[]{:S(2)}) copy-start(s32[1,128]{1,0:T(1,128)} %param.9) | copy-start | bytes 1540
  3.4 69.9 %all-to-all-start = ((bf16[64,16,1152]{2,1,0:T(8,128)(2,1)}), bf16[64,16,1152]{2,1,0:T(8,128)(2,1)}, u32[]{:S(2)}, u32[]{:S(2)}) async-start(bf16[64,16,1152]{2,1,0:T(8,128)(2,1)} %pack_natural.1), calls=%async_computation | async-start | bytes 4718592 | tf_op jit(solution)/shard_map/all_to_all | solution.py:213
  17.5 1.3 copy-start.1
  73.3 57.2 %all-to-all-start.2 = ((bf16[64,16,1024]{2,1,0:T(8,128)(2,1)}), bf16[64,16,1024]{2,1,0:T(8,128)(2,1)S(1)}, u32[]{:S(2)}, u32[]{:S(2)}) async-start(bf16[64,16,1024]{2,1,0:T(8,128)(2,1)} %copy-done.1), calls=%async_computation.2 | async-start | bytes 4194304 | tf_op jit(solution)/shard_map/all_to_all | solution.py:213
  79.3 19.9 %copy-start.15 = (s32[2,1024]{1,0:T(2,128)S(1)}, s32[2,1024]{1,0:T(2,128)}, u32[]{:S(2)}) copy-start(s32[2,1024]{1,0:T(2,128)} %param.8) | copy-start | bytes 24580
  80.3 13.5 %collective-permute-start.2 = (bf16[1024,128]{1,0:T(8,128)(2,1)S(1)}, bf16[1024,128]{1,0:T(8,128)(2,1)S(1)}, u32[]{:S(2)}, u32[]{:S(2)}) collective-permute-start(bf16[1024,128]{1,0:T(8,128)(2,1)S(1)} %get-tuple-element.12), channel_id=1, source_target_pairs={{0,3},{1,0},{2,1},{3,2},{4,7},{5,4},{6,5},{7,6},{8,11},{9,8},{10,9... | collective-permute-start | bytes 786440 | tf_op jit(solution)/shard_map/ppermute | solution.py:217
  83.1 10.7 %collective-permute-start.1 = (bf16[1024,128]{1,0:T(8,128)(2,1)S(1)}, bf16[1024,128]{1,0:T(8,128)(2,1)S(1)}, u32[]{:S(2)}, u32[]{:S(2)}) collective-permute-start(bf16[1024,128]{1,0:T(8,128)(2,1)S(1)} %get-tuple-element.12), channel_id=1, source_target_pairs={{0,2},{1,3},{2,0},{3,1},{4,6},{5,7},{6,4},{7,5},{8,10},{9,11},{10,... | collective-permute-start | bytes 786440 | tf_op jit(solution)/shard_map/ppermute | solution.py:217
  83.5 15.0 %collective-permute-start = (bf16[1024,128]{1,0:T(8,128)(2,1)S(1)}, bf16[1024,128]{1,0:T(8,128)(2,1)S(1)}, u32[]{:S(2)}, u32[]{:S(2)}) collective-permute-start(bf16[1024,128]{1,0:T(8,128)(2,1)S(1)} %get-tuple-element.12), channel_id=1, source_target_pairs={{0,1},{1,2},{2,3},{3,0},{4,5},{5,6},{6,7},{7,4},{8,9},{9,10},{10,1... | collective-permute-start | bytes 786440 | tf_op jit(solution)/shard_map/ppermute | solution.py:217
  98.6 3.0 %collective-permute-start.3 = (bf16[4,1024,128]{2,1,0:T(8,128)(2,1)S(1)}, bf16[4,1024,128]{2,1,0:T(8,128)(2,1)}, u32[]{:S(2)}, u32[]{:S(2)}) collective-permute-start(bf16[4,1024,128]{2,1,0:T(8,128)(2,1)S(1)} %pad_maximum_fusion.own_ref), channel_id=1, source_target_pairs={{0,4},{4,0},{8,12},{12,8},{16,20},{20,16},{24,28},{28,24},{32,36},... | collective-permute-start | bytes 3145736 | tf_op jit(solution)/shard_map/ppermute | solution.py:221
  101.6 1.0 copy-start.5
  102.7 3.9 %copy-start.6 = (s32[2,1024]{0,1:T(8,128)S(1)}, s32[2,1024]{0,1:T(8,128)}, u32[]{:S(2)}) copy-start(s32[2,1024]{0,1:T(8,128)} %copy.8) | copy-start | bytes 24580
  102.7 4.0 %copy-start.13 = (s32[2,65536]{1,0:T(2,128)S(1)}, s32[2,65536]{1,0:T(2,128)}, u32[]{:S(2)}) copy-start(s32[2,65536]{1,0:T(2,128)} %spans_ref.3) | copy-start | bytes 1572868
  117.6 1.3 copy-start.4
  118.9 1.3 copy-start.9
  120.3 1.3 copy-start.11
  130.5 1.3 copy-start.2
  131.9 6.0 %copy-start.7 = (s32[2,1024]{0,1:T(8,128)S(1)}, s32[2,1024]{0,1:T(8,128)}, u32[]{:S(2)}) copy-start(s32[2,1024]{0,1:T(8,128)} %copy.8) | copy-start | bytes 24580
  131.9 6.0 %copy-start.14 = (s32[2,65536]{1,0:T(2,128)S(1)}, s32[2,65536]{1,0:T(2,128)}, u32[]{:S(2)}) copy-start(s32[2,65536]{1,0:T(2,128)} %spans_ref.3) | copy-start | bytes 1572868
  131.9 57.2 %all-to-all-start.1 = ((bf16[64,16,1024]{2,1,0:T(8,128)(2,1)}), bf16[64,16,1024]{2,1,0:T(8,128)(2,1)S(1)}, u32[]{:S(2)}, u32[]{:S(2)}) async-start(bf16[64,16,1024]{2,1,0:T(8,128)(2,1)} %bitcast.16), calls=%async_computation.1 | async-start | bytes 4194304 | tf_op jit(solution)/shard_map/all_to_all | solution.py:213
  137.9 1.6 copy-start.3
  139.5 1.6 copy-start.10
  141.1 1.6 copy-start.12

commit v4 on v0

v4 whole, which is shorter than its diff:
```python
import jax
import jax.numpy as jnp
from jax import lax
from jax.experimental import pallas as pl
from jax.experimental.pallas import tpu as pltpu
from jax.sharding import PartitionSpec as P

DAYS = 1024
PANEL = 512
BAND = 1024
N_X, N_Z, N_C, N_Y = 4, 8, 2, 4
PLANE = N_X * N_Z * N_C
LOCAL = DAYS // PLANE
QUARTER = BAND // N_Y
SLOTS = 2
SHARE = SLOTS * PANEL
WIDTH = 256
MAIN = SHARE + PANEL
FORCED = (1, 7, 2, 6, 3, 5, 4)
PLANE_X = N_X * N_C
SHIFTS = [(0, 0), (1, 0), (3, 0), (2, 0), (0, 1), (1, 1), (3, 1), (2, 1)]
VMEM_LIMIT = 56 * 1024 * 1024


def params(limit=VMEM_LIMIT):
    return pltpu.CompilerParams(vmem_limit_bytes=limit)


def shape(*sizes, dtype=jnp.bfloat16):
    return jax.ShapeDtypeStruct(sizes, dtype)


def whole(*sizes):
    return pl.BlockSpec(sizes, lambda i, *_: (0,) * len(sizes))


def pack(returns, order, where):
    def body(order_ref, where_ref, in_ref, main_ref, *out_refs):
        def panel(owner, slot):
            start = pl.multiple_of(order_ref[owner * SLOTS + slot] * PANEL, PANEL)
            return in_ref[:, pl.ds(start, PANEL)]

        for k in range(N_Z):
            z = lax.rem(where_ref[1] + k, N_Z)
            for x in range(N_X):
                for core in range(N_C):
                    owner = (x * N_Z + z) * N_C + core
                    place = x * N_C + core
                    out_refs[k][:, place * PANEL : (place + 1) * PANEL] = panel(owner, 1)
        for owner in range(PLANE):
            main_ref[owner, :, :SHARE] = in_ref[:, owner * SHARE : (owner + 1) * SHARE]
            main_ref[owner, :, SHARE:] = panel(owner, 0)

    return pl.pallas_call(
        body,
        grid_spec=pltpu.PrefetchScalarGridSpec(
            num_scalar_prefetch=2,
            grid=(1,),
            in_specs=[whole(*returns.shape)],
            out_specs=[whole(PLANE, LOCAL, MAIN)] + [whole(LOCAL, PLANE_X * PANEL)] * N_Z,
        ),
        out_shape=[shape(PLANE, LOCAL, MAIN)] + [shape(LOCAL, PLANE_X * PANEL)] * N_Z,
        compiler_params=params(),
        name="pack",
    )(order, where, returns)


def repack(pieces, where):
    def body(where_ref, *refs):
        x, z, core = where_ref[0], where_ref[1], where_ref[2]
        for k in range(N_Z):
            rows = pl.ds(pl.multiple_of(lax.rem(z - k + N_Z, N_Z) * LOCAL, LOCAL), LOCAL)
            for j, (dx, dc) in enumerate(SHIFTS):
                target = lax.rem(x + dx, N_X) * N_C + lax.rem(core + dc, N_C)
                start = pl.multiple_of(target * PANEL, PANEL)
                refs[N_Z + j][rows, :] = refs[k][:, pl.ds(start, PANEL)]

    return pl.pallas_call(
        body,
        grid_spec=pltpu.PrefetchScalarGridSpec(
            num_scalar_prefetch=1,
            grid=(1,),
            in_specs=[whole(LOCAL, PLANE_X * PANEL)] * N_Z,
            out_specs=[whole(N_Z * LOCAL, PANEL)] * len(SHIFTS),
        ),
        out_shape=[shape(N_Z * LOCAL, PANEL)] * len(SHIFTS),
        compiler_params=params(),
        name="repack",
    )(where, *pieces)


def prepare_band(own, swapped, band_columns, where):
    def body(where_ref, spans_ref, own_ref, swapped_ref, masked_ref, mask_ref, days):
        k = pl.program_id(0)
        x, z, core, y = where_ref[0], where_ref[1], where_ref[2], where_ref[3]
        for side, part_ref in ((0, own_ref), (1, swapped_ref)):
            for j in range(N_X):
                for m in range(N_Z):
                    source = lax.rem(x - j + N_X, N_X) * N_Z + lax.rem(z - m // 2 - 4 * (m % 2) + N_Z, N_Z)
                    source = source * N_C + lax.rem(core + side, N_C)
                    days[pl.ds(pl.multiple_of(source * LOCAL, LOCAL), LOCAL), :] = part_ref[0, j, m * LOCAL : (m + 1) * LOCAL]
        rows = pl.ds(pl.multiple_of(lax.rem(y - k + N_Y, N_Y) * QUARTER, QUARTER), QUARTER)
        day = lax.broadcasted_iota(jnp.int32, (QUARTER, DAYS), 1)
        inside = (day >= spans_ref[rows, 0:1]) & (day <= spans_ref[rows, 1:2])
        flipped = jnp.transpose(days[...].astype(jnp.float32))
        masked_ref[rows, :] = jnp.where(inside, flipped, 0.0).astype(jnp.bfloat16)
        mask_ref[rows, :] = jnp.where(inside, 1.0, 0.0).astype(jnp.bfloat16)

    part = pl.BlockSpec((1, N_X, N_Z * LOCAL, QUARTER), lambda i, where: (i, 0, 0, 0))
    return pl.pallas_call(
        body,
        grid_spec=pltpu.PrefetchScalarGridSpec(
            num_scalar_prefetch=1,
            grid=(N_Y,),
            in_specs=[whole(BAND, 2), part, part],
            out_specs=[whole(BAND, DAYS)] * 2,
            scratch_shapes=[pltpu.VMEM((DAYS, QUARTER), jnp.bfloat16)],
        ),
        out_shape=[shape(BAND, DAYS)] * 2,
        compiler_params=params(),
        name="prepare_band",
    )(where, band_columns, own, swapped)


def listed(spans):
    day = lax.broadcasted_iota(jnp.int32, (DAYS, WIDTH), 0)
    return (day >= spans[0:1, :]) & (day <= spans[1:2, :])


def masked_returns(inside, column_returns):
    return jnp.where(inside, column_returns.astype(jnp.float32), 0.0).astype(jnp.bfloat16)


def factors(inside, spans, band_masked, band_columns):
    mask = jnp.where(inside, 1.0, 0.0).astype(jnp.bfloat16)
    band_sum = jnp.dot(band_masked, mask, preferred_element_type=jnp.float32)
    common = jnp.minimum(band_columns[:, 1:2], spans[1:2, :]) - jnp.maximum(band_columns[:, 0:1], spans[0:1, :]) + 1
    correlation = jnp.maximum(common, 0).astype(jnp.float32)
    scale = 1.0 / jnp.maximum(correlation - 1.0, 1.0)
    return scale, band_sum * scale / jnp.maximum(correlation, 1.0)


def covariance(spans, band_columns, band_masked, band_mask, column_returns):
    inside = listed(spans)
    masked = masked_returns(inside, column_returns)
    scale, mean = factors(inside, spans, band_masked, band_columns)
    gram = jnp.dot(band_masked, masked, preferred_element_type=jnp.float32)
    column_sum = jnp.dot(band_mask, masked, preferred_element_type=jnp.float32)
    return (gram * scale - column_sum * mean).astype(jnp.bfloat16)


def natural_rows(fetched, spans, band_masked, band_mask, band_columns, where):
    steps = SHARE // WIDTH

    def body(where_ref, spans_ref, band_ref, masked_ref, mask_ref, in_ref, rows_ref):
        rows_ref[...] = covariance(
            spans_ref[...], band_ref[...], masked_ref[...], mask_ref[...], in_ref[...]
        )

    return pl.pallas_call(
        body,
        grid_spec=pltpu.PrefetchScalarGridSpec(
            num_scalar_prefetch=1,
            grid=(steps,),
            in_specs=[
                pl.BlockSpec((2, WIDTH), lambda i, where: (0, where[4] * steps + i)),
                whole(BAND, 2),
                whole(BAND, DAYS),
                whole(BAND, DAYS),
                pl.BlockSpec((DAYS, WIDTH), lambda i, where: (0, i)),
            ],
            out_specs=pl.BlockSpec((BAND, WIDTH), lambda i, where: (0, i)),
        ),
        out_shape=shape(BAND, SHARE),
        compiler_params=params(),
        cost_estimate=pl.CostEstimate(flops=6 * BAND * DAYS * SHARE, bytes_accessed=12 << 20, transcendentals=0),
        name="natural_rows",
    )(where, spans, band_columns, band_masked, band_mask, fetched)


def flip(rows):
    def body(in_ref, out_ref):
        out_ref[0] = jnp.transpose(in_ref[...].astype(jnp.float32)).astype(jnp.bfloat16)

    return pl.pallas_call(
        body,
        grid=(SHARE // WIDTH,),
        in_specs=[pl.BlockSpec((BAND, WIDTH), lambda i: (0, i))],
        out_specs=pl.BlockSpec((1, WIDTH, BAND), lambda i: (0, i, 0)),
        out_shape=shape(1, SHARE, BAND),
        compiler_params=params(),
        name="flip",
    )(rows)


def assigned_first(fetched, spans, band_masked, band_mask, band_columns, owned):
    halves = PANEL // WIDTH

    def body(owned_ref, spans_ref, band_ref, masked_ref, mask_ref, in_ref, out_ref):
        out_ref[0, 0] = covariance(
            spans_ref[...], band_ref[...], masked_ref[...], mask_ref[...], in_ref[...]
        )

    return pl.pallas_call(
        body,
        grid_spec=pltpu.PrefetchScalarGridSpec(
            num_scalar_prefetch=1,
            grid=(halves,),
            in_specs=[
                pl.BlockSpec((2, WIDTH), lambda i, owned: (0, owned[0] * halves + i)),
                whole(BAND, 2),
                whole(BAND, DAYS),
                whole(BAND, DAYS),
                pl.BlockSpec((DAYS, WIDTH), lambda i, owned: (0, SHARE // WIDTH + i)),
            ],
            out_specs=pl.BlockSpec((1, 1, BAND, WIDTH), lambda i, owned: (0, 0, 0, i)),
        ),
        out_shape=shape(1, SLOTS, BAND, PANEL),
        compiler_params=params(),
        cost_estimate=pl.CostEstimate(flops=6 * BAND * DAYS * PANEL, bytes_accessed=6 << 20, transcendentals=0),
        name="assigned_first",
    )(owned, spans, band_columns, band_masked, band_mask, fetched)


def assigned_second(tiles, chunks, spans, band_masked, band_mask, band_columns, owned, where):
    halves = PANEL // WIDTH

    def body(owned_ref, where_ref, tiles_ref, spans_ref, band_ref, masked_ref, mask_ref, *refs):
        out_ref, days = refs[-2:]
        for j, (dx, dc) in enumerate(SHIFTS):
            x = lax.rem(where_ref[0] - dx + N_X, N_X)
            core = lax.rem(where_ref[2] + dc, N_C)
            for z in range(N_Z):
                start = pl.multiple_of(((x * N_Z + z) * N_C + core) * LOCAL, LOCAL)
                days[pl.ds(start, LOCAL), :] = refs[j][z * LOCAL : (z + 1) * LOCAL, :]
        out_ref[0, 0] = covariance(
            spans_ref[...], band_ref[...], masked_ref[...], mask_ref[...], days[...]
        )

    return pl.pallas_call(
        body,
        grid_spec=pltpu.PrefetchScalarGridSpec(
            num_scalar_prefetch=2,
            grid=(halves,),
            in_specs=[
                pl.BlockSpec(memory_space=pl.ANY),
                pl.BlockSpec((2, WIDTH), lambda i, owned, where: (0, owned[1] * halves + i)),
                whole(BAND, 2),
                whole(BAND, DAYS),
                whole(BAND, DAYS),
            ]
            + [pl.BlockSpec((N_Z * LOCAL, WIDTH), lambda i, owned, where: (0, i))] * len(SHIFTS),
            out_specs=pl.BlockSpec((1, 1, BAND, WIDTH), lambda i, owned, where: (0, 1, 0, i)),
            scratch_shapes=[pltpu.VMEM((DAYS, WIDTH), jnp.bfloat16)],
        ),
        out_shape=shape(1, SLOTS, BAND, PANEL),
        input_output_aliases={2: 0},
        compiler_params=params(),
        cost_estimate=pl.CostEstimate(flops=6 * BAND * DAYS * PANEL, bytes_accessed=6 << 20, transcendentals=0),
        name="assigned_second",
    )(owned, where, tiles, spans, band_columns, band_masked, band_mask, *chunks)


def unpack_rows(arrived):
    per_step = 32

    def body(in_ref, out_ref):
        for piece in range(per_step):
            out_ref[:, piece * SHARE : (piece + 1) * SHARE] = in_ref[piece]

    return pl.pallas_call(
        body,
        grid=(PLANE // per_step,),
        in_specs=[pl.BlockSpec((per_step, LOCAL, SHARE), lambda i: (i, 0, 0))],
        out_specs=pl.BlockSpec((LOCAL, per_step * SHARE), lambda i: (0, i)),
        out_shape=shape(LOCAL, PLANE * SHARE),
        compiler_params=params(24 * 1024 * 1024),
        name="unpack_rows",
    )(arrived)


def exchange(pieces):
    return lax.all_to_all(pieces, "tiles", split_axis=0, concat_axis=0, tiled=True)


def shift_rows(array, step):
    return lax.ppermute(array, "rows", [(y, (y + step) % N_Y) for y in range(N_Y)])


def swap(array, bit):
    return lax.ppermute(array, "tiles", [(i, i ^ bit) for i in range(PLANE)])


def shift(array, dx, dz, dc):
    def to(i):
        x, z, core = i // (N_Z * N_C) + dx, i // N_C % N_Z + dz, i % N_C + dc
        return (x % N_X * N_Z + z % N_Z) * N_C + core % N_C

    return lax.ppermute(array, "tiles", [(i, to(i)) for i in range(PLANE)])


def on_device(returns, security_spans, band_returns, band_spans, assignment):
    tile_index = lax.axis_index("tiles")
    x, z, core = tile_index // (N_Z * N_C), (tile_index // N_C) % N_Z, tile_index % N_C
    where = jnp.stack([x, z, core, lax.axis_index("rows"), tile_index]).astype(jnp.int32)
    order = assignment[0]
    owned = lax.dynamic_slice_in_dim(order, tile_index * SLOTS, SLOTS)
    band_columns = jnp.transpose(band_spans)

    packed, *sends = pack(returns, order, where)
    pair = jnp.concatenate([band_returns, shift(band_returns, 0, 4, 0)])
    pair, packed, sends = lax.optimization_barrier((pair, packed, sends))
    share = jnp.concatenate([pair] + [shift(pair, 0, k, 0) for k in range(1, 4)])
    packed, share = lax.optimization_barrier((packed, share))
    fetched = exchange(packed).reshape(DAYS, MAIN)
    own = jnp.stack([share] + [shift(share, j, 0, 0) for j in range(1, N_X)])
    own = jnp.stack([own] + [shift_rows(own, k) for k in range(1, N_Y)])
    swapped = swap(own, 1)
    band = prepare_band(own, swapped, band_columns, where)
    *band, sends = lax.optimization_barrier((*band, sends))
    pieces = [sends[0]] + [shift(sends[k], 0, k, 0) for k in range(1, N_Z)]

    rows = natural_rows(fetched, security_spans, *band, band_columns, where)
    rows, fetched, *forced = lax.optimization_barrier((rows, fetched, *(pieces[k] for k in FORCED)))
    for k, piece in zip(FORCED, forced):
        pieces[k] = piece
    arrived = exchange(rows.reshape(PLANE, BAND // PLANE, SHARE))
    col_cov = flip(rows)
    tiles = assigned_first(fetched, security_spans, *band, band_columns, owned)
    chunks = [shift(part, dx, 0, dc) if dx or dc else part for part, (dx, dc) in zip(repack(pieces, where), SHIFTS)]
    tile_cov = assigned_second(tiles, chunks, security_spans, *band, band_columns, owned, where)
    return (unpack_rows(arrived), col_cov, tile_cov)


def solution(mesh):
    placed = (P("tiles", "rows"), P(None, "rows"), P("tiles", "rows"), P(), P("rows", None))
    return jax.shard_map(
        on_device,
        mesh=mesh,
        in_specs=placed,
        out_specs=(P("tiles", "rows"), P("rows", "tiles", None), P("rows", "tiles", None, None)),
        check_vma=False,
    )
```

time: 414 us -> 187 us (0.45)
  matrix products: 105 us -> 0 us
  waiting for transfers between devices: 155 us -> 63.8 us
  local copies, waits for them, and re-layouts: 52.9 us -> 4.77 us
  Pallas kernels: 0 us -> 47.9 us
  starting transfers between devices: 33.3 us -> 69.4 us
  other arithmetic: 30.4 us -> 0.19 us
  between operations: 24.3 us -> 0.91 us
  blocking collectives: 10.9 us -> 0 us
    all_to_all x3 -> x2, waiting for transfers between devices: 125 us -> 10.3 us  [exchange(): lax.all_to_all(pieces, 'tiles', split_axis=0, concat_axis=0, tiled=True)]
    dot_general x13 -> x0, matrix products: 105 us -> none  [add_block(): lax.dot_general(left_block, right_block, (((0,), (0,)), ((), ())), prefer...]
    ppermute x0 -> x25, waiting for transfers between devices: none -> 53.5 us  [the longest x21 42.7 us: shift(): return lax.ppermute(array, 'tiles', [(i, to(i)) for i in range(PLANE)])]
    ppermute x0 -> x25, starting transfers between devices: none -> 51.2 us  [the longest x21 43.8 us: shift(): return lax.ppermute(array, 'tiles', [(i, to(i)) for i in range(PLANE)])]
    pallas_call x0 -> x8, Pallas kernels: none -> 47.9 us  [the longest x1 12 us: natural_rows(): pl.pallas_call(body, grid_spec=pltpu.PrefetchScalarGridSpec(num_scalar_pr...]
    all_gather x1 -> x0, waiting for transfers between devices: 30.2 us -> none  [on_device(): band_full = lax.all_gather(band_part, 'tiles', axis=0, tiled=True)]
    all_to_all x3 -> x2, starting transfers between devices: 33.3 us -> 18.2 us  [exchange(): lax.all_to_all(pieces, 'tiles', split_axis=0, concat_axis=0, tiled=True)]
    another operation x3 -> x1, local copies, waits for them, and re-layouts: 12.1 us -> 0.68 us  [on_device(): jnp.stack([x, z, core, lax.axis_index('rows'), tile_index])]
  transfers between devices with their start and end apart: 4 -> 27, of which waited for: 4 -> 14; matrix products, arithmetic and copies ran while one was open for 5% -> 1% of each run, Pallas kernels for 0% -> 25%
where the time goes in v4:
time: 187 us
  starting transfers between devices  69.4 us (37%)
  waiting for transfers between devices  63.8 us (34%)
  Pallas kernels  47.9 us (26%)
  local copies, waits for them, and re-layouts  4.77 us (3%)
    ppermute x21, starting transfers between devices, shift(): return lax.ppermute(array, 'tiles', [(i, to(i)) for i in range(PLANE)])  43.8 us
    ppermute x21, waiting for transfers between devices, shift(): return lax.ppermute(array, 'tiles', [(i, to(i)) for i in range(PLANE)])  42.7 us
    all_to_all x2, starting transfers between devices, exchange(): lax.all_to_all(pieces, 'tiles', split_axis=0, concat_axis=0, tiled=True)  18.2 us
    pallas_call x1, Pallas kernels, natural_rows(): pl.pallas_call(body, grid_spec=pltpu.PrefetchScalarGridSpec(num_scalar_pr...  12 us
    all_to_all x2, waiting for transfers between devices, exchange(): lax.all_to_all(pieces, 'tiles', split_axis=0, concat_axis=0, tiled=True)  10.3 us
    ppermute x3, waiting for transfers between devices, shift_rows(): lax.ppermute(array, 'rows', [(y, (y + step) % N_Y) for y in range(N_Y)])  9.51 us
    pallas_call x1, Pallas kernels, assigned_second(): pl.pallas_call(body, grid_spec=pltpu.PrefetchScalarGridSpec(num_scalar_pr...  8.26 us
    pallas_call x1, Pallas kernels, assigned_first(): pl.pallas_call(body, grid_spec=pltpu.PrefetchScalarGridSpec(num_scalar_pr...  8.02 us
  transfers between devices with their start and end apart: 27, of which 14 were waited for; matrix products, arithmetic and copies ran while one was open for 1% of the time, Pallas kernels for 25%

profile of v4, /device:TPU:1, one launch (start us, length us, event | category | flops | bytes accessed | tf_op | source)
XLA Modules:
  0.0 187.0 jit_solution(18110809056925349524)
XLA Ops:
  0.6 7.8 %collective-permute-start = (bf16[16,256]{1,0:T(8,128)(2,1)}, bf16[16,256]{1,0:T(8,128)(2,1)S(1)}, u32[]{:S(2)}, u32[]{:S(2)}) collective-permute-start(bf16[16,256]{1,0:T(8,128)(2,1)} %param.7), channel_id=1, source_target_pairs={{0,32},{4,36},{8,40},{12,44},{16,48},{20,52},{24,56},{28,60},{32,0... | collective-permute-start | bytes 24584 | tf_op jit(solution)/shard_map/ppermute | solution.py:299
  9.1 4.5 %pack.1 = (bf16[64,16,1536]{2,1,0:T(8,128)(2,1)}, bf16[16,4096]{1,0:T(8,128)(2,1)}, bf16[16,4096]{1,0:T(8,128)(2,1)}, bf16[16,4096]{1,0:T(8,128)(2,1)}, bf16[16,...) custom-call(s32[128]{0:T(128)} %bitcast.32, ...), custom_call_target="tpu_custom_call" | custom-call | tf_op jit(solution)/shard_map/pack/pallas_call | solution.py:54
  17.6 1.6 collective-permute-done.2
  19.2 2.2 %collective-permute-done.3 = bf16[32,256]{1,0:T(8,128)(2,1)S(1)} collective-permute-done((bf16[32,256]{1,0:T(8,128)(2,1)S(1)}, bf16[32,256]{1,0:T(8,128)(2,1)S(1)}, u32[]{:S(2)}, u32[]{:S(2)}) %collective-permute-start.3) | collective-permute-done | bytes 16416 | tf_op jit(solution)/shard_map/ppermute | solution.py:299
  21.5 10.1 %all-to-all-start = ((bf16[64,16,1536]{2,1,0:T(8,128)(2,1)}), bf16[64,16,1536]{2,1,0:T(8,128)(2,1)}, u32[]{:S(2)}, u32[]{:S(2)}) async-start(bf16[64,16,1536]{2,1,0:T(8,128)(2,1)} %get-tuple-element.77), calls=%async_computation | async-start | bytes 6291456 | tf_op jit(solution)/shard_map/all_to_all | solution.py:283
  31.6 2.9 %collective-permute-start.6 = (bf16[128,256]{1,0:T(8,128)(2,1)S(1)}, bf16[128,256]{1,0:T(8,128)(2,1)S(1)}, u32[]{:S(2)}, u32[]{:S(2)}) collective-permute-start(bf16[128,256]{1,0:T(8,128)(2,1)S(1)} %pad_maximum_fusion.2), channel_id=1, source_target_pairs={{0,192},{4,196},{8,200},{12,204},{16,208},{20,212},{24,216},{28,22... | collective-permute-start | bytes 196616 | tf_op jit(solution)/shard_map/ppermute | solution.py:299
  34.5 1.6 collective-permute-start.5
  36.1 5.8 %collective-permute-done.6 = bf16[128,256]{1,0:T(8,128)(2,1)S(1)} collective-permute-done((bf16[128,256]{1,0:T(8,128)(2,1)S(1)}, bf16[128,256]{1,0:T(8,128)(2,1)S(1)}, u32[]{:S(2)}, u32[]{:S(2)}) %collective-permute-start.6) | collective-permute-done | bytes 65568 | tf_op jit(solution)/shard_map/ppermute | solution.py:299
  43.1 2.0 %collective-permute-done.5 = bf16[128,256]{1,0:T(8,128)(2,1)S(1)} collective-permute-done((bf16[128,256]{1,0:T(8,128)(2,1)S(1)}, bf16[128,256]{1,0:T(8,128)(2,1)S(1)}, u32[]{:S(2)}, u32[]{:S(2)}) %collective-permute-start.5) | collective-permute-done | bytes 65568 | tf_op jit(solution)/shard_map/ppermute | solution.py:299
  46.5 2.6 %collective-permute-start.8 = (bf16[4,128,256]{2,1,0:T(8,128)(2,1)S(1)}, bf16[4,128,256]{2,1,0:T(8,128)(2,1)S(1)}, u32[]{:S(2)}, u32[]{:S(2)}) collective-permute-start(bf16[4,128,256]{2,1,0:T(8,128)(2,1)S(1)} %get-tuple-element.104), channel_id=1, source_target_pairs={{0,2},{1,3},{2,0},{3,1},{4,6},{5,7},{6,4},{7,5},{8,10},{9,11},{10,... | collective-permute-start | bytes 786440 | tf_op jit(solution)/shard_map/ppermute | solution.py:287
  50.2 2.8 %collective-permute-done.7 = bf16[4,128,256]{2,1,0:T(8,128)(2,1)S(1)} collective-permute-done((bf16[4,128,256]{2,1,0:T(8,128)(2,1)S(1)}, bf16[4,128,256]{2,1,0:T(8,128)(2,1)S(1)}, u32[]{:S(2)}, u32[]{:S(2)}) %collective-permute-start.7) | collective-permute-done | bytes 262176 | tf_op jit(solution)/shard_map/ppermute | solution.py:287
  53.0 6.7 %collective-permute-done.8 = bf16[4,128,256]{2,1,0:T(8,128)(2,1)S(1)} collective-permute-done((bf16[4,128,256]{2,1,0:T(8,128)(2,1)S(1)}, bf16[4,128,256]{2,1,0:T(8,128)(2,1)S(1)}, u32[]{:S(2)}, u32[]{:S(2)}) %collective-permute-start.8) | collective-permute-done | bytes 262176 | tf_op jit(solution)/shard_map/ppermute | solution.py:287
  59.9 2.4 %collective-permute-start.10 = (bf16[4,4,128,256]{3,2,1,0:T(8,128)(2,1)S(1)}, bf16[4,4,128,256]{3,2,1,0:T(8,128)(2,1)S(1)}, u32[]{:S(2)}, u32[]{:S(2)}) collective-permute-start(bf16[4,4,128,256]{3,2,1,0:T(8,128)(2,1)S(1)} %pad_maximum_fusion.own_ref), channel_id=1, source_target_pairs={{0,4},{4,0},{8,12},{12,8},{16,20},{20,16},{24,28},{28,24},{32,36},... | collective-permute-start | bytes 3145736 | tf_op jit(solution)/shard_map/ppermute | solution.py:291
  65.5 6.5 %prepare_band.1 = (bf16[1024,1024]{1,0:T(8,128)(2,1)}, bf16[1024,1024]{1,0:T(8,128)(2,1)}) custom-call(s32[5]{0:T(128)} %stack.53.where_ref, s32[1024,2]{1,0:T(8,128)} %bitcast.21, bf16[4,4,128,256]{3,2,1,0:T(8,128)(2,1)} %copy-done, bf16[4,4,128,256]{3,2,1,0:T(8,128)(2,1)} %copy-done.1), custom_call_target="tpu_custom_call" | custom-call | tf_op jit(solution)/shard_map/prepare_band/pallas_call | solution.py:110
  72.1 4.5 %collective-permute-start.11 = (bf16[16,4096]{1,0:T(8,128)(2,1)S(1)}, bf16[16,4096]{1,0:T(8,128)(2,1)S(1)}, u32[]{:S(2)}, u32[]{:S(2)}) collective-permute-start(bf16[16,4096]{1,0:T(8,128)(2,1)S(1)} %copy-done.17), channel_id=1, source_target_pairs={{0,8},{4,12},{8,16},{12,20},{16,24},{20,28},{24,32},{28,36},{32,40... | collective-permute-start | bytes 393224 | tf_op jit(solution)/shard_map/ppermute | solution.py:299
  78.0 2.3 %collective-permute-start.13 = (bf16[16,4096]{1,0:T(8,128)(2,1)}, bf16[16,4096]{1,0:T(8,128)(2,1)S(1)}, u32[]{:S(2)}, u32[]{:S(2)}) collective-permute-start(bf16[16,4096]{1,0:T(8,128)(2,1)} %get-tuple-element.80), channel_id=1, source_target_pairs={{0,16},{4,20},{8,24},{12,28},{16,32},{20,36},{24,40},{28,44},{32,4... | collective-permute-start | bytes 393224 | tf_op jit(solution)/shard_map/ppermute | solution.py:299
  82.7 21.8 %collective-permute-done.11.refs_1_ = bf16[16,4096]{1,0:T(8,128)(2,1)S(1)} collective-permute-done((bf16[16,4096]{1,0:T(8,128)(2,1)S(1)}, bf16[16,4096]{1,0:T(8,128)(2,1)S(1)}, u32[]{:S(2)}, u32[]{:S(2)}) %collective-permute-start.11) | collective-permute-done | bytes 131104 | tf_op jit(solution)/shard_map/ppermute | solution.py:299
  104.5 3.5 %collective-permute-start.16 = (bf16[16,4096]{1,0:T(8,128)(2,1)S(1)}, bf16[16,4096]{1,0:T(8,128)(2,1)S(1)}, u32[]{:S(2)}, u32[]{:S(2)}) collective-permute-start(bf16[16,4096]{1,0:T(8,128)(2,1)S(1)} %copy-done.13), channel_id=1, source_target_pairs={{0,40},{4,44},{8,48},{12,52},{16,56},{20,60},{24,0},{28,4},{32,8},... | collective-permute-start | bytes 393224 | tf_op jit(solution)/shard_map/ppermute | solution.py:299
  108.2 12.0 %natural_rows.1.in_ref = bf16[1024,1024]{1,0:T(8,128)(2,1)} custom-call(s32[5]{0:T(128)} %stack.53.where_ref, s32[2,65536]{1,0:T(2,128)} %spans_ref.5, s32[1024,2]{1,0:T(8,128)} %bitcast.22, bf16[1024,1024]{1,0:T(8,128)(2,1)} %get-tuple-element.75.masked_ref, bf16[1024,1024]{1,0:T(8,128)(2,1)} %get-tuple-element.76.mask_ref, bf16[1024,1536]{1,0:T(8,128)(2,1)} %bitcast.15.in_ref), custom_call_target="tpu_custom_call" | custom-call | flops 6442450944 | bytes 12582912 | tf_op jit(solution)/shard_map/natural_rows/pallas_call | solution.py:160
  121.0 4.5 %collective-permute-done.17.refs_4_ = bf16[16,4096]{1,0:T(8,128)(2,1)S(1)} collective-permute-done((bf16[16,4096]{1,0:T(8,128)(2,1)S(1)}, bf16[16,4096]{1,0:T(8,128)(2,1)S(1)}, u32[]{:S(2)}, u32[]{:S(2)}) %collective-permute-start.17) | collective-permute-done | bytes 131104 | tf_op jit(solution)/shard_map/ppermute | solution.py:299
  126.2 8.1 %all-to-all-start.1 = ((bf16[64,16,1024]{2,1,0:T(8,128)(2,1)}), bf16[64,16,1024]{2,1,0:T(8,128)(2,1)S(1)}, u32[]{:S(2)}, u32[]{:S(2)}) async-start(bf16[64,16,1024]{2,1,0:T(8,128)(2,1)} %bitcast.20), calls=%async_computation.1 | async-start | bytes 4194304 | tf_op jit(solution)/shard_map/all_to_all | solution.py:283
  134.3 3.0 %repack.1 = (bf16[128,512]{1,0:T(8,128)(2,1)}, bf16[128,512]{1,0:T(8,128)(2,1)}, bf16[128,512]{1,0:T(8,128)(2,1)}, bf16[128,512]{1,0:T(8,128)(2,1)}, bf16[128,51...) custom-call(s32[5]{0:T(128)} %stack.53.where_ref, ...), custom_call_target="tpu_custom_call" | custom-call | tf_op jit(solution)/shard_map/repack/pallas_call | solution.py:78
  137.4 1.4 collective-permute-start.18
  138.7 1.5 collective-permute-start.19
  140.9 1.6 collective-permute-start.20
  143.9 1.7 collective-permute-done.18.refs_1_
  145.7 3.7 %collective-permute-start.23 = (bf16[128,512]{1,0:T(8,128)(2,1)}, bf16[128,512]{1,0:T(8,128)(2,1)S(1)}, u32[]{:S(2)}, u32[]{:S(2)}) collective-permute-start(bf16[128,512]{1,0:T(8,128)(2,1)} %get-tuple-element.101), channel_id=1, source_target_pairs={{0,196},{4,192},{8,204},{12,200},{16,212},{20,208},{24,220},{28,21... | collective-permute-start | bytes 393224 | tf_op jit(solution)/shard_map/ppermute | solution.py:299
  149.4 4.7 %collective-permute-start.24 = (bf16[128,512]{1,0:T(8,128)(2,1)}, bf16[128,512]{1,0:T(8,128)(2,1)S(1)}, u32[]{:S(2)}, u32[]{:S(2)}) collective-permute-start(bf16[128,512]{1,0:T(8,128)(2,1)} %get-tuple-element.102), channel_id=1, source_target_pairs={{0,132},{4,128},{8,140},{12,136},{16,148},{20,144},{24,156},{28,15... | collective-permute-start | bytes 393224 | tf_op jit(solution)/shard_map/ppermute | solution.py:299
  154.0 8.0 %assigned_first.1.tiles_ref = bf16[1,2,1024,512]{3,2,1,0:T(8,128)(2,1)} custom-call(s32[2]{0:T(128)} %dynamic-slice_bitcast_fusion.owned_ref, s32[2,65536]{1,0:T(2,128)} %spans_ref.5, s32[1024,2]{1,0:T(8,128)} %bitcast.23, bf16[1024,1024]{1,0:T(8,128)(2,1)} %get-tuple-element.75.masked_ref, bf16[1024,1024]{1,0:T(8,128)(2,1)} %get-tuple-element.76.mask_ref, ...), custom_call_target="tpu_custom_call" | custom-call | flops 3221225472 | bytes 6291456 | tf_op jit(solution)/shard_map/assigned_first/pallas_call | solution.py:204
  162.1 4.1 %flip.1 = bf16[1,1024,1024]{2,1,0:T(8,128)(2,1)} custom-call(bf16[1024,1024]{1,0:T(8,128)(2,1)} %natural_rows.1.in_ref), custom_call_target="tpu_custom_call" | custom-call | tf_op jit(solution)/shard_map/flip/pallas_call | solution.py:185
  167.1 8.3 %assigned_second.1 = bf16[1,2,1024,512]{3,2,1,0:T(8,128)(2,1)} custom-call(s32[2]{0:T(128)} %dynamic-slice_bitcast_fusion.owned_ref, s32[5]{0:T(128)} %stack.53.where_ref, bf16[1,2,1024,512]{3,2,1,0:T(8,128)(2,1)} %assigned_first.1.tiles_ref, s32[2,65536]{1,0:T(2,128)} %spans_ref.5, s32[1024,2]{1,0:T(8,128)} %bitcast.24, ...), custom_call_target="tpu_custom_call", output_to_operand_aliasing={{}: (2, {})} | custom-call | flops 3221225472 | bytes 6291456 | tf_op jit(solution)/shard_map/assigned_second/pallas_call | solution.py:240
  175.3 10.3 %all-to-all-done.1.in_ref = bf16[64,16,1024]{2,1,0:T(8,128)(2,1)S(1)} async-done(((bf16[64,16,1024]{2,1,0:T(8,128)(2,1)}), bf16[64,16,1024]{2,1,0:T(8,128)(2,1)S(1)}, u32[]{:S(2)}, u32[]{:S(2)}) %all-to-all-start.1) | async-done | bytes 2097184 | tf_op jit(solution)/shard_map/all_to_all | solution.py:283
  (87 shorter events, 21.3 us)
Async XLA Ops:
  0.6 13.1 %collective-permute-start = (bf16[16,256]{1,0:T(8,128)(2,1)}, bf16[16,256]{1,0:T(8,128)(2,1)S(1)}, u32[]{:S(2)}, u32[]{:S(2)}) collective-permute-start(bf16[16,256]{1,0:T(8,128)(2,1)} %param.7), channel_id=1, source_target_pairs={{0,32},{4,36},{8,40},{12,44},{16,48},{20,52},{24,56},{28,60},{32,0... | collective-permute-start | bytes 24584 | tf_op jit(solution)/shard_map/ppermute | solution.py:299
  13.7 3.9 %collective-permute-start.1 = (bf16[32,256]{1,0:T(8,128)(2,1)S(1)}, bf16[32,256]{1,0:T(8,128)(2,1)S(1)}, u32[]{:S(2)}, u32[]{:S(2)}) collective-permute-start(bf16[32,256]{1,0:T(8,128)(2,1)S(1)} %pad_maximum_fusion.3), channel_id=1, source_target_pairs={{0,8},{4,12},{8,16},{12,20},{16,24},{20,28},{24,32},{28,36},{32,40... | collective-permute-start | bytes 49160 | tf_op jit(solution)/shard_map/ppermute | solution.py:299
  14.5 4.7 %collective-permute-start.2 = (bf16[32,256]{1,0:T(8,128)(2,1)S(1)}, bf16[32,256]{1,0:T(8,128)(2,1)S(1)}, u32[]{:S(2)}, u32[]{:S(2)}) collective-permute-start(bf16[32,256]{1,0:T(8,128)(2,1)S(1)} %pad_maximum_fusion.3), channel_id=1, source_target_pairs={{0,16},{4,20},{8,24},{12,28},{16,32},{20,36},{24,40},{28,44},{32,4... | collective-permute-start | bytes 49160 | tf_op jit(solution)/shard_map/ppermute | solution.py:299
  15.7 5.7 %collective-permute-start.3 = (bf16[32,256]{1,0:T(8,128)(2,1)S(1)}, bf16[32,256]{1,0:T(8,128)(2,1)S(1)}, u32[]{:S(2)}, u32[]{:S(2)}) collective-permute-start(bf16[32,256]{1,0:T(8,128)(2,1)S(1)} %pad_maximum_fusion.3), channel_id=1, source_target_pairs={{0,24},{4,28},{8,32},{12,36},{16,40},{20,44},{24,48},{28,52},{32,5... | collective-permute-start | bytes 49160 | tf_op jit(solution)/shard_map/ppermute | solution.py:299
  21.5 86.7 %all-to-all-start = ((bf16[64,16,1536]{2,1,0:T(8,128)(2,1)}), bf16[64,16,1536]{2,1,0:T(8,128)(2,1)}, u32[]{:S(2)}, u32[]{:S(2)}) async-start(bf16[64,16,1536]{2,1,0:T(8,128)(2,1)} %get-tuple-element.77), calls=%async_computation | async-start | bytes 6291456 | tf_op jit(solution)/shard_map/all_to_all | solution.py:283
  31.6 30.7 %copy-start.9 = (s32[2,1024]{1,0:T(2,128)S(1)}, s32[2,1024]{1,0:T(2,128)}, u32[]{:S(2)}) copy-start(s32[2,1024]{1,0:T(2,128)} %param.8) | copy-start | bytes 24580
  31.6 10.3 %collective-permute-start.6 = (bf16[128,256]{1,0:T(8,128)(2,1)S(1)}, bf16[128,256]{1,0:T(8,128)(2,1)S(1)}, u32[]{:S(2)}, u32[]{:S(2)}) collective-permute-start(bf16[128,256]{1,0:T(8,128)(2,1)S(1)} %pad_maximum_fusion.2), channel_id=1, source_target_pairs={{0,192},{4,196},{8,200},{12,204},{16,208},{20,212},{24,216},{28,22... | collective-permute-start | bytes 196616 | tf_op jit(solution)/shard_map/ppermute | solution.py:299
  34.5 8.6 %collective-permute-start.4 = (bf16[128,256]{1,0:T(8,128)(2,1)S(1)}, bf16[128,256]{1,0:T(8,128)(2,1)S(1)}, u32[]{:S(2)}, u32[]{:S(2)}) collective-permute-start(bf16[128,256]{1,0:T(8,128)(2,1)S(1)} %pad_maximum_fusion.2), channel_id=1, source_target_pairs={{0,64},{4,68},{8,72},{12,76},{16,80},{20,84},{24,88},{28,92},{32,9... | collective-permute-start | bytes 196616 | tf_op jit(solution)/shard_map/ppermute | solution.py:299
  34.5 10.6 %collective-permute-start.5 = (bf16[128,256]{1,0:T(8,128)(2,1)S(1)}, bf16[128,256]{1,0:T(8,128)(2,1)S(1)}, u32[]{:S(2)}, u32[]{:S(2)}) collective-permute-start(bf16[128,256]{1,0:T(8,128)(2,1)S(1)} %pad_maximum_fusion.2), channel_id=1, source_target_pairs={{0,128},{4,132},{8,136},{12,140},{16,144},{20,148},{24,152},{28,15... | collective-permute-start | bytes 196616 | tf_op jit(solution)/shard_map/ppermute | solution.py:299
  45.1 7.8 %collective-permute-start.7 = (bf16[4,128,256]{2,1,0:T(8,128)(2,1)S(1)}, bf16[4,128,256]{2,1,0:T(8,128)(2,1)S(1)}, u32[]{:S(2)}, u32[]{:S(2)}) collective-permute-start(bf16[4,128,256]{2,1,0:T(8,128)(2,1)S(1)} %get-tuple-element.104), channel_id=1, source_target_pairs={{0,1},{1,2},{2,3},{3,0},{4,5},{5,6},{6,7},{7,4},{8,9},{9,10},{10,1... | collective-permute-start | bytes 786440 | tf_op jit(solution)/shard_map/ppermute | solution.py:287
  46.5 13.2 %collective-permute-start.8 = (bf16[4,128,256]{2,1,0:T(8,128)(2,1)S(1)}, bf16[4,128,256]{2,1,0:T(8,128)(2,1)S(1)}, u32[]{:S(2)}, u32[]{:S(2)}) collective-permute-start(bf16[4,128,256]{2,1,0:T(8,128)(2,1)S(1)} %get-tuple-element.104), channel_id=1, source_target_pairs={{0,2},{1,3},{2,0},{3,1},{4,6},{5,7},{6,4},{7,5},{8,10},{9,11},{10,... | collective-permute-start | bytes 786440 | tf_op jit(solution)/shard_map/ppermute | solution.py:287
  49.1 10.6 %collective-permute-start.9 = (bf16[4,128,256]{2,1,0:T(8,128)(2,1)S(1)}, bf16[4,128,256]{2,1,0:T(8,128)(2,1)S(1)}, u32[]{:S(2)}, u32[]{:S(2)}) collective-permute-start(bf16[4,128,256]{2,1,0:T(8,128)(2,1)S(1)} %get-tuple-element.104), channel_id=1, source_target_pairs={{0,3},{1,0},{2,1},{3,2},{4,7},{5,4},{6,5},{7,6},{8,11},{9,8},{10,9... | collective-permute-start | bytes 786440 | tf_op jit(solution)/shard_map/ppermute | solution.py:287
  59.9 20.4 %copy-start.15 = (bf16[16,4096]{1,0:T(8,128)(2,1)S(1)}, bf16[16,4096]{1,0:T(8,128)(2,1)}, u32[]{:S(2)}) copy-start(bf16[16,4096]{1,0:T(8,128)(2,1)} %get-tuple-element.81) | copy-start | bytes 393220
  59.9 21.7 %copy-start.14 = (bf16[16,4096]{1,0:T(8,128)(2,1)S(1)}, bf16[16,4096]{1,0:T(8,128)(2,1)}, u32[]{:S(2)}) copy-start(bf16[16,4096]{1,0:T(8,128)(2,1)} %get-tuple-element.82) | copy-start | bytes 393220
  59.9 44.6 %copy-start.13 = (bf16[16,4096]{1,0:T(8,128)(2,1)S(1)}, bf16[16,4096]{1,0:T(8,128)(2,1)}, u32[]{:S(2)}) copy-start(bf16[16,4096]{1,0:T(8,128)(2,1)} %get-tuple-element.83) | copy-start | bytes 393220
  59.9 48.1 %copy-start.12 = (bf16[16,4096]{1,0:T(8,128)(2,1)S(1)}, bf16[16,4096]{1,0:T(8,128)(2,1)}, u32[]{:S(2)}) copy-start(bf16[16,4096]{1,0:T(8,128)(2,1)} %get-tuple-element.84) | copy-start | bytes 393220
  59.9 4.7 %collective-permute-start.10 = (bf16[4,4,128,256]{3,2,1,0:T(8,128)(2,1)S(1)}, bf16[4,4,128,256]{3,2,1,0:T(8,128)(2,1)S(1)}, u32[]{:S(2)}, u32[]{:S(2)}) collective-permute-start(bf16[4,4,128,256]{3,2,1,0:T(8,128)(2,1)S(1)} %pad_maximum_fusion.own_ref), channel_id=1, source_target_pairs={{0,4},{4,0},{8,12},{12,8},{16,20},{20,16},{24,28},{28,24},{32,36},... | collective-permute-start | bytes 3145736 | tf_op jit(solution)/shard_map/ppermute | solution.py:291
  72.1 32.5 %collective-permute-start.11 = (bf16[16,4096]{1,0:T(8,128)(2,1)S(1)}, bf16[16,4096]{1,0:T(8,128)(2,1)S(1)}, u32[]{:S(2)}, u32[]{:S(2)}) collective-permute-start(bf16[16,4096]{1,0:T(8,128)(2,1)S(1)} %copy-done.17), channel_id=1, source_target_pairs={{0,8},{4,12},{8,16},{12,20},{16,24},{20,28},{24,32},{28,36},{32,40... | collective-permute-start | bytes 393224 | tf_op jit(solution)/shard_map/ppermute | solution.py:299
  76.6 31.4 %collective-permute-start.12 = (bf16[16,4096]{1,0:T(8,128)(2,1)S(1)}, bf16[16,4096]{1,0:T(8,128)(2,1)S(1)}, u32[]{:S(2)}, u32[]{:S(2)}) collective-permute-start(bf16[16,4096]{1,0:T(8,128)(2,1)S(1)} %copy-done.16), channel_id=1, source_target_pairs={{0,56},{4,60},{8,0},{12,4},{16,8},{20,12},{24,16},{28,20},{32,24},... | collective-permute-start | bytes 393224 | tf_op jit(solution)/shard_map/ppermute | solution.py:299
  78.0 42.3 %collective-permute-start.13 = (bf16[16,4096]{1,0:T(8,128)(2,1)}, bf16[16,4096]{1,0:T(8,128)(2,1)S(1)}, u32[]{:S(2)}, u32[]{:S(2)}) collective-permute-start(bf16[16,4096]{1,0:T(8,128)(2,1)} %get-tuple-element.80), channel_id=1, source_target_pairs={{0,16},{4,20},{8,24},{12,28},{16,32},{20,36},{24,40},{28,44},{32,4... | collective-permute-start | bytes 393224 | tf_op jit(solution)/shard_map/ppermute | solution.py:299
  80.2 40.0 %collective-permute-start.14 = (bf16[16,4096]{1,0:T(8,128)(2,1)S(1)}, bf16[16,4096]{1,0:T(8,128)(2,1)S(1)}, u32[]{:S(2)}, u32[]{:S(2)}) collective-permute-start(bf16[16,4096]{1,0:T(8,128)(2,1)S(1)} %copy-done.15), channel_id=1, source_target_pairs={{0,48},{4,52},{8,56},{12,60},{16,0},{20,4},{24,8},{28,12},{32,16},... | collective-permute-start | bytes 393224 | tf_op jit(solution)/shard_map/ppermute | solution.py:299
  81.5 39.5 %collective-permute-start.15 = (bf16[16,4096]{1,0:T(8,128)(2,1)S(1)}, bf16[16,4096]{1,0:T(8,128)(2,1)S(1)}, u32[]{:S(2)}, u32[]{:S(2)}) collective-permute-start(bf16[16,4096]{1,0:T(8,128)(2,1)S(1)} %copy-done.14), channel_id=1, source_target_pairs={{0,24},{4,28},{8,32},{12,36},{16,40},{20,44},{24,48},{28,52},{32,5... | collective-permute-start | bytes 393224 | tf_op jit(solution)/shard_map/ppermute | solution.py:299
  104.5 16.5 %collective-permute-start.16 = (bf16[16,4096]{1,0:T(8,128)(2,1)S(1)}, bf16[16,4096]{1,0:T(8,128)(2,1)S(1)}, u32[]{:S(2)}, u32[]{:S(2)}) collective-permute-start(bf16[16,4096]{1,0:T(8,128)(2,1)S(1)} %copy-done.13), channel_id=1, source_target_pairs={{0,40},{4,44},{8,48},{12,52},{16,56},{20,60},{24,0},{28,4},{32,8},... | collective-permute-start | bytes 393224 | tf_op jit(solution)/shard_map/ppermute | solution.py:299
  108.0 17.5 %collective-permute-start.17 = (bf16[16,4096]{1,0:T(8,128)(2,1)S(1)}, bf16[16,4096]{1,0:T(8,128)(2,1)S(1)}, u32[]{:S(2)}, u32[]{:S(2)}) collective-permute-start(bf16[16,4096]{1,0:T(8,128)(2,1)S(1)} %copy-done.12), channel_id=1, source_target_pairs={{0,32},{4,36},{8,40},{12,44},{16,48},{20,52},{24,56},{28,60},{32,0... | collective-permute-start | bytes 393224 | tf_op jit(solution)/shard_map/ppermute | solution.py:299
  126.2 59.4 %all-to-all-start.1 = ((bf16[64,16,1024]{2,1,0:T(8,128)(2,1)}), bf16[64,16,1024]{2,1,0:T(8,128)(2,1)S(1)}, u32[]{:S(2)}, u32[]{:S(2)}) async-start(bf16[64,16,1024]{2,1,0:T(8,128)(2,1)} %bitcast.20), calls=%async_computation.1 | async-start | bytes 4194304 | tf_op jit(solution)/shard_map/all_to_all | solution.py:283
  137.4 8.3 %collective-permute-start.18 = (bf16[128,512]{1,0:T(8,128)(2,1)}, bf16[128,512]{1,0:T(8,128)(2,1)S(1)}, u32[]{:S(2)}, u32[]{:S(2)}) collective-permute-start(bf16[128,512]{1,0:T(8,128)(2,1)} %get-tuple-element.96), channel_id=1, source_target_pairs={{0,64},{4,68},{8,72},{12,76},{16,80},{20,84},{24,88},{28,92},{32,9... | collective-permute-start | bytes 393224 | tf_op jit(solution)/shard_map/ppermute | solution.py:299
  138.7 10.6 %collective-permute-start.19 = (bf16[128,512]{1,0:T(8,128)(2,1)}, bf16[128,512]{1,0:T(8,128)(2,1)S(1)}, u32[]{:S(2)}, u32[]{:S(2)}) collective-permute-start(bf16[128,512]{1,0:T(8,128)(2,1)} %get-tuple-element.97), channel_id=1, source_target_pairs={{0,192},{4,196},{8,200},{12,204},{16,208},{20,212},{24,216},{28,22... | collective-permute-start | bytes 393224 | tf_op jit(solution)/shard_map/ppermute | solution.py:299
  140.9 25.4 %collective-permute-start.20 = (bf16[128,512]{1,0:T(8,128)(2,1)}, bf16[128,512]{1,0:T(8,128)(2,1)S(1)}, u32[]{:S(2)}, u32[]{:S(2)}) collective-permute-start(bf16[128,512]{1,0:T(8,128)(2,1)} %get-tuple-element.98), channel_id=1, source_target_pairs={{0,128},{4,132},{8,136},{12,140},{16,144},{20,148},{24,152},{28,15... | collective-permute-start | bytes 393224 | tf_op jit(solution)/shard_map/ppermute | solution.py:299
  142.4 23.8 %collective-permute-start.21 = (bf16[128,512]{1,0:T(8,128)(2,1)}, bf16[128,512]{1,0:T(8,128)(2,1)S(1)}, u32[]{:S(2)}, u32[]{:S(2)}) collective-permute-start(bf16[128,512]{1,0:T(8,128)(2,1)} %get-tuple-element.99), channel_id=1, source_target_pairs={{0,4},{4,0},{8,12},{12,8},{16,20},{20,16},{24,28},{28,24},{32,36},... | collective-permute-start | bytes 393224 | tf_op jit(solution)/shard_map/ppermute | solution.py:299
  143.6 22.6 %collective-permute-start.22 = (bf16[128,512]{1,0:T(8,128)(2,1)}, bf16[128,512]{1,0:T(8,128)(2,1)S(1)}, u32[]{:S(2)}, u32[]{:S(2)}) collective-permute-start(bf16[128,512]{1,0:T(8,128)(2,1)} %get-tuple-element.100), channel_id=1, source_target_pairs={{0,68},{4,64},{8,76},{12,72},{16,84},{20,80},{24,92},{28,88},{32,1... | collective-permute-start | bytes 393224 | tf_op jit(solution)/shard_map/ppermute | solution.py:299
  145.7 20.6 %collective-permute-start.23 = (bf16[128,512]{1,0:T(8,128)(2,1)}, bf16[128,512]{1,0:T(8,128)(2,1)S(1)}, u32[]{:S(2)}, u32[]{:S(2)}) collective-permute-start(bf16[128,512]{1,0:T(8,128)(2,1)} %get-tuple-element.101), channel_id=1, source_target_pairs={{0,196},{4,192},{8,204},{12,200},{16,212},{20,208},{24,220},{28,21... | collective-permute-start | bytes 393224 | tf_op jit(solution)/shard_map/ppermute | solution.py:299
  149.4 16.9 %collective-permute-start.24 = (bf16[128,512]{1,0:T(8,128)(2,1)}, bf16[128,512]{1,0:T(8,128)(2,1)S(1)}, u32[]{:S(2)}, u32[]{:S(2)}) collective-permute-start(bf16[128,512]{1,0:T(8,128)(2,1)} %get-tuple-element.102), channel_id=1, source_target_pairs={{0,132},{4,128},{8,140},{12,136},{16,148},{20,144},{24,156},{28,15... | collective-permute-start | bytes 393224 | tf_op jit(solution)/shard_map/ppermute | solution.py:299
  (20 other events, 143.5 us)

commit v5 on v4

--- a/solution.py
+++ b/solution.py
@@ -16,7 +16,7 @@
 SHARE = SLOTS * PANEL
 WIDTH = 256
 MAIN = SHARE + PANEL
-FORCED = (1, 7, 2, 6, 3, 5, 4)
+FORCED = (1, 7, 2, 6, 3, 5)
 PLANE_X = N_X * N_C
 SHIFTS = [(0, 0), (1, 0), (3, 0), (2, 0), (0, 1), (1, 1), (3, 1), (2, 1)]
 VMEM_LIMIT = 56 * 1024 * 1024
@@ -85,6 +85,7 @@
         ),
         out_shape=[shape(N_Z * LOCAL, PANEL)] * len(SHIFTS),
         compiler_params=params(),
+        cost_estimate=pl.CostEstimate(flops=1 << 37, bytes_accessed=1 << 30, transcendentals=0),
         name="repack",
     )(where, *pieces)
 
@@ -131,13 +132,17 @@
     return jnp.where(inside, column_returns.astype(jnp.float32), 0.0).astype(jnp.bfloat16)
 
 
+def scales(spans, band_columns):
+    common = jnp.minimum(band_columns[:, 1:2], spans[1:2, :]) - jnp.maximum(band_columns[:, 0:1], spans[0:1, :]) + 1
+    correlation = jnp.maximum(common, 0).astype(jnp.float32)
+    return jnp.maximum(correlation, 1.0), 1.0 / jnp.maximum(correlation - 1.0, 1.0)
+
+
 def factors(inside, spans, band_masked, band_columns):
     mask = jnp.where(inside, 1.0, 0.0).astype(jnp.bfloat16)
     band_sum = jnp.dot(band_masked, mask, preferred_element_type=jnp.float32)
-    common = jnp.minimum(band_columns[:, 1:2], spans[1:2, :]) - jnp.maximum(band_columns[:, 0:1], spans[0:1, :]) + 1
-    correlation = jnp.maximum(common, 0).astype(jnp.float32)
-    scale = 1.0 / jnp.maximum(correlation - 1.0, 1.0)
-    return scale, band_sum * scale / jnp.maximum(correlation, 1.0)
+    at_least, scale = scales(spans, band_columns)
+    return scale, band_sum * scale / at_least
 
 
 def covariance(spans, band_columns, band_masked, band_mask, column_returns):
@@ -149,13 +154,12 @@
     return (gram * scale - column_sum * mean).astype(jnp.bfloat16)
 
 
-def natural_rows(fetched, spans, band_masked, band_mask, band_columns, where):
+def natural_means(spans, band_masked, band_columns, where):
     steps = SHARE // WIDTH
 
-    def body(where_ref, spans_ref, band_ref, masked_ref, mask_ref, in_ref, rows_ref):
-        rows_ref[...] = covariance(
-            spans_ref[...], band_ref[...], masked_ref[...], mask_ref[...], in_ref[...]
-        )
+    def body(where_ref, spans_ref, band_ref, masked_ref, mean_ref):
+        spans = spans_ref[...]
+        _, mean_ref[...] = factors(listed(spans), spans, masked_ref[...], band_ref[...])
 
     return pl.pallas_call(
         body,
@@ -166,7 +170,36 @@
                 pl.BlockSpec((2, WIDTH), lambda i, where: (0, where[4] * steps + i)),
                 whole(BAND, 2),
                 whole(BAND, DAYS),
-                whole(BAND, DAYS),
+            ],
+            out_specs=pl.BlockSpec((BAND, WIDTH), lambda i, where: (0, i)),
+        ),
+        out_shape=shape(BAND, SHARE, dtype=jnp.float32),
+        compiler_params=params(),
+        name="natural_means",
+    )(where, spans, band_columns, band_masked)
+
+
+def natural_rows(fetched, spans, band_masked, band_mask, band_columns, mean, where):
+    steps = SHARE // WIDTH
+
+    def body(where_ref, spans_ref, band_ref, masked_ref, mask_ref, mean_ref, in_ref, rows_ref):
+        spans = spans_ref[...]
+        masked = masked_returns(listed(spans), in_ref[...])
+        gram = jnp.dot(masked_ref[...], masked, preferred_element_type=jnp.float32)
+        column_sum = jnp.dot(mask_ref[...], masked, preferred_element_type=jnp.float32)
+        rows_ref[...] = (gram * scales(spans, band_ref[...])[1] - column_sum * mean_ref[...]).astype(jnp.bfloat16)
+
+    return pl.pallas_call(
+        body,
+        grid_spec=pltpu.PrefetchScalarGridSpec(
+            num_scalar_prefetch=1,
+            grid=(steps,),
+            in_specs=[
+                pl.BlockSpec((2, WIDTH), lambda i, where: (0, where[4] * steps + i)),
+                whole(BAND, 2),
+                whole(BAND, DAYS),
+                whole(BAND, DAYS),
+                pl.BlockSpec((BAND, WIDTH), lambda i, where: (0, i)),
                 pl.BlockSpec((DAYS, WIDTH), lambda i, where: (0, i)),
             ],
             out_specs=pl.BlockSpec((BAND, WIDTH), lambda i, where: (0, i)),
@@ -175,7 +208,7 @@
         compiler_params=params(),
         cost_estimate=pl.CostEstimate(flops=6 * BAND * DAYS * SHARE, bytes_accessed=12 << 20, transcendentals=0),
         name="natural_rows",
-    )(where, spans, band_columns, band_masked, band_mask, fetched)
+    )(where, spans, band_columns, band_masked, band_mask, mean, fetched)
 
 
 def flip(rows):
@@ -320,7 +353,8 @@
     *band, sends = lax.optimization_barrier((*band, sends))
     pieces = [sends[0]] + [shift(sends[k], 0, k, 0) for k in range(1, N_Z)]
 
-    rows = natural_rows(fetched, security_spans, *band, band_columns, where)
+    mean = natural_means(security_spans, band[0], band_columns, where)
+    rows = natural_rows(fetched, security_spans, *band, band_columns, mean, where)
     rows, fetched, *forced = lax.optimization_barrier((rows, fetched, *(pieces[k] for k in FORCED)))
     for k, piece in zip(FORCED, forced):
         pieces[k] = piece

time: 187 us -> 186 us (level)
  waiting for transfers between devices: 63.8 us -> 53.7 us
  Pallas kernels: 47.9 us -> 55.5 us
    ppermute x21, waiting for transfers between devices: 42.7 us -> 33 us  [shift(): return lax.ppermute(array, 'tiles', [(i, to(i)) for i in range(PLANE)])]
    pallas_call x0 -> x1, Pallas kernels: none -> 7.61 us  [natural_means(): pl.pallas_call(body, grid_spec=pltpu.PrefetchScalarGridSpec(num_scalar_pr...]
    all_to_all x2, starting transfers between devices: 18.2 us -> 20.6 us  [exchange(): lax.all_to_all(pieces, 'tiles', split_axis=0, concat_axis=0, tiled=True)]
    ppermute x21, starting transfers between devices: 43.8 us -> 41.5 us  [shift(): return lax.ppermute(array, 'tiles', [(i, to(i)) for i in range(PLANE)])]
    unnamed x51 -> x53, local copies, waits for them, and re-layouts: 3.48 us -> 4.19 us
  transfers between devices with their start and end apart: 27 -> 27, of which waited for: 14 -> 12; matrix products, arithmetic and copies ran while one was open for 1% -> 1% of each run, Pallas kernels for 25% -> 29%
where the time goes in v5:
time: 186 us; the launch traced here: 185 us
  starting transfers between devices  69.1 us (37%)
  Pallas kernels  55.5 us (30%)
  waiting for transfers between devices  53.7 us (29%)
  local copies, waits for them, and re-layouts  5.47 us (3%)
    ppermute x21, starting transfers between devices, shift(): return lax.ppermute(array, 'tiles', [(i, to(i)) for i in range(PLANE)])  41.5 us
    ppermute x21, waiting for transfers between devices, shift(): return lax.ppermute(array, 'tiles', [(i, to(i)) for i in range(PLANE)])  33 us
    all_to_all x2, starting transfers between devices, exchange(): lax.all_to_all(pieces, 'tiles', split_axis=0, concat_axis=0, tiled=True)  20.6 us
    pallas_call x1, Pallas kernels, natural_rows(): pl.pallas_call(body, grid_spec=pltpu.PrefetchScalarGridSpec(num_scalar_pr...  10.7 us
    all_to_all x2, waiting for transfers between devices, exchange(): lax.all_to_all(pieces, 'tiles', split_axis=0, concat_axis=0, tiled=True)  10.1 us
    ppermute x3, waiting for transfers between devices, shift_rows(): lax.ppermute(array, 'rows', [(y, (y + step) % N_Y) for y in range(N_Y)])  9.31 us
    pallas_call x1, Pallas kernels, assigned_second(): pl.pallas_call(body, grid_spec=pltpu.PrefetchScalarGridSpec(num_scalar_pr...  8.28 us
    pallas_call x1, Pallas kernels, assigned_first(): pl.pallas_call(body, grid_spec=pltpu.PrefetchScalarGridSpec(num_scalar_pr...  8.02 us
  transfers between devices with their start and end apart: 27, of which 12 were waited for; matrix products, arithmetic and copies ran while one was open for 1% of the time, Pallas kernels for 29%

profile of v5, /device:TPU:1, one launch (start us, length us, event | category | flops | bytes accessed | tf_op | source)
XLA Modules:
  0.0 185.0 jit_solution(13494512373351735024)
XLA Ops:
  0.6 7.8 %collective-permute-start = (bf16[16,256]{1,0:T(8,128)(2,1)}, bf16[16,256]{1,0:T(8,128)(2,1)S(1)}, u32[]{:S(2)}, u32[]{:S(2)}) collective-permute-start(bf16[16,256]{1,0:T(8,128)(2,1)} %param.7), channel_id=1, source_target_pairs={{0,32},{4,36},{8,40},{12,44},{16,48},{20,52},{24,56},{28,60},{32,0... | collective-permute-start | bytes 24584 | tf_op jit(solution)/shard_map/ppermute | solution.py:332
  9.1 4.6 %pack.1 = (bf16[64,16,1536]{2,1,0:T(8,128)(2,1)}, bf16[16,4096]{1,0:T(8,128)(2,1)}, bf16[16,4096]{1,0:T(8,128)(2,1)}, bf16[16,4096]{1,0:T(8,128)(2,1)}, bf16[16,...) custom-call(s32[128]{0:T(128)} %bitcast.33, ...), custom_call_target="tpu_custom_call" | custom-call | tf_op jit(solution)/shard_map/pack/pallas_call | solution.py:54
  13.8 1.7 collective-permute-start.3
  16.6 3.1 %collective-permute-done.3 = bf16[32,256]{1,0:T(8,128)(2,1)S(1)} collective-permute-done((bf16[32,256]{1,0:T(8,128)(2,1)S(1)}, bf16[32,256]{1,0:T(8,128)(2,1)S(1)}, u32[]{:S(2)}, u32[]{:S(2)}) %collective-permute-start.3) | collective-permute-done | bytes 16416 | tf_op jit(solution)/shard_map/ppermute | solution.py:332
  20.4 10.8 %all-to-all-start = ((bf16[64,16,1536]{2,1,0:T(8,128)(2,1)}), bf16[64,16,1536]{2,1,0:T(8,128)(2,1)}, u32[]{:S(2)}, u32[]{:S(2)}) async-start(bf16[64,16,1536]{2,1,0:T(8,128)(2,1)} %get-tuple-element.76), calls=%async_computation | async-start | bytes 6291456 | tf_op jit(solution)/shard_map/all_to_all | solution.py:316
  31.2 2.9 %collective-permute-start.6 = (bf16[128,256]{1,0:T(8,128)(2,1)S(1)}, bf16[128,256]{1,0:T(8,128)(2,1)S(1)}, u32[]{:S(2)}, u32[]{:S(2)}) collective-permute-start(bf16[128,256]{1,0:T(8,128)(2,1)S(1)} %pad_maximum_fusion.2), channel_id=1, source_target_pairs={{0,192},{4,196},{8,200},{12,204},{16,208},{20,212},{24,216},{28,22... | collective-permute-start | bytes 196616 | tf_op jit(solution)/shard_map/ppermute | solution.py:332
  35.1 6.4 %collective-permute-done.6 = bf16[128,256]{1,0:T(8,128)(2,1)S(1)} collective-permute-done((bf16[128,256]{1,0:T(8,128)(2,1)S(1)}, bf16[128,256]{1,0:T(8,128)(2,1)S(1)}, u32[]{:S(2)}, u32[]{:S(2)}) %collective-permute-start.6) | collective-permute-done | bytes 65568 | tf_op jit(solution)/shard_map/ppermute | solution.py:332
  41.6 1.5 collective-permute-done.5
  44.5 3.0 %collective-permute-start.8 = (bf16[4,128,256]{2,1,0:T(8,128)(2,1)S(1)}, bf16[4,128,256]{2,1,0:T(8,128)(2,1)S(1)}, u32[]{:S(2)}, u32[]{:S(2)}) collective-permute-start(bf16[4,128,256]{2,1,0:T(8,128)(2,1)S(1)} %get-tuple-element.102), channel_id=1, source_target_pairs={{0,2},{1,3},{2,0},{3,1},{4,6},{5,7},{6,4},{7,5},{8,10},{9,11},{10,... | collective-permute-start | bytes 786440 | tf_op jit(solution)/shard_map/ppermute | solution.py:320
  47.9 2.3 %collective-permute-start.9 = (bf16[4,128,256]{2,1,0:T(8,128)(2,1)S(1)}, bf16[4,128,256]{2,1,0:T(8,128)(2,1)S(1)}, u32[]{:S(2)}, u32[]{:S(2)}) collective-permute-start(bf16[4,128,256]{2,1,0:T(8,128)(2,1)S(1)} %get-tuple-element.102), channel_id=1, source_target_pairs={{0,3},{1,0},{2,1},{3,2},{4,7},{5,4},{6,5},{7,6},{8,11},{9,8},{10,9... | collective-permute-start | bytes 786440 | tf_op jit(solution)/shard_map/ppermute | solution.py:320
  50.2 2.4 %collective-permute-done.8 = bf16[4,128,256]{2,1,0:T(8,128)(2,1)S(1)} collective-permute-done((bf16[4,128,256]{2,1,0:T(8,128)(2,1)S(1)}, bf16[4,128,256]{2,1,0:T(8,128)(2,1)S(1)}, u32[]{:S(2)}, u32[]{:S(2)}) %collective-permute-start.8) | collective-permute-done | bytes 262176 | tf_op jit(solution)/shard_map/ppermute | solution.py:320
  52.5 6.9 %collective-permute-done.7 = bf16[4,128,256]{2,1,0:T(8,128)(2,1)S(1)} collective-permute-done((bf16[4,128,256]{2,1,0:T(8,128)(2,1)S(1)}, bf16[4,128,256]{2,1,0:T(8,128)(2,1)S(1)}, u32[]{:S(2)}, u32[]{:S(2)}) %collective-permute-start.7) | collective-permute-done | bytes 262176 | tf_op jit(solution)/shard_map/ppermute | solution.py:320
  64.3 6.5 %prepare_band.1 = (bf16[1024,1024]{1,0:T(8,128)(2,1)}, bf16[1024,1024]{1,0:T(8,128)(2,1)}) custom-call(s32[5]{0:T(128)} %stack.53.where_ref, s32[1024,2]{1,0:T(8,128)} %bitcast.21, bf16[4,4,128,256]{3,2,1,0:T(8,128)(2,1)} %copy-done, bf16[4,4,128,256]{3,2,1,0:T(8,128)(2,1)} %copy-done.1), custom_call_target="tpu_custom_call" | custom-call | tf_op jit(solution)/shard_map/prepare_band/pallas_call | solution.py:111
  70.8 2.9 %collective-permute-start.11 = (bf16[16,4096]{1,0:T(8,128)(2,1)S(1)}, bf16[16,4096]{1,0:T(8,128)(2,1)S(1)}, u32[]{:S(2)}, u32[]{:S(2)}) collective-permute-start(bf16[16,4096]{1,0:T(8,128)(2,1)S(1)} %copy-done.11), channel_id=1, source_target_pairs={{0,8},{4,12},{8,16},{12,20},{16,24},{20,28},{24,32},{28,36},{32,40... | collective-permute-start | bytes 393224 | tf_op jit(solution)/shard_map/ppermute | solution.py:332
  73.7 3.3 %collective-permute-start.12 = (bf16[16,4096]{1,0:T(8,128)(2,1)S(1)}, bf16[16,4096]{1,0:T(8,128)(2,1)S(1)}, u32[]{:S(2)}, u32[]{:S(2)}) collective-permute-start(bf16[16,4096]{1,0:T(8,128)(2,1)S(1)} %copy-done.10), channel_id=1, source_target_pairs={{0,56},{4,60},{8,0},{12,4},{16,8},{20,12},{24,16},{28,20},{32,24},... | collective-permute-start | bytes 393224 | tf_op jit(solution)/shard_map/ppermute | solution.py:332
  78.2 2.4 %collective-permute-start.14 = (bf16[16,4096]{1,0:T(8,128)(2,1)S(1)}, bf16[16,4096]{1,0:T(8,128)(2,1)S(1)}, u32[]{:S(2)}, u32[]{:S(2)}) collective-permute-start(bf16[16,4096]{1,0:T(8,128)(2,1)S(1)} %copy-done.8), channel_id=1, source_target_pairs={{0,48},{4,52},{8,56},{12,60},{16,0},{20,4},{24,8},{28,12},{32,16},... | collective-permute-start | bytes 393224 | tf_op jit(solution)/shard_map/ppermute | solution.py:332
  81.3 7.6 %natural_means.1.mean_ref = f32[1024,1024]{1,0:T(8,128)} custom-call(s32[5]{0:T(128)} %stack.53.where_ref, s32[2,65536]{1,0:T(2,128)} %spans_ref.7, s32[1024,2]{1,0:T(8,128)} %bitcast.22, bf16[1024,1024]{1,0:T(8,128)(2,1)} %get-tuple-element.74.masked_ref), custom_call_target="tpu_custom_call" | custom-call | tf_op jit(solution)/shard_map/natural_means/pallas_call | solution.py:164
  88.9 15.3 %collective-permute-done.11.refs_1_ = bf16[16,4096]{1,0:T(8,128)(2,1)S(1)} collective-permute-done((bf16[16,4096]{1,0:T(8,128)(2,1)S(1)}, bf16[16,4096]{1,0:T(8,128)(2,1)S(1)}, u32[]{:S(2)}, u32[]{:S(2)}) %collective-permute-start.11) | collective-permute-done | bytes 131104 | tf_op jit(solution)/shard_map/ppermute | solution.py:332
  104.1 3.5 %collective-permute-start.16 = (bf16[16,4096]{1,0:T(8,128)(2,1)S(1)}, bf16[16,4096]{1,0:T(8,128)(2,1)S(1)}, u32[]{:S(2)}, u32[]{:S(2)}) collective-permute-start(bf16[16,4096]{1,0:T(8,128)(2,1)S(1)} %copy-done.6), channel_id=1, source_target_pairs={{0,40},{4,44},{8,48},{12,52},{16,56},{20,60},{24,0},{28,4},{32,8},... | collective-permute-start | bytes 393224 | tf_op jit(solution)/shard_map/ppermute | solution.py:332
  107.8 10.7 %natural_rows.1.in_ref = bf16[1024,1024]{1,0:T(8,128)(2,1)} custom-call(s32[5]{0:T(128)} %stack.53.where_ref, s32[2,65536]{1,0:T(2,128)} %spans_ref.7, s32[1024,2]{1,0:T(8,128)} %bitcast.23, bf16[1024,1024]{1,0:T(8,128)(2,1)} %get-tuple-element.74.masked_ref, bf16[1024,1024]{1,0:T(8,128)(2,1)} %get-tuple-element.75.mask_ref, ...), custom_call_target="tpu_custom_call" | custom-call | flops 6442450944 | bytes 12582912 | tf_op jit(solution)/shard_map/natural_rows/pallas_call | solution.py:192
  118.6 2.1 %collective-permute-done.15.refs_3_ = bf16[16,4096]{1,0:T(8,128)(2,1)S(1)} collective-permute-done((bf16[16,4096]{1,0:T(8,128)(2,1)S(1)}, bf16[16,4096]{1,0:T(8,128)(2,1)S(1)}, u32[]{:S(2)}, u32[]{:S(2)}) %collective-permute-start.15) | collective-permute-done | bytes 131104 | tf_op jit(solution)/shard_map/ppermute | solution.py:332
  121.4 9.8 %all-to-all-start.1 = ((bf16[64,16,1024]{2,1,0:T(8,128)(2,1)}), bf16[64,16,1024]{2,1,0:T(8,128)(2,1)}, u32[]{:S(2)}, u32[]{:S(2)}) async-start(bf16[64,16,1024]{2,1,0:T(8,128)(2,1)} %bitcast.20), calls=%async_computation.1 | async-start | bytes 4194304 | tf_op jit(solution)/shard_map/all_to_all | solution.py:316
  131.9 3.0 %repack.1 = (bf16[128,512]{1,0:T(8,128)(2,1)}, bf16[128,512]{1,0:T(8,128)(2,1)}, bf16[128,512]{1,0:T(8,128)(2,1)}, bf16[128,512]{1,0:T(8,128)(2,1)}, bf16[128,51...) custom-call(s32[5]{0:T(128)} %stack.53.where_ref, ...), custom_call_target="tpu_custom_call" | custom-call | flops 137438953472 | bytes 1073741824 | tf_op jit(solution)/shard_map/repack/pallas_call | solution.py:78
  138.4 1.6 collective-permute-start.20
  141.4 2.5 %collective-permute-done.18.refs_1_ = bf16[128,512]{1,0:T(8,128)(2,1)S(1)} collective-permute-done((bf16[128,512]{1,0:T(8,128)(2,1)}, bf16[128,512]{1,0:T(8,128)(2,1)S(1)}, u32[]{:S(2)}, u32[]{:S(2)}) %collective-permute-start.18) | collective-permute-done | bytes 131104 | tf_op jit(solution)/shard_map/ppermute | solution.py:332
  144.0 2.4 %collective-permute-start.23 = (bf16[128,512]{1,0:T(8,128)(2,1)}, bf16[128,512]{1,0:T(8,128)(2,1)S(1)}, u32[]{:S(2)}, u32[]{:S(2)}) collective-permute-start(bf16[128,512]{1,0:T(8,128)(2,1)} %get-tuple-element.99), channel_id=1, source_target_pairs={{0,196},{4,192},{8,204},{12,200},{16,212},{20,208},{24,220},{28,21... | collective-permute-start | bytes 393224 | tf_op jit(solution)/shard_map/ppermute | solution.py:332
  146.3 4.6 %collective-permute-start.24 = (bf16[128,512]{1,0:T(8,128)(2,1)}, bf16[128,512]{1,0:T(8,128)(2,1)S(1)}, u32[]{:S(2)}, u32[]{:S(2)}) collective-permute-start(bf16[128,512]{1,0:T(8,128)(2,1)} %get-tuple-element.100), channel_id=1, source_target_pairs={{0,132},{4,128},{8,140},{12,136},{16,148},{20,144},{24,156},{28,15... | collective-permute-start | bytes 393224 | tf_op jit(solution)/shard_map/ppermute | solution.py:332
  150.9 8.0 %assigned_first.1.tiles_ref = bf16[1,2,1024,512]{3,2,1,0:T(8,128)(2,1)} custom-call(s32[2]{0:T(128)} %dynamic-slice_bitcast_fusion.owned_ref, s32[2,65536]{1,0:T(2,128)} %spans_ref.7, s32[1024,2]{1,0:T(8,128)} %bitcast.24, bf16[1024,1024]{1,0:T(8,128)(2,1)} %get-tuple-element.74.masked_ref, bf16[1024,1024]{1,0:T(8,128)(2,1)} %get-tuple-element.75.mask_ref, ...), custom_call_target="tpu_custom_call" | custom-call | flops 3221225472 | bytes 6291456 | tf_op jit(solution)/shard_map/assigned_first/pallas_call | solution.py:237
  159.0 4.1 %flip.1 = bf16[1,1024,1024]{2,1,0:T(8,128)(2,1)} custom-call(bf16[1024,1024]{1,0:T(8,128)(2,1)} %natural_rows.1.in_ref), custom_call_target="tpu_custom_call" | custom-call | tf_op jit(solution)/shard_map/flip/pallas_call | solution.py:218
  164.0 8.3 %assigned_second.1 = bf16[1,2,1024,512]{3,2,1,0:T(8,128)(2,1)} custom-call(s32[2]{0:T(128)} %dynamic-slice_bitcast_fusion.owned_ref, s32[5]{0:T(128)} %stack.53.where_ref, bf16[1,2,1024,512]{3,2,1,0:T(8,128)(2,1)} %assigned_first.1.tiles_ref, s32[2,65536]{1,0:T(2,128)} %spans_ref.7, s32[1024,2]{1,0:T(8,128)} %bitcast.25, ...), custom_call_target="tpu_custom_call", output_to_operand_aliasing={{}: (2, {})} | custom-call | flops 3221225472 | bytes 6291456 | tf_op jit(solution)/shard_map/assigned_second/pallas_call | solution.py:273
  172.2 10.1 %all-to-all-done.1.in_ref = bf16[64,16,1024]{2,1,0:T(8,128)(2,1)} async-done(((bf16[64,16,1024]{2,1,0:T(8,128)(2,1)}), bf16[64,16,1024]{2,1,0:T(8,128)(2,1)}, u32[]{:S(2)}, u32[]{:S(2)}) %all-to-all-start.1) | async-done | bytes 2097184 | tf_op jit(solution)/shard_map/all_to_all | solution.py:316
  182.4 2.6 %unpack_rows.1 = bf16[16,65536]{1,0:T(8,128)(2,1)} custom-call(bf16[64,16,1024]{2,1,0:T(8,128)(2,1)} %all-to-all-done.1.in_ref), custom_call_target="tpu_custom_call" | custom-call | tf_op jit(solution)/shard_map/unpack_rows/pallas_call | solution.py:304
  (90 shorter events, 19.3 us)
Async XLA Ops:
  0.6 13.1 %collective-permute-start = (bf16[16,256]{1,0:T(8,128)(2,1)}, bf16[16,256]{1,0:T(8,128)(2,1)S(1)}, u32[]{:S(2)}, u32[]{:S(2)}) collective-permute-start(bf16[16,256]{1,0:T(8,128)(2,1)} %param.7), channel_id=1, source_target_pairs={{0,32},{4,36},{8,40},{12,44},{16,48},{20,52},{24,56},{28,60},{32,0... | collective-permute-start | bytes 24584 | tf_op jit(solution)/shard_map/ppermute | solution.py:332
  13.8 5.9 %collective-permute-start.3 = (bf16[32,256]{1,0:T(8,128)(2,1)S(1)}, bf16[32,256]{1,0:T(8,128)(2,1)S(1)}, u32[]{:S(2)}, u32[]{:S(2)}) collective-permute-start(bf16[32,256]{1,0:T(8,128)(2,1)S(1)} %pad_maximum_fusion.3), channel_id=1, source_target_pairs={{0,24},{4,28},{8,32},{12,36},{16,40},{20,44},{24,48},{28,52},{32,5... | collective-permute-start | bytes 49160 | tf_op jit(solution)/shard_map/ppermute | solution.py:332
  15.5 4.9 %collective-permute-start.2 = (bf16[32,256]{1,0:T(8,128)(2,1)S(1)}, bf16[32,256]{1,0:T(8,128)(2,1)S(1)}, u32[]{:S(2)}, u32[]{:S(2)}) collective-permute-start(bf16[32,256]{1,0:T(8,128)(2,1)S(1)} %pad_maximum_fusion.3), channel_id=1, source_target_pairs={{0,16},{4,20},{8,24},{12,28},{16,32},{20,36},{24,40},{28,44},{32,4... | collective-permute-start | bytes 49160 | tf_op jit(solution)/shard_map/ppermute | solution.py:332
  15.8 4.5 %collective-permute-start.1 = (bf16[32,256]{1,0:T(8,128)(2,1)S(1)}, bf16[32,256]{1,0:T(8,128)(2,1)S(1)}, u32[]{:S(2)}, u32[]{:S(2)}) collective-permute-start(bf16[32,256]{1,0:T(8,128)(2,1)S(1)} %pad_maximum_fusion.3), channel_id=1, source_target_pairs={{0,8},{4,12},{8,16},{12,20},{16,24},{20,28},{24,32},{28,36},{32,40... | collective-permute-start | bytes 49160 | tf_op jit(solution)/shard_map/ppermute | solution.py:332
  20.4 87.4 %all-to-all-start = ((bf16[64,16,1536]{2,1,0:T(8,128)(2,1)}), bf16[64,16,1536]{2,1,0:T(8,128)(2,1)}, u32[]{:S(2)}, u32[]{:S(2)}) async-start(bf16[64,16,1536]{2,1,0:T(8,128)(2,1)} %get-tuple-element.76), calls=%async_computation | async-start | bytes 6291456 | tf_op jit(solution)/shard_map/all_to_all | solution.py:316
  31.2 29.8 %copy-start.2 = (s32[2,1024]{1,0:T(2,128)S(1)}, s32[2,1024]{1,0:T(2,128)}, u32[]{:S(2)}) copy-start(s32[2,1024]{1,0:T(2,128)} %param.8) | copy-start | bytes 24580
  31.2 10.3 %collective-permute-start.6 = (bf16[128,256]{1,0:T(8,128)(2,1)S(1)}, bf16[128,256]{1,0:T(8,128)(2,1)S(1)}, u32[]{:S(2)}, u32[]{:S(2)}) collective-permute-start(bf16[128,256]{1,0:T(8,128)(2,1)S(1)} %pad_maximum_fusion.2), channel_id=1, source_target_pairs={{0,192},{4,196},{8,200},{12,204},{16,208},{20,212},{24,216},{28,22... | collective-permute-start | bytes 196616 | tf_op jit(solution)/shard_map/ppermute | solution.py:332
  34.1 9.0 %collective-permute-start.5 = (bf16[128,256]{1,0:T(8,128)(2,1)S(1)}, bf16[128,256]{1,0:T(8,128)(2,1)S(1)}, u32[]{:S(2)}, u32[]{:S(2)}) collective-permute-start(bf16[128,256]{1,0:T(8,128)(2,1)S(1)} %pad_maximum_fusion.2), channel_id=1, source_target_pairs={{0,128},{4,132},{8,136},{12,140},{16,144},{20,148},{24,152},{28,15... | collective-permute-start | bytes 196616 | tf_op jit(solution)/shard_map/ppermute | solution.py:332
  34.5 10.0 %collective-permute-start.4 = (bf16[128,256]{1,0:T(8,128)(2,1)S(1)}, bf16[128,256]{1,0:T(8,128)(2,1)S(1)}, u32[]{:S(2)}, u32[]{:S(2)}) collective-permute-start(bf16[128,256]{1,0:T(8,128)(2,1)S(1)} %pad_maximum_fusion.2), channel_id=1, source_target_pairs={{0,64},{4,68},{8,72},{12,76},{16,80},{20,84},{24,88},{28,92},{32,9... | collective-permute-start | bytes 196616 | tf_op jit(solution)/shard_map/ppermute | solution.py:332
  44.5 8.0 %collective-permute-start.8 = (bf16[4,128,256]{2,1,0:T(8,128)(2,1)S(1)}, bf16[4,128,256]{2,1,0:T(8,128)(2,1)S(1)}, u32[]{:S(2)}, u32[]{:S(2)}) collective-permute-start(bf16[4,128,256]{2,1,0:T(8,128)(2,1)S(1)} %get-tuple-element.102), channel_id=1, source_target_pairs={{0,2},{1,3},{2,0},{3,1},{4,6},{5,7},{6,4},{7,5},{8,10},{9,11},{10,... | collective-permute-start | bytes 786440 | tf_op jit(solution)/shard_map/ppermute | solution.py:320
  47.5 12.0 %collective-permute-start.7 = (bf16[4,128,256]{2,1,0:T(8,128)(2,1)S(1)}, bf16[4,128,256]{2,1,0:T(8,128)(2,1)S(1)}, u32[]{:S(2)}, u32[]{:S(2)}) collective-permute-start(bf16[4,128,256]{2,1,0:T(8,128)(2,1)S(1)} %get-tuple-element.102), channel_id=1, source_target_pairs={{0,1},{1,2},{2,3},{3,0},{4,5},{5,6},{6,7},{7,4},{8,9},{9,10},{10,1... | collective-permute-start | bytes 786440 | tf_op jit(solution)/shard_map/ppermute | solution.py:320
  47.9 11.6 %collective-permute-start.9 = (bf16[4,128,256]{2,1,0:T(8,128)(2,1)S(1)}, bf16[4,128,256]{2,1,0:T(8,128)(2,1)S(1)}, u32[]{:S(2)}, u32[]{:S(2)}) collective-permute-start(bf16[4,128,256]{2,1,0:T(8,128)(2,1)S(1)} %get-tuple-element.102), channel_id=1, source_target_pairs={{0,3},{1,0},{2,1},{3,2},{4,7},{5,4},{6,5},{7,6},{8,11},{9,8},{10,9... | collective-permute-start | bytes 786440 | tf_op jit(solution)/shard_map/ppermute | solution.py:320
  59.6 18.6 %copy-start.8 = (bf16[16,4096]{1,0:T(8,128)(2,1)S(1)}, bf16[16,4096]{1,0:T(8,128)(2,1)}, u32[]{:S(2)}) copy-start(bf16[16,4096]{1,0:T(8,128)(2,1)} %get-tuple-element.80) | copy-start | bytes 393220
  59.7 21.0 %copy-start.7 = (bf16[16,4096]{1,0:T(8,128)(2,1)S(1)}, bf16[16,4096]{1,0:T(8,128)(2,1)}, u32[]{:S(2)}) copy-start(bf16[16,4096]{1,0:T(8,128)(2,1)} %get-tuple-element.81) | copy-start | bytes 393220
  59.7 3.7 %collective-permute-start.10 = (bf16[4,4,128,256]{3,2,1,0:T(8,128)(2,1)S(1)}, bf16[4,4,128,256]{3,2,1,0:T(8,128)(2,1)S(1)}, u32[]{:S(2)}, u32[]{:S(2)}) collective-permute-start(bf16[4,4,128,256]{3,2,1,0:T(8,128)(2,1)S(1)} %pad_maximum_fusion.own_ref), channel_id=1, source_target_pairs={{0,4},{4,0},{8,12},{12,8},{16,20},{20,16},{24,28},{28,24},{32,36},... | collective-permute-start | bytes 3145736 | tf_op jit(solution)/shard_map/ppermute | solution.py:324
  70.8 33.3 %copy-start.6 = (bf16[16,4096]{1,0:T(8,128)(2,1)S(1)}, bf16[16,4096]{1,0:T(8,128)(2,1)}, u32[]{:S(2)}) copy-start(bf16[16,4096]{1,0:T(8,128)(2,1)} %get-tuple-element.82) | copy-start | bytes 393220
  70.8 36.8 %copy-start.5 = (bf16[16,4096]{1,0:T(8,128)(2,1)S(1)}, bf16[16,4096]{1,0:T(8,128)(2,1)}, u32[]{:S(2)}) copy-start(bf16[16,4096]{1,0:T(8,128)(2,1)} %get-tuple-element.89) | copy-start | bytes 393220
  70.8 33.3 %collective-permute-start.11 = (bf16[16,4096]{1,0:T(8,128)(2,1)S(1)}, bf16[16,4096]{1,0:T(8,128)(2,1)S(1)}, u32[]{:S(2)}, u32[]{:S(2)}) collective-permute-start(bf16[16,4096]{1,0:T(8,128)(2,1)S(1)} %copy-done.11), channel_id=1, source_target_pairs={{0,8},{4,12},{8,16},{12,20},{16,24},{20,28},{24,32},{28,36},{32,40... | collective-permute-start | bytes 393224 | tf_op jit(solution)/shard_map/ppermute | solution.py:332
  73.7 33.9 %collective-permute-start.12 = (bf16[16,4096]{1,0:T(8,128)(2,1)S(1)}, bf16[16,4096]{1,0:T(8,128)(2,1)S(1)}, u32[]{:S(2)}, u32[]{:S(2)}) collective-permute-start(bf16[16,4096]{1,0:T(8,128)(2,1)S(1)} %copy-done.10), channel_id=1, source_target_pairs={{0,56},{4,60},{8,0},{12,4},{16,8},{20,12},{24,16},{28,20},{32,24},... | collective-permute-start | bytes 393224 | tf_op jit(solution)/shard_map/ppermute | solution.py:332
  77.0 41.5 %collective-permute-start.13 = (bf16[16,4096]{1,0:T(8,128)(2,1)S(1)}, bf16[16,4096]{1,0:T(8,128)(2,1)S(1)}, u32[]{:S(2)}, u32[]{:S(2)}) collective-permute-start(bf16[16,4096]{1,0:T(8,128)(2,1)S(1)} %copy-done.9), channel_id=1, source_target_pairs={{0,16},{4,20},{8,24},{12,28},{16,32},{20,36},{24,40},{28,44},{32,4... | collective-permute-start | bytes 393224 | tf_op jit(solution)/shard_map/ppermute | solution.py:332
  78.2 40.3 %collective-permute-start.14 = (bf16[16,4096]{1,0:T(8,128)(2,1)S(1)}, bf16[16,4096]{1,0:T(8,128)(2,1)S(1)}, u32[]{:S(2)}, u32[]{:S(2)}) collective-permute-start(bf16[16,4096]{1,0:T(8,128)(2,1)S(1)} %copy-done.8), channel_id=1, source_target_pairs={{0,48},{4,52},{8,56},{12,60},{16,0},{20,4},{24,8},{28,12},{32,16},... | collective-permute-start | bytes 393224 | tf_op jit(solution)/shard_map/ppermute | solution.py:332
  80.6 40.0 %collective-permute-start.15 = (bf16[16,4096]{1,0:T(8,128)(2,1)S(1)}, bf16[16,4096]{1,0:T(8,128)(2,1)S(1)}, u32[]{:S(2)}, u32[]{:S(2)}) collective-permute-start(bf16[16,4096]{1,0:T(8,128)(2,1)S(1)} %copy-done.7), channel_id=1, source_target_pairs={{0,24},{4,28},{8,32},{12,36},{16,40},{20,44},{24,48},{28,52},{32,5... | collective-permute-start | bytes 393224 | tf_op jit(solution)/shard_map/ppermute | solution.py:332
  104.1 16.5 %collective-permute-start.16 = (bf16[16,4096]{1,0:T(8,128)(2,1)S(1)}, bf16[16,4096]{1,0:T(8,128)(2,1)S(1)}, u32[]{:S(2)}, u32[]{:S(2)}) collective-permute-start(bf16[16,4096]{1,0:T(8,128)(2,1)S(1)} %copy-done.6), channel_id=1, source_target_pairs={{0,40},{4,44},{8,48},{12,52},{16,56},{20,60},{24,0},{28,4},{32,8},... | collective-permute-start | bytes 393224 | tf_op jit(solution)/shard_map/ppermute | solution.py:332
  107.7 23.6 %collective-permute-start.17 = (bf16[16,4096]{1,0:T(8,128)(2,1)S(1)}, bf16[16,4096]{1,0:T(8,128)(2,1)S(1)}, u32[]{:S(2)}, u32[]{:S(2)}) collective-permute-start(bf16[16,4096]{1,0:T(8,128)(2,1)S(1)} %copy-done.5), channel_id=1, source_target_pairs={{0,32},{4,36},{8,40},{12,44},{16,48},{20,52},{24,56},{28,60},{32,0... | collective-permute-start | bytes 393224 | tf_op jit(solution)/shard_map/ppermute | solution.py:332
  121.4 61.0 %all-to-all-start.1 = ((bf16[64,16,1024]{2,1,0:T(8,128)(2,1)}), bf16[64,16,1024]{2,1,0:T(8,128)(2,1)}, u32[]{:S(2)}, u32[]{:S(2)}) async-start(bf16[64,16,1024]{2,1,0:T(8,128)(2,1)} %bitcast.20), calls=%async_computation.1 | async-start | bytes 4194304 | tf_op jit(solution)/shard_map/all_to_all | solution.py:316
  134.9 9.1 %collective-permute-start.18 = (bf16[128,512]{1,0:T(8,128)(2,1)}, bf16[128,512]{1,0:T(8,128)(2,1)S(1)}, u32[]{:S(2)}, u32[]{:S(2)}) collective-permute-start(bf16[128,512]{1,0:T(8,128)(2,1)} %get-tuple-element.94), channel_id=1, source_target_pairs={{0,64},{4,68},{8,72},{12,76},{16,80},{20,84},{24,88},{28,92},{32,9... | collective-permute-start | bytes 393224 | tf_op jit(solution)/shard_map/ppermute | solution.py:332
  136.3 10.0 %collective-permute-start.19 = (bf16[128,512]{1,0:T(8,128)(2,1)}, bf16[128,512]{1,0:T(8,128)(2,1)S(1)}, u32[]{:S(2)}, u32[]{:S(2)}) collective-permute-start(bf16[128,512]{1,0:T(8,128)(2,1)} %get-tuple-element.95), channel_id=1, source_target_pairs={{0,192},{4,196},{8,200},{12,204},{16,208},{20,212},{24,216},{28,22... | collective-permute-start | bytes 393224 | tf_op jit(solution)/shard_map/ppermute | solution.py:332
  138.4 24.7 %collective-permute-start.20 = (bf16[128,512]{1,0:T(8,128)(2,1)}, bf16[128,512]{1,0:T(8,128)(2,1)S(1)}, u32[]{:S(2)}, u32[]{:S(2)}) collective-permute-start(bf16[128,512]{1,0:T(8,128)(2,1)} %get-tuple-element.96), channel_id=1, source_target_pairs={{0,128},{4,132},{8,136},{12,140},{16,144},{20,148},{24,152},{28,15... | collective-permute-start | bytes 393224 | tf_op jit(solution)/shard_map/ppermute | solution.py:332
  140.0 23.1 %collective-permute-start.21 = (bf16[128,512]{1,0:T(8,128)(2,1)}, bf16[128,512]{1,0:T(8,128)(2,1)S(1)}, u32[]{:S(2)}, u32[]{:S(2)}) collective-permute-start(bf16[128,512]{1,0:T(8,128)(2,1)} %get-tuple-element.97), channel_id=1, source_target_pairs={{0,4},{4,0},{8,12},{12,8},{16,20},{20,16},{24,28},{28,24},{32,36},... | collective-permute-start | bytes 393224 | tf_op jit(solution)/shard_map/ppermute | solution.py:332
  141.2 21.9 %collective-permute-start.22 = (bf16[128,512]{1,0:T(8,128)(2,1)}, bf16[128,512]{1,0:T(8,128)(2,1)S(1)}, u32[]{:S(2)}, u32[]{:S(2)}) collective-permute-start(bf16[128,512]{1,0:T(8,128)(2,1)} %get-tuple-element.98), channel_id=1, source_target_pairs={{0,68},{4,64},{8,76},{12,72},{16,84},{20,80},{24,92},{28,88},{32,1... | collective-permute-start | bytes 393224 | tf_op jit(solution)/shard_map/ppermute | solution.py:332
  144.0 19.2 %collective-permute-start.23 = (bf16[128,512]{1,0:T(8,128)(2,1)}, bf16[128,512]{1,0:T(8,128)(2,1)S(1)}, u32[]{:S(2)}, u32[]{:S(2)}) collective-permute-start(bf16[128,512]{1,0:T(8,128)(2,1)} %get-tuple-element.99), channel_id=1, source_target_pairs={{0,196},{4,192},{8,204},{12,200},{16,212},{20,208},{24,220},{28,21... | collective-permute-start | bytes 393224 | tf_op jit(solution)/shard_map/ppermute | solution.py:332
  146.3 16.8 %collective-permute-start.24 = (bf16[128,512]{1,0:T(8,128)(2,1)}, bf16[128,512]{1,0:T(8,128)(2,1)S(1)}, u32[]{:S(2)}, u32[]{:S(2)}) collective-permute-start(bf16[128,512]{1,0:T(8,128)(2,1)} %get-tuple-element.100), channel_id=1, source_target_pairs={{0,132},{4,128},{8,140},{12,136},{16,148},{20,144},{24,156},{28,15... | collective-permute-start | bytes 393224 | tf_op jit(solution)/shard_map/ppermute | solution.py:332
  (21 other events, 129.9 us)

commit v6 on v5

--- a/solution.py
+++ b/solution.py
@@ -16,7 +16,7 @@
 SHARE = SLOTS * PANEL
 WIDTH = 256
 MAIN = SHARE + PANEL
-FORCED = (1, 7, 2, 6, 3, 5)
+FORCED = (1, 7, 2, 6)
 PLANE_X = N_X * N_C
 SHIFTS = [(0, 0), (1, 0), (3, 0), (2, 0), (0, 1), (1, 1), (3, 1), (2, 1)]
 VMEM_LIMIT = 56 * 1024 * 1024
@@ -295,18 +295,22 @@
 
 
 def unpack_rows(arrived):
-    per_step = 32
-
-    def body(in_ref, out_ref):
-        for piece in range(per_step):
-            out_ref[:, piece * SHARE : (piece + 1) * SHARE] = in_ref[piece]
-
-    return pl.pallas_call(
-        body,
-        grid=(PLANE // per_step,),
-        in_specs=[pl.BlockSpec((per_step, LOCAL, SHARE), lambda i: (i, 0, 0))],
-        out_specs=pl.BlockSpec((LOCAL, per_step * SHARE), lambda i: (0, i)),
+    def body(in_ref, out_ref, done):
+        copies = [
+            pltpu.make_async_copy(in_ref.at[piece], out_ref.at[:, pl.ds(piece * SHARE, SHARE)], done.at[piece])
+            for piece in range(PLANE)
+        ]
+        for copy in copies:
+            copy.start()
+        for copy in copies:
+            copy.wait()
+
+    return pl.pallas_call(
+        body,
+        in_specs=[pl.BlockSpec(memory_space=pl.ANY)],
+        out_specs=pl.BlockSpec(memory_space=pl.ANY),
         out_shape=shape(LOCAL, PLANE * SHARE),
+        scratch_shapes=[pltpu.SemaphoreType.DMA((PLANE,))],
         compiler_params=params(24 * 1024 * 1024),
         name="unpack_rows",
     )(arrived)

time: 186 us -> 248 us (1.33)
  Pallas kernels: 55.5 us -> 118 us
    pallas_call x1, Pallas kernels: 2.61 us -> 65.2 us  [unpack_rows(): pl.pallas_call(body, in_specs=[pl.BlockSpec(memory_space=pl.ANY)], out_sp...]
  transfers between devices with their start and end apart: 27 -> 27, of which waited for: 12 -> 11; matrix products, arithmetic and copies ran while one was open for 1% -> 1% of each run, Pallas kernels for 29% -> 21%
where the time goes in v6:
time: 248 us
  Pallas kernels  118 us (48%)
  starting transfers between devices  69.9 us (28%)
  waiting for transfers between devices  52.2 us (21%)
  local copies, waits for them, and re-layouts  6.12 us (2%)
    pallas_call x1, Pallas kernels, unpack_rows(): pl.pallas_call(body, in_specs=[pl.BlockSpec(memory_space=pl.ANY)], out_sp...  65.2 us
    ppermute x21, starting transfers between devices, shift(): return lax.ppermute(array, 'tiles', [(i, to(i)) for i in range(PLANE)])  40.2 us
    ppermute x21, waiting for transfers between devices, shift(): return lax.ppermute(array, 'tiles', [(i, to(i)) for i in range(PLANE)])  31.4 us
    all_to_all x2, starting transfers between devices, exchange(): lax.all_to_all(pieces, 'tiles', split_axis=0, concat_axis=0, tiled=True)  22.7 us
    pallas_call x1, Pallas kernels, natural_rows(): pl.pallas_call(body, grid_spec=pltpu.PrefetchScalarGridSpec(num_scalar_pr...  10.7 us
    all_to_all x2, waiting for transfers between devices, exchange(): lax.all_to_all(pieces, 'tiles', split_axis=0, concat_axis=0, tiled=True)  10.2 us
    ppermute x3, waiting for transfers between devices, shift_rows(): lax.ppermute(array, 'rows', [(y, (y + step) % N_Y) for y in range(N_Y)])  9.31 us
    pallas_call x1, Pallas kernels, assigned_second(): pl.pallas_call(body, grid_spec=pltpu.PrefetchScalarGridSpec(num_scalar_pr...  8.28 us
  transfers between devices with their start and end apart: 27, of which 11 were waited for; matrix products, arithmetic and copies ran while one was open for 1% of the time, Pallas kernels for 21%

profile of v6, /device:TPU:1, one launch (start us, length us, event | category | flops | bytes accessed | tf_op | source)
XLA Modules:
  0.0 247.7 jit_solution(4025714623710152216)
XLA Ops:
  0.6 7.8 %collective-permute-start = (bf16[16,256]{1,0:T(8,128)(2,1)}, bf16[16,256]{1,0:T(8,128)(2,1)S(1)}, u32[]{:S(2)}, u32[]{:S(2)}) collective-permute-start(bf16[16,256]{1,0:T(8,128)(2,1)} %param.7), channel_id=1, source_target_pairs={{0,32},{4,36},{8,40},{12,44},{16,48},{20,52},{24,56},{28,60},{32,0... | collective-permute-start | bytes 24584 | tf_op jit(solution)/shard_map/ppermute | solution.py:336
  9.1 4.6 %pack.1 = (bf16[64,16,1536]{2,1,0:T(8,128)(2,1)}, bf16[16,4096]{1,0:T(8,128)(2,1)}, bf16[16,4096]{1,0:T(8,128)(2,1)}, bf16[16,4096]{1,0:T(8,128)(2,1)}, bf16[16,...) custom-call(s32[128]{0:T(128)} %bitcast.33, ...), custom_call_target="tpu_custom_call" | custom-call | tf_op jit(solution)/shard_map/pack/pallas_call | solution.py:54
  13.8 1.7 collective-permute-start.3
  16.6 3.1 %collective-permute-done.3 = bf16[32,256]{1,0:T(8,128)(2,1)S(1)} collective-permute-done((bf16[32,256]{1,0:T(8,128)(2,1)S(1)}, bf16[32,256]{1,0:T(8,128)(2,1)S(1)}, u32[]{:S(2)}, u32[]{:S(2)}) %collective-permute-start.3) | collective-permute-done | bytes 16416 | tf_op jit(solution)/shard_map/ppermute | solution.py:336
  20.4 10.8 %all-to-all-start = ((bf16[64,16,1536]{2,1,0:T(8,128)(2,1)}), bf16[64,16,1536]{2,1,0:T(8,128)(2,1)}, u32[]{:S(2)}, u32[]{:S(2)}) async-start(bf16[64,16,1536]{2,1,0:T(8,128)(2,1)} %get-tuple-element.74), calls=%async_computation | async-start | bytes 6291456 | tf_op jit(solution)/shard_map/all_to_all | solution.py:320
  31.2 2.9 %collective-permute-start.6 = (bf16[128,256]{1,0:T(8,128)(2,1)S(1)}, bf16[128,256]{1,0:T(8,128)(2,1)S(1)}, u32[]{:S(2)}, u32[]{:S(2)}) collective-permute-start(bf16[128,256]{1,0:T(8,128)(2,1)S(1)} %pad_maximum_fusion.2), channel_id=1, source_target_pairs={{0,192},{4,196},{8,200},{12,204},{16,208},{20,212},{24,216},{28,22... | collective-permute-start | bytes 196616 | tf_op jit(solution)/shard_map/ppermute | solution.py:336
  35.1 6.4 %collective-permute-done.6 = bf16[128,256]{1,0:T(8,128)(2,1)S(1)} collective-permute-done((bf16[128,256]{1,0:T(8,128)(2,1)S(1)}, bf16[128,256]{1,0:T(8,128)(2,1)S(1)}, u32[]{:S(2)}, u32[]{:S(2)}) %collective-permute-start.6) | collective-permute-done | bytes 65568 | tf_op jit(solution)/shard_map/ppermute | solution.py:336
  41.6 1.5 collective-permute-done.5
  44.5 3.0 %collective-permute-start.8 = (bf16[4,128,256]{2,1,0:T(8,128)(2,1)S(1)}, bf16[4,128,256]{2,1,0:T(8,128)(2,1)S(1)}, u32[]{:S(2)}, u32[]{:S(2)}) collective-permute-start(bf16[4,128,256]{2,1,0:T(8,128)(2,1)S(1)} %get-tuple-element.98), channel_id=1, source_target_pairs={{0,2},{1,3},{2,0},{3,1},{4,6},{5,7},{6,4},{7,5},{8,10},{9,11},{10,... | collective-permute-start | bytes 786440 | tf_op jit(solution)/shard_map/ppermute | solution.py:324
  47.9 2.3 collective-permute-start.9
  50.2 2.4 collective-permute-done.8
  52.5 6.9 %collective-permute-done.7 = bf16[4,128,256]{2,1,0:T(8,128)(2,1)S(1)} collective-permute-done((bf16[4,128,256]{2,1,0:T(8,128)(2,1)S(1)}, bf16[4,128,256]{2,1,0:T(8,128)(2,1)S(1)}, u32[]{:S(2)}, u32[]{:S(2)}) %collective-permute-start.7) | collective-permute-done | bytes 262176 | tf_op jit(solution)/shard_map/ppermute | solution.py:324
  64.3 6.5 %prepare_band.1 = (bf16[1024,1024]{1,0:T(8,128)(2,1)}, bf16[1024,1024]{1,0:T(8,128)(2,1)}) custom-call(s32[5]{0:T(128)} %stack.53.where_ref, s32[1024,2]{1,0:T(8,128)} %bitcast.21, bf16[4,4,128,256]{3,2,1,0:T(8,128)(2,1)} %copy-done, bf16[4,4,128,256]{3,2,1,0:T(8,128)(2,1)} %copy-done.1), custom_call_target="tpu_custom_call" | custom-call | tf_op jit(solution)/shard_map/prepare_band/pallas_call | solution.py:111
  70.8 2.9 %collective-permute-start.11 = (bf16[16,4096]{1,0:T(8,128)(2,1)S(1)}, bf16[16,4096]{1,0:T(8,128)(2,1)S(1)}, u32[]{:S(2)}, u32[]{:S(2)}) collective-permute-start(bf16[16,4096]{1,0:T(8,128)(2,1)S(1)} %copy-done.11), channel_id=1, source_target_pairs={{0,8},{4,12},{8,16},{12,20},{16,24},{20,28},{24,32},{28,36},{32,40... | collective-permute-start | bytes 393224 | tf_op jit(solution)/shard_map/ppermute | solution.py:336
  73.7 3.3 %collective-permute-start.12 = (bf16[16,4096]{1,0:T(8,128)(2,1)S(1)}, bf16[16,4096]{1,0:T(8,128)(2,1)S(1)}, u32[]{:S(2)}, u32[]{:S(2)}) collective-permute-start(bf16[16,4096]{1,0:T(8,128)(2,1)S(1)} %copy-done.10), channel_id=1, source_target_pairs={{0,56},{4,60},{8,0},{12,4},{16,8},{20,12},{24,16},{28,20},{32,24},... | collective-permute-start | bytes 393224 | tf_op jit(solution)/shard_map/ppermute | solution.py:336
  78.2 2.4 collective-permute-start.14
  81.3 7.6 %natural_means.1.mean_ref = f32[1024,1024]{1,0:T(8,128)} custom-call(s32[5]{0:T(128)} %stack.53.where_ref, s32[2,65536]{1,0:T(2,128)} %spans_ref.7, s32[1024,2]{1,0:T(8,128)} %bitcast.22, bf16[1024,1024]{1,0:T(8,128)(2,1)} %get-tuple-element.72.masked_ref), custom_call_target="tpu_custom_call" | custom-call | tf_op jit(solution)/shard_map/natural_means/pallas_call | solution.py:164
  88.9 15.3 %collective-permute-done.11.refs_1_ = bf16[16,4096]{1,0:T(8,128)(2,1)S(1)} collective-permute-done((bf16[16,4096]{1,0:T(8,128)(2,1)S(1)}, bf16[16,4096]{1,0:T(8,128)(2,1)S(1)}, u32[]{:S(2)}, u32[]{:S(2)}) %collective-permute-start.11) | collective-permute-done | bytes 131104 | tf_op jit(solution)/shard_map/ppermute | solution.py:336
  104.1 3.4 %collective-permute-start.16 = (bf16[16,4096]{1,0:T(8,128)(2,1)S(1)}, bf16[16,4096]{1,0:T(8,128)(2,1)S(1)}, u32[]{:S(2)}, u32[]{:S(2)}) collective-permute-start(bf16[16,4096]{1,0:T(8,128)(2,1)S(1)} %copy-done.6), channel_id=1, source_target_pairs={{0,32},{4,36},{8,40},{12,44},{16,48},{20,52},{24,56},{28,60},{32,0... | collective-permute-start | bytes 393224 | tf_op jit(solution)/shard_map/ppermute | solution.py:336
  107.8 10.7 %natural_rows.1.in_ref = bf16[1024,1024]{1,0:T(8,128)(2,1)} custom-call(s32[5]{0:T(128)} %stack.53.where_ref, s32[2,65536]{1,0:T(2,128)} %spans_ref.7, s32[1024,2]{1,0:T(8,128)} %bitcast.23, bf16[1024,1024]{1,0:T(8,128)(2,1)} %get-tuple-element.72.masked_ref, bf16[1024,1024]{1,0:T(8,128)(2,1)} %get-tuple-element.73.mask_ref, ...), custom_call_target="tpu_custom_call" | custom-call | flops 6442450944 | bytes 12582912 | tf_op jit(solution)/shard_map/natural_rows/pallas_call | solution.py:192
  119.2 11.9 %all-to-all-start.1 = ((bf16[64,16,1024]{2,1,0:T(8,128)(2,1)}), bf16[64,16,1024]{2,1,0:T(8,128)(2,1)}, u32[]{:S(2)}, u32[]{:S(2)}) async-start(bf16[64,16,1024]{2,1,0:T(8,128)(2,1)} %bitcast.20), calls=%async_computation.1 | async-start | bytes 4194304 | tf_op jit(solution)/shard_map/all_to_all | solution.py:320
  132.5 3.0 %repack.1 = (bf16[128,512]{1,0:T(8,128)(2,1)}, bf16[128,512]{1,0:T(8,128)(2,1)}, bf16[128,512]{1,0:T(8,128)(2,1)}, bf16[128,512]{1,0:T(8,128)(2,1)}, bf16[128,51...) custom-call(s32[5]{0:T(128)} %stack.53.where_ref, ...), custom_call_target="tpu_custom_call" | custom-call | flops 137438953472 | bytes 1073741824 | tf_op jit(solution)/shard_map/repack/pallas_call | solution.py:78
  136.9 1.5 collective-permute-start.19
  139.0 1.6 collective-permute-start.20
  142.1 3.0 %collective-permute-done.18.refs_1_ = bf16[128,512]{1,0:T(8,128)(2,1)S(1)} collective-permute-done((bf16[128,512]{1,0:T(8,128)(2,1)}, bf16[128,512]{1,0:T(8,128)(2,1)S(1)}, u32[]{:S(2)}, u32[]{:S(2)}) %collective-permute-start.18) | collective-permute-done | bytes 131104 | tf_op jit(solution)/shard_map/ppermute | solution.py:336
  145.1 2.1 collective-permute-start.23
  147.2 3.6 %collective-permute-start.24 = (bf16[128,512]{1,0:T(8,128)(2,1)}, bf16[128,512]{1,0:T(8,128)(2,1)S(1)}, u32[]{:S(2)}, u32[]{:S(2)}) collective-permute-start(bf16[128,512]{1,0:T(8,128)(2,1)} %get-tuple-element.96), channel_id=1, source_target_pairs={{0,132},{4,128},{8,140},{12,136},{16,148},{20,144},{24,156},{28,15... | collective-permute-start | bytes 393224 | tf_op jit(solution)/shard_map/ppermute | solution.py:336
  150.7 8.0 %assigned_first.1.tiles_ref = bf16[1,2,1024,512]{3,2,1,0:T(8,128)(2,1)} custom-call(s32[2]{0:T(128)} %dynamic-slice_bitcast_fusion.owned_ref, s32[2,65536]{1,0:T(2,128)} %spans_ref.7, s32[1024,2]{1,0:T(8,128)} %bitcast.24, bf16[1024,1024]{1,0:T(8,128)(2,1)} %get-tuple-element.72.masked_ref, bf16[1024,1024]{1,0:T(8,128)(2,1)} %get-tuple-element.73.mask_ref, ...), custom_call_target="tpu_custom_call" | custom-call | flops 3221225472 | bytes 6291456 | tf_op jit(solution)/shard_map/assigned_first/pallas_call | solution.py:237
  158.8 4.1 %flip.1 = bf16[1,1024,1024]{2,1,0:T(8,128)(2,1)} custom-call(bf16[1024,1024]{1,0:T(8,128)(2,1)} %natural_rows.1.in_ref), custom_call_target="tpu_custom_call" | custom-call | tf_op jit(solution)/shard_map/flip/pallas_call | solution.py:218
  163.8 8.3 %assigned_second.1 = bf16[1,2,1024,512]{3,2,1,0:T(8,128)(2,1)} custom-call(s32[2]{0:T(128)} %dynamic-slice_bitcast_fusion.owned_ref, s32[5]{0:T(128)} %stack.53.where_ref, bf16[1,2,1024,512]{3,2,1,0:T(8,128)(2,1)} %assigned_first.1.tiles_ref, s32[2,65536]{1,0:T(2,128)} %spans_ref.7, s32[1024,2]{1,0:T(8,128)} %bitcast.25, ...), custom_call_target="tpu_custom_call", output_to_operand_aliasing={{}: (2, {})} | custom-call | flops 3221225472 | bytes 6291456 | tf_op jit(solution)/shard_map/assigned_second/pallas_call | solution.py:273
  172.0 10.2 %all-to-all-done.1.in_ref = bf16[64,16,1024]{2,1,0:T(8,128)(2,1)} async-done(((bf16[64,16,1024]{2,1,0:T(8,128)(2,1)}), bf16[64,16,1024]{2,1,0:T(8,128)(2,1)}, u32[]{:S(2)}, u32[]{:S(2)}) %all-to-all-start.1) | async-done | bytes 2097184 | tf_op jit(solution)/shard_map/all_to_all | solution.py:320
  182.3 65.2 %unpack_rows.1 = bf16[16,65536]{1,0:T(8,128)(2,1)} custom-call(bf16[64,16,1024]{2,1,0:T(8,128)(2,1)} %all-to-all-done.1.in_ref), custom_call_target="tpu_custom_call" | custom-call | tf_op jit(solution)/shard_map/unpack_rows/pallas_call | solution.py:308
  (90 shorter events, 18.5 us)
Async XLA Ops:
  0.6 13.1 %collective-permute-start = (bf16[16,256]{1,0:T(8,128)(2,1)}, bf16[16,256]{1,0:T(8,128)(2,1)S(1)}, u32[]{:S(2)}, u32[]{:S(2)}) collective-permute-start(bf16[16,256]{1,0:T(8,128)(2,1)} %param.7), channel_id=1, source_target_pairs={{0,32},{4,36},{8,40},{12,44},{16,48},{20,52},{24,56},{28,60},{32,0... | collective-permute-start | bytes 24584 | tf_op jit(solution)/shard_map/ppermute | solution.py:336
  13.8 5.9 %collective-permute-start.3 = (bf16[32,256]{1,0:T(8,128)(2,1)S(1)}, bf16[32,256]{1,0:T(8,128)(2,1)S(1)}, u32[]{:S(2)}, u32[]{:S(2)}) collective-permute-start(bf16[32,256]{1,0:T(8,128)(2,1)S(1)} %pad_maximum_fusion.3), channel_id=1, source_target_pairs={{0,24},{4,28},{8,32},{12,36},{16,40},{20,44},{24,48},{28,52},{32,5... | collective-permute-start | bytes 49160 | tf_op jit(solution)/shard_map/ppermute | solution.py:336
  15.5 4.9 %collective-permute-start.2 = (bf16[32,256]{1,0:T(8,128)(2,1)S(1)}, bf16[32,256]{1,0:T(8,128)(2,1)S(1)}, u32[]{:S(2)}, u32[]{:S(2)}) collective-permute-start(bf16[32,256]{1,0:T(8,128)(2,1)S(1)} %pad_maximum_fusion.3), channel_id=1, source_target_pairs={{0,16},{4,20},{8,24},{12,28},{16,32},{20,36},{24,40},{28,44},{32,4... | collective-permute-start | bytes 49160 | tf_op jit(solution)/shard_map/ppermute | solution.py:336
  15.8 4.5 %collective-permute-start.1 = (bf16[32,256]{1,0:T(8,128)(2,1)S(1)}, bf16[32,256]{1,0:T(8,128)(2,1)S(1)}, u32[]{:S(2)}, u32[]{:S(2)}) collective-permute-start(bf16[32,256]{1,0:T(8,128)(2,1)S(1)} %pad_maximum_fusion.3), channel_id=1, source_target_pairs={{0,8},{4,12},{8,16},{12,20},{16,24},{20,28},{24,32},{28,36},{32,40... | collective-permute-start | bytes 49160 | tf_op jit(solution)/shard_map/ppermute | solution.py:336
  20.4 87.4 %all-to-all-start = ((bf16[64,16,1536]{2,1,0:T(8,128)(2,1)}), bf16[64,16,1536]{2,1,0:T(8,128)(2,1)}, u32[]{:S(2)}, u32[]{:S(2)}) async-start(bf16[64,16,1536]{2,1,0:T(8,128)(2,1)} %get-tuple-element.74), calls=%async_computation | async-start | bytes 6291456 | tf_op jit(solution)/shard_map/all_to_all | solution.py:320
  31.2 29.8 %copy-start.2 = (s32[2,1024]{1,0:T(2,128)S(1)}, s32[2,1024]{1,0:T(2,128)}, u32[]{:S(2)}) copy-start(s32[2,1024]{1,0:T(2,128)} %param.8) | copy-start | bytes 24580
  31.2 10.3 %collective-permute-start.6 = (bf16[128,256]{1,0:T(8,128)(2,1)S(1)}, bf16[128,256]{1,0:T(8,128)(2,1)S(1)}, u32[]{:S(2)}, u32[]{:S(2)}) collective-permute-start(bf16[128,256]{1,0:T(8,128)(2,1)S(1)} %pad_maximum_fusion.2), channel_id=1, source_target_pairs={{0,192},{4,196},{8,200},{12,204},{16,208},{20,212},{24,216},{28,22... | collective-permute-start | bytes 196616 | tf_op jit(solution)/shard_map/ppermute | solution.py:336
  34.1 9.0 %collective-permute-start.5 = (bf16[128,256]{1,0:T(8,128)(2,1)S(1)}, bf16[128,256]{1,0:T(8,128)(2,1)S(1)}, u32[]{:S(2)}, u32[]{:S(2)}) collective-permute-start(bf16[128,256]{1,0:T(8,128)(2,1)S(1)} %pad_maximum_fusion.2), channel_id=1, source_target_pairs={{0,128},{4,132},{8,136},{12,140},{16,144},{20,148},{24,152},{28,15... | collective-permute-start | bytes 196616 | tf_op jit(solution)/shard_map/ppermute | solution.py:336
  34.5 10.0 %collective-permute-start.4 = (bf16[128,256]{1,0:T(8,128)(2,1)S(1)}, bf16[128,256]{1,0:T(8,128)(2,1)S(1)}, u32[]{:S(2)}, u32[]{:S(2)}) collective-permute-start(bf16[128,256]{1,0:T(8,128)(2,1)S(1)} %pad_maximum_fusion.2), channel_id=1, source_target_pairs={{0,64},{4,68},{8,72},{12,76},{16,80},{20,84},{24,88},{28,92},{32,9... | collective-permute-start | bytes 196616 | tf_op jit(solution)/shard_map/ppermute | solution.py:336
  44.5 8.0 %collective-permute-start.8 = (bf16[4,128,256]{2,1,0:T(8,128)(2,1)S(1)}, bf16[4,128,256]{2,1,0:T(8,128)(2,1)S(1)}, u32[]{:S(2)}, u32[]{:S(2)}) collective-permute-start(bf16[4,128,256]{2,1,0:T(8,128)(2,1)S(1)} %get-tuple-element.98), channel_id=1, source_target_pairs={{0,2},{1,3},{2,0},{3,1},{4,6},{5,7},{6,4},{7,5},{8,10},{9,11},{10,... | collective-permute-start | bytes 786440 | tf_op jit(solution)/shard_map/ppermute | solution.py:324
  47.5 12.0 %collective-permute-start.7 = (bf16[4,128,256]{2,1,0:T(8,128)(2,1)S(1)}, bf16[4,128,256]{2,1,0:T(8,128)(2,1)S(1)}, u32[]{:S(2)}, u32[]{:S(2)}) collective-permute-start(bf16[4,128,256]{2,1,0:T(8,128)(2,1)S(1)} %get-tuple-element.98), channel_id=1, source_target_pairs={{0,1},{1,2},{2,3},{3,0},{4,5},{5,6},{6,7},{7,4},{8,9},{9,10},{10,1... | collective-permute-start | bytes 786440 | tf_op jit(solution)/shard_map/ppermute | solution.py:324
  47.9 11.6 %collective-permute-start.9 = (bf16[4,128,256]{2,1,0:T(8,128)(2,1)S(1)}, bf16[4,128,256]{2,1,0:T(8,128)(2,1)S(1)}, u32[]{:S(2)}, u32[]{:S(2)}) collective-permute-start(bf16[4,128,256]{2,1,0:T(8,128)(2,1)S(1)} %get-tuple-element.98), channel_id=1, source_target_pairs={{0,3},{1,0},{2,1},{3,2},{4,7},{5,4},{6,5},{7,6},{8,11},{9,8},{10,9... | collective-permute-start | bytes 786440 | tf_op jit(solution)/shard_map/ppermute | solution.py:324
  59.6 18.6 %copy-start.8 = (bf16[16,4096]{1,0:T(8,128)(2,1)S(1)}, bf16[16,4096]{1,0:T(8,128)(2,1)}, u32[]{:S(2)}) copy-start(bf16[16,4096]{1,0:T(8,128)(2,1)} %get-tuple-element.78) | copy-start | bytes 393220
  59.7 21.0 %copy-start.7 = (bf16[16,4096]{1,0:T(8,128)(2,1)S(1)}, bf16[16,4096]{1,0:T(8,128)(2,1)}, u32[]{:S(2)}) copy-start(bf16[16,4096]{1,0:T(8,128)(2,1)} %get-tuple-element.84) | copy-start | bytes 393220
  59.7 3.7 %collective-permute-start.10 = (bf16[4,4,128,256]{3,2,1,0:T(8,128)(2,1)S(1)}, bf16[4,4,128,256]{3,2,1,0:T(8,128)(2,1)S(1)}, u32[]{:S(2)}, u32[]{:S(2)}) collective-permute-start(bf16[4,4,128,256]{3,2,1,0:T(8,128)(2,1)S(1)} %pad_maximum_fusion.own_ref), channel_id=1, source_target_pairs={{0,4},{4,0},{8,12},{12,8},{16,20},{20,16},{24,28},{28,24},{32,36},... | collective-permute-start | bytes 3145736 | tf_op jit(solution)/shard_map/ppermute | solution.py:328
  70.8 33.3 %copy-start.6 = (bf16[16,4096]{1,0:T(8,128)(2,1)S(1)}, bf16[16,4096]{1,0:T(8,128)(2,1)}, u32[]{:S(2)}) copy-start(bf16[16,4096]{1,0:T(8,128)(2,1)} %get-tuple-element.85) | copy-start | bytes 393220
  70.8 36.7 %copy-start.5 = (bf16[16,4096]{1,0:T(8,128)(2,1)S(1)}, bf16[16,4096]{1,0:T(8,128)(2,1)}, u32[]{:S(2)}) copy-start(bf16[16,4096]{1,0:T(8,128)(2,1)} %get-tuple-element.86) | copy-start | bytes 393220
  70.8 33.3 %collective-permute-start.11 = (bf16[16,4096]{1,0:T(8,128)(2,1)S(1)}, bf16[16,4096]{1,0:T(8,128)(2,1)S(1)}, u32[]{:S(2)}, u32[]{:S(2)}) collective-permute-start(bf16[16,4096]{1,0:T(8,128)(2,1)S(1)} %copy-done.11), channel_id=1, source_target_pairs={{0,8},{4,12},{8,16},{12,20},{16,24},{20,28},{24,32},{28,36},{32,40... | collective-permute-start | bytes 393224 | tf_op jit(solution)/shard_map/ppermute | solution.py:336
  73.7 33.8 %collective-permute-start.12 = (bf16[16,4096]{1,0:T(8,128)(2,1)S(1)}, bf16[16,4096]{1,0:T(8,128)(2,1)S(1)}, u32[]{:S(2)}, u32[]{:S(2)}) collective-permute-start(bf16[16,4096]{1,0:T(8,128)(2,1)S(1)} %copy-done.10), channel_id=1, source_target_pairs={{0,56},{4,60},{8,0},{12,4},{16,8},{20,12},{24,16},{28,20},{32,24},... | collective-permute-start | bytes 393224 | tf_op jit(solution)/shard_map/ppermute | solution.py:336
  77.0 41.5 %collective-permute-start.13 = (bf16[16,4096]{1,0:T(8,128)(2,1)S(1)}, bf16[16,4096]{1,0:T(8,128)(2,1)S(1)}, u32[]{:S(2)}, u32[]{:S(2)}) collective-permute-start(bf16[16,4096]{1,0:T(8,128)(2,1)S(1)} %copy-done.9), channel_id=1, source_target_pairs={{0,16},{4,20},{8,24},{12,28},{16,32},{20,36},{24,40},{28,44},{32,4... | collective-permute-start | bytes 393224 | tf_op jit(solution)/shard_map/ppermute | solution.py:336
  78.2 40.3 %collective-permute-start.14 = (bf16[16,4096]{1,0:T(8,128)(2,1)S(1)}, bf16[16,4096]{1,0:T(8,128)(2,1)S(1)}, u32[]{:S(2)}, u32[]{:S(2)}) collective-permute-start(bf16[16,4096]{1,0:T(8,128)(2,1)S(1)} %copy-done.8), channel_id=1, source_target_pairs={{0,48},{4,52},{8,56},{12,60},{16,0},{20,4},{24,8},{28,12},{32,16},... | collective-permute-start | bytes 393224 | tf_op jit(solution)/shard_map/ppermute | solution.py:336
  80.6 50.5 %collective-permute-start.15 = (bf16[16,4096]{1,0:T(8,128)(2,1)S(1)}, bf16[16,4096]{1,0:T(8,128)(2,1)S(1)}, u32[]{:S(2)}, u32[]{:S(2)}) collective-permute-start(bf16[16,4096]{1,0:T(8,128)(2,1)S(1)} %copy-done.7), channel_id=1, source_target_pairs={{0,24},{4,28},{8,32},{12,36},{16,40},{20,44},{24,48},{28,52},{32,5... | collective-permute-start | bytes 393224 | tf_op jit(solution)/shard_map/ppermute | solution.py:336
  104.1 27.0 %collective-permute-start.16 = (bf16[16,4096]{1,0:T(8,128)(2,1)S(1)}, bf16[16,4096]{1,0:T(8,128)(2,1)S(1)}, u32[]{:S(2)}, u32[]{:S(2)}) collective-permute-start(bf16[16,4096]{1,0:T(8,128)(2,1)S(1)} %copy-done.6), channel_id=1, source_target_pairs={{0,32},{4,36},{8,40},{12,44},{16,48},{20,52},{24,56},{28,60},{32,0... | collective-permute-start | bytes 393224 | tf_op jit(solution)/shard_map/ppermute | solution.py:336
  107.6 23.6 %collective-permute-start.17 = (bf16[16,4096]{1,0:T(8,128)(2,1)S(1)}, bf16[16,4096]{1,0:T(8,128)(2,1)S(1)}, u32[]{:S(2)}, u32[]{:S(2)}) collective-permute-start(bf16[16,4096]{1,0:T(8,128)(2,1)S(1)} %copy-done.5), channel_id=1, source_target_pairs={{0,40},{4,44},{8,48},{12,52},{16,56},{20,60},{24,0},{28,4},{32,8},... | collective-permute-start | bytes 393224 | tf_op jit(solution)/shard_map/ppermute | solution.py:336
  119.2 63.1 %all-to-all-start.1 = ((bf16[64,16,1024]{2,1,0:T(8,128)(2,1)}), bf16[64,16,1024]{2,1,0:T(8,128)(2,1)}, u32[]{:S(2)}, u32[]{:S(2)}) async-start(bf16[64,16,1024]{2,1,0:T(8,128)(2,1)} %bitcast.20), calls=%async_computation.1 | async-start | bytes 4194304 | tf_op jit(solution)/shard_map/all_to_all | solution.py:320
  135.5 9.5 %collective-permute-start.18 = (bf16[128,512]{1,0:T(8,128)(2,1)}, bf16[128,512]{1,0:T(8,128)(2,1)S(1)}, u32[]{:S(2)}, u32[]{:S(2)}) collective-permute-start(bf16[128,512]{1,0:T(8,128)(2,1)} %get-tuple-element.90), channel_id=1, source_target_pairs={{0,64},{4,68},{8,72},{12,76},{16,80},{20,84},{24,88},{28,92},{32,9... | collective-permute-start | bytes 393224 | tf_op jit(solution)/shard_map/ppermute | solution.py:336
  136.9 10.2 %collective-permute-start.19 = (bf16[128,512]{1,0:T(8,128)(2,1)}, bf16[128,512]{1,0:T(8,128)(2,1)S(1)}, u32[]{:S(2)}, u32[]{:S(2)}) collective-permute-start(bf16[128,512]{1,0:T(8,128)(2,1)} %get-tuple-element.91), channel_id=1, source_target_pairs={{0,192},{4,196},{8,200},{12,204},{16,208},{20,212},{24,216},{28,22... | collective-permute-start | bytes 393224 | tf_op jit(solution)/shard_map/ppermute | solution.py:336
  139.0 23.9 %collective-permute-start.20 = (bf16[128,512]{1,0:T(8,128)(2,1)}, bf16[128,512]{1,0:T(8,128)(2,1)S(1)}, u32[]{:S(2)}, u32[]{:S(2)}) collective-permute-start(bf16[128,512]{1,0:T(8,128)(2,1)} %get-tuple-element.92), channel_id=1, source_target_pairs={{0,128},{4,132},{8,136},{12,140},{16,144},{20,148},{24,152},{28,15... | collective-permute-start | bytes 393224 | tf_op jit(solution)/shard_map/ppermute | solution.py:336
  140.6 22.3 %collective-permute-start.21 = (bf16[128,512]{1,0:T(8,128)(2,1)}, bf16[128,512]{1,0:T(8,128)(2,1)S(1)}, u32[]{:S(2)}, u32[]{:S(2)}) collective-permute-start(bf16[128,512]{1,0:T(8,128)(2,1)} %get-tuple-element.93), channel_id=1, source_target_pairs={{0,4},{4,0},{8,12},{12,8},{16,20},{20,16},{24,28},{28,24},{32,36},... | collective-permute-start | bytes 393224 | tf_op jit(solution)/shard_map/ppermute | solution.py:336
  141.8 21.1 %collective-permute-start.22 = (bf16[128,512]{1,0:T(8,128)(2,1)}, bf16[128,512]{1,0:T(8,128)(2,1)S(1)}, u32[]{:S(2)}, u32[]{:S(2)}) collective-permute-start(bf16[128,512]{1,0:T(8,128)(2,1)} %get-tuple-element.94), channel_id=1, source_target_pairs={{0,68},{4,64},{8,76},{12,72},{16,84},{20,80},{24,92},{28,88},{32,1... | collective-permute-start | bytes 393224 | tf_op jit(solution)/shard_map/ppermute | solution.py:336
  145.1 17.9 %collective-permute-start.23 = (bf16[128,512]{1,0:T(8,128)(2,1)}, bf16[128,512]{1,0:T(8,128)(2,1)S(1)}, u32[]{:S(2)}, u32[]{:S(2)}) collective-permute-start(bf16[128,512]{1,0:T(8,128)(2,1)} %get-tuple-element.95), channel_id=1, source_target_pairs={{0,196},{4,192},{8,204},{12,200},{16,212},{20,208},{24,220},{28,21... | collective-permute-start | bytes 393224 | tf_op jit(solution)/shard_map/ppermute | solution.py:336
  147.2 15.8 %collective-permute-start.24 = (bf16[128,512]{1,0:T(8,128)(2,1)}, bf16[128,512]{1,0:T(8,128)(2,1)S(1)}, u32[]{:S(2)}, u32[]{:S(2)}) collective-permute-start(bf16[128,512]{1,0:T(8,128)(2,1)} %get-tuple-element.96), channel_id=1, source_target_pairs={{0,132},{4,128},{8,140},{12,136},{16,148},{20,144},{24,156},{28,15... | collective-permute-start | bytes 393224 | tf_op jit(solution)/shard_map/ppermute | solution.py:336
  (21 other events, 125.5 us)
